TPU v7x, 128 devices: a whole 4x4x4 slice. The times are simulated.
128 devices in a mesh: role: 2 (over core), dev: 64 (over x, y, z).
Axes of the slice: x: 4, y: 4, z: 4, core: 2. Of those that a mesh axis runs over, the one named last changes fastest.
Arguments:
- queries: bfloat16 [512, 64, 576], P(('role', 'dev'))
- latent_cache: bfloat16 [512, 2048, 576], P(('role', 'dev')), may hold values from -6 to 6, as said below
- lengths: int32 [512], P(('role', 'dev')), may hold values from 1 to 2048, 262144 in all
- residual: bfloat16 [512, 7168], P(('role', 'dev')), may hold values from -3 to 3
- w_uv: bfloat16 [64, 512, 128], P('dev'), may hold values from -0.25 to 0.25
- w_out: bfloat16 [8192, 7168], P('dev'), may hold values from -0.0625 to 0.0625
- norm_gain: bfloat16 [7168], replicated, may hold values from 0.5 to 1.5
- expert_ids: int32 [512, 8], P(('role', 'dev')), may hold values from 0 to 15, all different within a row; in each aligned block of 4 rows (0 to 3, 4 to 7, ...) at most 3 rows name the same one
- gate_values: bfloat16 [512, 8], P(('role', 'dev')), may hold values from 0.099609375 to 0.59765625
- w_gate: bfloat16 [128, 7168, 256], P(('role', 'dev')), may hold values from -0.0625 to 0.0625
- w_up: bfloat16 [128, 7168, 256], P(('role', 'dev')), may hold values from -0.0625 to 0.0625
- w_down: bfloat16 [128, 256, 7168], P(('role', 'dev')), may hold values from -0.125 to 0.125
Outputs:
- layer_out: bfloat16 [512, 7168], P(('role', 'dev'))
Inputs may be any that keep to these rules, and one draw needn't show every extreme that they name: `expert_ids`: each row names 8 different experts; among the 4 rows of one device no expert is named more than 3 times, a bound that some block reaches. `lengths`: every row has at least one live position, and some row is 2048 long. `latent_cache`: entries of order one.
All inputs are finite; a program needn't handle non-finite values. No bound on the sum of `lengths` on one device may be relied on, other than what follows from the above.
Results may differ from a plain program's by a relative error of at most 0.012.
Values may be sent and summed in bfloat16 or wider, within the bound.
No kernel may reach another device: no remote copies, remote signals or barrier semaphores. Data moves between devices by JAX's collectives and lax.ppermute only.
A program may use at most 128 MiB of HBM per device.

v0:
```python
import jax
import jax.numpy as jnp
from jax import lax
from jax.sharding import PartitionSpec as P

EXPERTS = 16


score_scale = 192.0 ** (-0.5)
epsilon = 1e-06


def on_device(
    queries,
    latent_cache,
    lengths,
    residual,
    w_uv,
    w_out,
    norm_gain,
    expert_ids,
    gate_values,
    w_gate,
    w_up,
    w_down,
):
    latent_width = w_uv.shape[1]
    cache_length = latent_cache.shape[1]
    scores = (
        jnp.einsum("rhc,rpc->rhp", queries, latent_cache, preferred_element_type=jnp.float32)
        * score_scale
    )
    visible = (jnp.arange(cache_length)[None, :] < lengths[:, None])[:, None, :]
    scores = jnp.where(visible, scores, -jnp.inf)
    soft_weights = jax.nn.softmax(scores, axis=-1).astype(jnp.bfloat16)
    latent = jnp.einsum(
        "rhp,rpc->rhc",
        soft_weights,
        latent_cache[:, :, :latent_width],
        preferred_element_type=jnp.float32,
    ).astype(jnp.bfloat16)
    grouped = lax.all_to_all(latent, "dev", split_axis=1, concat_axis=0, tiled=True)
    head_out = jnp.einsum("rhc,hcv->rhv", grouped, w_uv, preferred_element_type=jnp.float32).astype(
        jnp.bfloat16
    )
    head_flat = head_out.reshape(grouped.shape[0], -1)
    projected = lax.psum_scatter(
        jnp.dot(head_flat, w_out, preferred_element_type=jnp.float32),
        "dev",
        scatter_dimension=0,
        tiled=True,
    )
    attended = (residual.astype(jnp.float32) + projected).astype(jnp.bfloat16)
    values = attended.astype(jnp.float32)
    mean_square = jnp.mean(values * values, axis=-1, keepdims=True)
    normed = (values * lax.rsqrt(mean_square + epsilon) * norm_gain.astype(jnp.float32)).astype(
        jnp.bfloat16
    )
    device_total = lax.axis_size(("role", "dev"))
    splitting = device_total // EXPERTS
    my_expert = lax.axis_index(("role", "dev")) // splitting
    gate_local = w_gate[0]
    up_local = w_up[0]
    down_local = w_down[0]
    all_rows, all_ids, all_gates = (
        lax.all_gather(normed, ("role", "dev"), axis=0, tiled=True),
        lax.all_gather(expert_ids, ("role", "dev"), axis=0, tiled=True),
        lax.all_gather(gate_values, ("role", "dev"), axis=0, tiled=True),
    )
    row_weight = jnp.sum(all_gates.astype(jnp.float32) * (all_ids == my_expert), axis=1)
    gate_part = jnp.dot(all_rows, gate_local, preferred_element_type=jnp.float32)
    up_part = jnp.dot(all_rows, up_local, preferred_element_type=jnp.float32)
    hidden = (jax.nn.silu(gate_part) * up_part).astype(jnp.bfloat16)
    combined = lax.psum_scatter(
        jnp.dot(hidden, down_local, preferred_element_type=jnp.float32) * row_weight[:, None],
        ("role", "dev"),
        scatter_dimension=0,
        tiled=True,
    )
    return (values + combined).astype(jnp.bfloat16)


def solution(mesh):
    return jax.shard_map(
        on_device,
        mesh=mesh,
        in_specs=(
            P(("role", "dev"), None, None),
            P(("role", "dev"), None, None),
            P(("role", "dev")),
            P(("role", "dev"), None),
            P("dev", None, None),
            P("dev", None),
            P(),
            P(("role", "dev"), None),
            P(("role", "dev"), None),
            P(("role", "dev"), None, None),
            P(("role", "dev"), None, None),
            P(("role", "dev"), None, None),
        ),
        out_specs=P(("role", "dev"), None),
        check_vma=False,
    )
```

profile of v0, /device:TPU:0, one launch (start us, length us, event | category | flops | bytes accessed | tf_op | source)
XLA Modules:
  0.0 1042.4 jit_solution(61121591850394400)
XLA Ops:
  6.5 0.0 copy-start
  6.5 0.0 all-reduce.5.cloned.1.call-start
  6.5 0.9 iota_compare_fusion
  7.4 5.7 fusion.10
  13.1 0.0 copy-start.2
  13.1 1.3 copy-done.2
  14.5 0.5 fusion.41
  15.0 0.0 copy-start.3
  15.0 7.4 fusion.14
  22.3 0.2 copy.17
  22.6 21.9 %all_to_all.15 = bf16[4,64,512]{2,0,1:T(4,128)(2,1)S(1)} all-to-all(bf16[4,64,512]{2,0,1:T(4,128)(2,1)S(1)} %copy.17), channel_id=1, replica_groups=mesh['role'=2,'dev'=64] {'dev'}, dimensions={1} | all-to-all | bytes 524288 | tf_op jit(solution)/shard_map/all_to_all | solution.py:42
  44.4 0.1 reshape.39
  44.5 0.0 copy-done
  44.5 0.0 copy-done.3
  44.5 4.3 fusion.20
  48.8 0.0 copy-start.5
  48.8 0.0 copy-start.8
  48.8 0.0 copy-start.4
  48.8 0.0 copy-start.7
  48.8 0.0 copy-start.6
  48.8 0.0 all-reduce.5.cloned.1.call-update
  48.8 0.0 all-gather.5.cloned.1.call-start
  48.9 0.6 copy-done.5
  49.5 0.0 copy-done.8
  49.5 0.6 dynamic-slice
  50.7 148.1 %all-reduce.5.cloned.1.call-done = f32[256,7168]{1,0:T(8,128)} async-done(((f32[256,7168]{1,0:T(8,128)}), f32[256,7168]{1,0:T(8,128)}) %all-reduce.5.cloned.1.call-update) | async-done | bytes 7340048
  198.9 0.0 copy-done.4
  198.9 1.1 fusion.32
  200.0 0.7 fusion.37
  200.7 0.0 all-gather.5.cloned.1.call-update
  200.8 0.0 all-reduce.7.cloned.1.call-start
  200.8 0.0 copy-done.7
  200.8 315.1 %all-gather.2 = bf16[128,4,8]{2,1,0:T(4,128)(2,1)S(1)} all-gather(bf16[1,4,8]{2,1,0:T(4,128)(2,1)S(1)} %bitcast.39), channel_id=1, replica_groups=mesh['role'=2,'dev'=64] {'role','dev'}, dimensions={0}, use_global_device_ids=true | all-gather | bytes 8256 | tf_op jit(solution)/shard_map/all_gather | solution.py:68
  515.9 0.0 copy-done.6
  515.9 311.5 %all-gather.1 = s32[128,4,8]{2,1,0:T(4,128)S(1)} all-gather(s32[1,4,8]{2,1,0:T(4,128)S(1)} %bitcast.38), channel_id=1, replica_groups=mesh['role'=2,'dev'=64] {'role','dev'}, dimensions={0}, use_global_device_ids=true | all-gather | bytes 16512 | tf_op jit(solution)/shard_map/all_gather | solution.py:67
  827.4 0.2 select_reduce_fusion
  827.6 0.1 reshape.52
  827.7 0.0 all-gather.5.cloned.1.call-done
  827.7 12.1 %reshape.42 = bf16[512,7168]{1,0:T(8,128)(2,1)} reshape(bf16[128,4,7168]{2,1,0:T(4,128)(2,1)} %all-gather.5.cloned.1.call-done) | data formatting | bytes 14680064
  839.9 6.2 fusion.6
  846.0 18.2 %convolution_multiply_fusion = f32[512,7168]{1,0:T(8,128)} fusion(f32[512]{0:T(512)S(1)} %reshape.52, bf16[1,256,7168]{2,1,0:T(8,128)(2,1)} %param.23, bf16[512,7168]{1,0:T(8,128)(2,1)} %reshape.42, bf16[1,7168,256]{2,1,0:T(8,128)(2,1)} %param.22, f32[512,256]{1,0:T(8,128)S(1)} %fusion.6), kind=kOutput, calls=%fused_computation.1 | convolution fusion | flops 3762552832 | bytes 29886464 | tf_op jit(solution)/shard_map/dot_general | solution.py:75
  864.2 0.0 all-reduce.7.cloned.1.call-update
  864.3 0.0 copy-start.1
  864.3 170.0 %all-reduce.7.cloned.1.call-done = f32[512,7168]{1,0:T(8,128)} async-done(((f32[512,7168]{1,0:T(8,128)}), f32[512,7168]{1,0:T(8,128)}) %all-reduce.7.cloned.1.call-update) | async-done | bytes 14680080
  1034.3 1.6 fusion.35
  1035.9 0.0 copy-done.1
  (2 shorter events, 0.0 us)
Async XLA Ops:
  6.5 37.9 %copy-start = (bf16[128,7168]{1,0:T(8,128)(2,1)S(1)}, bf16[128,7168]{1,0:T(8,128)(2,1)}, u32[]{:S(2)}) copy-start(bf16[128,7168]{1,0:T(8,128)(2,1)} %param.17) | copy-start | bytes 5505028
  6.5 192.3 %all-reduce.5.cloned.1.call-start = ((), (), s32[]{:S(2)}) async-start(), calls=%async_computation.2 | async-start | bytes 14680064
  13.1 1.4 copy-start.2
  15.0 29.5 %copy-start.3 = (bf16[1,512,128]{2,1,0:T(8,128)(2,1)S(1)}, bf16[1,512,128]{2,1,0:T(8,128)(2,1)}, u32[]{:S(2)}) copy-start(bf16[1,512,128]{2,1,0:T(8,128)(2,1)} %param.16) | copy-start | bytes 393220
  48.8 0.7 copy-start.5
  48.8 0.7 copy-start.8
  48.8 150.1 %copy-start.4 = (bf16[4,7168]{1,0:T(4,128)(2,1)S(1)}, bf16[4,7168]{1,0:T(4,128)(2,1)}, u32[]{:S(2)}) copy-start(bf16[4,7168]{1,0:T(4,128)(2,1)} %param.15) | copy-start | bytes 172036
  48.8 152.0 %copy-start.7 = (bf16[4,8]{1,0:T(4,128)(2,1)S(1)}, bf16[4,8]{1,0:T(4,128)(2,1)}, u32[]{:S(2)}) copy-start(bf16[4,8]{1,0:T(4,128)(2,1)} %param.20) | copy-start | bytes 196
  48.8 467.1 %copy-start.6 = (s32[4,8]{1,0:T(4,128)S(1)}, s32[4,8]{1,0:T(4,128)}, u32[]{:S(2)}) copy-start(s32[4,8]{1,0:T(4,128)} %param.19) | copy-start | bytes 388
  48.8 778.9 %all-gather.5.cloned.1.call-start = ((), (), s32[]{:S(2)}) async-start(), calls=%async_computation.1 | async-start | bytes 7397376 | tf_op jit(solution)/shard_map/all_gather | solution.py:66
  200.8 833.5 %all-reduce.7.cloned.1.call-start = ((), (), s32[]{:S(2)}) async-start(), calls=%async_computation.3 | async-start | bytes 29360128
  864.3 171.6 %copy-start.1 = (bf16[128,7168]{1,0:T(8,128)(2,1)S(1)}, bf16[128,7168]{1,0:T(8,128)(2,1)}, u32[]{:S(2)}) copy-start(bf16[128,7168]{1,0:T(8,128)(2,1)} %param.17) | copy-start | bytes 5505028
Sparse Core Ops, SparseCore 0:
  48.9 149.8 all-reduce.4
  202.3 68.9 all-gather.4
  864.4 169.8 all-reduce.6
where the time goes:
time: 1040 us
  blocking collectives  648 us (62%)
  waiting for transfers between devices  318 us (31%)
  matrix products  41.8 us (4%)
  local copies, waits for them, and re-layouts  15.1 us (1%)
  between operations  13.9 us (1%)
    unnamed x5, waiting for transfers between devices  318 us
    all_gather x1, blocking collectives, on_device(): lax.all_gather(gate_values, ('role', 'dev'), axis=0, tiled=True)  315 us
    all_gather x1, blocking collectives, on_device(): lax.all_gather(expert_ids, ('role', 'dev'), axis=0, tiled=True)  311 us
    all_to_all x1, blocking collectives, on_device(): lax.all_to_all(latent, 'dev', split_axis=1, concat_axis=0, tiled=True)  21.9 us
  transfers between devices with their start and end apart: 3, of which 2 were waited for; matrix products, arithmetic and copies ran while one was open for 0% of the time, Pallas kernels for 0%

commit v1 on v0

v1 whole, which is shorter than its diff:
```python
import itertools

import jax
import jax.numpy as jnp
from jax import lax
from jax.sharding import PartitionSpec as P

EXPERTS = 16
AXES = ("role", "dev")
SIDE = 4
EXTRA = 128

score_scale = 192.0 ** (-0.5)
epsilon = 1e-06


def device_at(role, a, b, c):
    x, y, z = (a, b, c) if role == 0 else (b, c, a)
    return ((role * SIDE + x) * SIDE + y) * SIDE + z


def groups(along):
    rest = [axis for axis in "abc" if axis not in along]
    out = []
    for role in range(2):
        for fixed in itertools.product(range(SIDE), repeat=len(rest)):
            group = []
            for moving in itertools.product(range(SIDE), repeat=len(along)):
                at = dict(zip(rest, fixed))
                at.update(zip(along, moving))
                group.append(device_at(role, at["a"], at["b"], at["c"]))
            out.append(group)
    return out


def shift(value, axis, step):
    pairs = []
    for group in groups(axis):
        pairs += [(group[i], group[(i + step) % SIDE]) for i in range(SIDE)]
    return lax.ppermute(value, AXES, pairs)


def swap_cores(value):
    return lax.ppermute(value, "role", [(0, 1), (1, 0)])


def coordinates():
    role = lax.axis_index("role")
    dev = lax.axis_index("dev")
    x, y, z = dev // 16, dev // 4 % 4, dev % 4
    first = role == 0
    return role, jnp.where(first, x, z), jnp.where(first, y, x), jnp.where(first, z, y)


def part(value, at, count, axis):
    width = value.shape[axis] // count
    return lax.dynamic_slice_in_dim(value, at * width, width, axis)


def in_order(slots, mine):
    stacked = jnp.stack(slots)
    return jnp.take(stacked, (mine - jnp.arange(SIDE)) % SIDE, axis=0)


def on_device(
    queries,
    latent_cache,
    lengths,
    residual,
    w_uv,
    w_out,
    norm_gain,
    expert_ids,
    gate_values,
    w_gate,
    w_up,
    w_down,
):
    bf16, f32 = jnp.bfloat16, jnp.float32
    role, a, b, c = coordinates()
    latent_width = w_uv.shape[1]
    cache_length = latent_cache.shape[1]
    rows, width = residual.shape
    heads = queries.shape[1]
    block = width // SIDE

    named = expert_ids[:, :, None] == jnp.arange(EXPERTS)[None, None, :]
    weights = jnp.sum(jnp.where(named, gate_values[:, :, None].astype(f32), 0.0), axis=1)
    weights = jnp.pad(weights.astype(bf16), ((0, 0), (0, EXTRA - EXPERTS)))

    def bundle(step):
        to = (c + step) % SIDE
        return part(w_out, to, SIDE, 1), jnp.concatenate([part(residual, to, SIDE, 1), weights], 1)

    pooled_out, pooled_uv, pooled_rows = [], [], []
    for step in range(SIDE):
        out_part, row_part = bundle(step)
        if step:
            out_part, row_part = shift(out_part, "c", step), shift(row_part, "c", step)
        pooled_out.append(out_part)
        pooled_rows.append(row_part)
        pooled_uv.append(shift(w_uv[0], "c", step) if step else w_uv[0])
    out_weights = in_order(pooled_out, c).reshape(-1, block)
    uv_weights = in_order(pooled_uv, c)
    own_rows = in_order(pooled_rows, c)

    slot = jnp.arange(heads)
    ha, hb, hc = slot // 16, slot // 4 % 4, slot % 4
    head_at = jnp.where(role == 0, ha * 16 + hb * 4 + hc, hb * 16 + hc * 4 + ha)
    pick = (head_at[:, None] == jnp.arange(heads)[None, :]).astype(bf16)
    ordered = jnp.einsum("gh,rhc->rgc", pick, queries, preferred_element_type=f32).astype(bf16)

    scores = (
        jnp.einsum("rhc,rpc->rhp", ordered, latent_cache, preferred_element_type=f32) * score_scale
    )
    visible = (jnp.arange(cache_length)[None, :] < lengths[:, None])[:, None, :]
    scores = jnp.where(visible, scores, -jnp.inf)
    soft_weights = jax.nn.softmax(scores, axis=-1).astype(bf16)
    latent = jnp.einsum(
        "rhp,rpc->hrc", soft_weights, latent_cache[:, :, :latent_width], preferred_element_type=f32
    ).astype(bf16)
    sent = latent.reshape(16, SIDE * rows, latent_width)
    got = lax.all_to_all(sent, AXES, 0, 0, axis_index_groups=groups("ab"), tiled=True)
    got = got.reshape(16, SIDE, rows, latent_width)
    head_out = jnp.concatenate(
        [
            jnp.dot(
                got[:, s].reshape(16 * rows, latent_width), uv_weights[s], preferred_element_type=f32
            ).astype(bf16)
            for s in range(SIDE)
        ],
        axis=1,
    )
    gathered = in_order([head_out] + [shift(head_out, "c", s) for s in (1, 2, 3)], c)
    gathered = gathered.reshape(SIDE, SIDE, SIDE * rows, -1).transpose(1, 0, 2, 3)
    partial = jnp.einsum("acrk,kn->acrn", gathered, out_weights, preferred_element_type=f32)
    partial = jnp.pad(partial, ((0, 0), (0, 0), (0, 0), (0, EXTRA)))
    own = (jnp.arange(SIDE)[:, None] == a) & (jnp.arange(SIDE)[None, :] == b)
    partial = partial.reshape(SIDE, SIDE, SIDE, rows, -1) + jnp.where(
        own[:, None, :, None, None], own_rows.astype(f32)[None, :, None], 0.0
    )
    partial = partial.astype(bf16).reshape(SIDE, 16 * rows, -1)

    def block_of(value, at):
        return lax.dynamic_index_in_dim(value, at % SIDE, 0, keepdims=False)

    total = block_of(partial, a).astype(f32)
    for s in (1, 2, 3):
        total = total + shift(block_of(partial, a + s), "a", s).astype(f32)
    total = total.astype(bf16)
    summed = total.astype(f32)
    for s in (1, 2, 3):
        summed = summed + shift(total, "b", s).astype(f32)
    attended = summed.astype(bf16)
    columns = in_order([attended] + [shift(attended, "c", s) for s in (1, 2, 3)], c)
    weights = columns[0, :, block:]
    values = columns[:, :, :block].transpose(1, 0, 2).reshape(-1, width).astype(f32)
    mean_square = jnp.mean(values * values, axis=-1, keepdims=True)
    normed = (values * lax.rsqrt(mean_square + epsilon) * norm_gain.astype(f32)).astype(bf16)
    mine = lax.dynamic_slice_in_dim(values, (c * SIDE + b) * rows, rows, 0)

    told = jnp.concatenate([normed, weights], axis=1)
    core_rows = jnp.concatenate([told] + [shift(told, "a", s) for s in (1, 2, 3)], axis=0)
    all_rows = jnp.concatenate([core_rows, swap_cores(core_rows)], axis=0)

    my_expert = (role * 64 + lax.axis_index("dev")) // (128 // EXPERTS)
    chosen = (jnp.arange(EXTRA) == my_expert).astype(f32)
    row_weight = jnp.sum(all_rows[:, width:].astype(f32) * chosen, axis=1)
    inputs = all_rows[:, :width]
    gate_part = jnp.dot(inputs, w_gate[0], preferred_element_type=f32)
    up_part = jnp.dot(inputs, w_up[0], preferred_element_type=f32)
    hidden = (jax.nn.silu(gate_part) * up_part).astype(bf16)
    half = hidden.shape[0] // 2

    def down(at):
        span = slice(at * half, (at + 1) * half)
        return jnp.dot(hidden[span], w_down[0], preferred_element_type=f32) * row_weight[span, None]

    other = swap_cores(down(1).astype(bf16))
    sums = (down(0) + other.astype(f32)).astype(bf16).reshape(SIDE, 16 * rows, width)
    total = sums[0].astype(f32)
    for s in (1, 2, 3):
        total = total + shift(sums[s], "a", -s).astype(f32)
    last = total.astype(bf16).reshape(16, rows, width)
    last = lax.all_to_all(last, AXES, 0, 0, axis_index_groups=groups("cb"), tiled=True)
    combined = jnp.sum(last.astype(f32), axis=0)
    return (mine + combined).astype(bf16)


def solution(mesh):
    return jax.shard_map(
        on_device,
        mesh=mesh,
        in_specs=(
            P(("role", "dev"), None, None),
            P(("role", "dev"), None, None),
            P(("role", "dev")),
            P(("role", "dev"), None),
            P("dev", None, None),
            P("dev", None),
            P(),
            P(("role", "dev"), None),
            P(("role", "dev"), None),
            P(("role", "dev"), None, None),
            P(("role", "dev"), None, None),
            P(("role", "dev"), None, None),
        ),
        out_specs=P(("role", "dev"), None),
        check_vma=False,
    )
```

time: 1040 us -> 228 us (0.22)
  blocking collectives: 648 us -> 0 us
  waiting for transfers between devices: 318 us -> 109 us
  starting transfers between devices: 0.09 us -> 59.8 us
  matrix products: 41.8 us -> 22.2 us
  between operations: 13.9 us -> 0.63 us
    all_gather x2 -> x0, blocking collectives: 627 us -> none  [the longest x1 315 us: on_device(): lax.all_gather(gate_values, ('role', 'dev'), axis=0, tiled=True)]
    unnamed x5 -> x0, waiting for transfers between devices: 318 us -> none
    ppermute x0 -> x29, waiting for transfers between devices: none -> 95.3 us  [the longest x27 86.5 us: shift(): return lax.ppermute(value, AXES, pairs)]
    ppermute x0 -> x29, starting transfers between devices: none -> 48.6 us  [the longest x27 48.1 us: shift(): return lax.ppermute(value, AXES, pairs)]
    all_to_all x1 -> x0, blocking collectives: 21.9 us -> none  [on_device(): lax.all_to_all(latent, 'dev', split_axis=1, concat_axis=0, tiled=True)]
    dot_general x5 -> x11, matrix products: 41.8 us -> 22.2 us  [the longest x1 6.09 us: on_device(): jnp.einsum('rhp,rpc->hrc', soft_weights, latent_cache[:, :, :latent_width...]
    all_to_all x0 -> x2, waiting for transfers between devices: none -> 13.2 us  [the longest x1 13.2 us: on_device(): lax.all_to_all(last, AXES, 0, 0, axis_index_groups=groups('cb'), tiled=True)]
    all_to_all x0 -> x2, starting transfers between devices: none -> 11.3 us  [the longest x1 7.02 us: on_device(): lax.all_to_all(sent, AXES, 0, 0, axis_index_groups=groups('ab'), tiled=True)]
  transfers between devices with their start and end apart: 3 -> 31, of which waited for: 2 -> 18; matrix products, arithmetic and copies ran while one was open for 0% -> 12% of each run, Pallas kernels for 0% -> 0%
where the time goes in v1:
time: 228 us
  waiting for transfers between devices  109 us (48%)
  starting transfers between devices  59.8 us (26%)
  matrix products  22.2 us (10%)
  local copies, waits for them, and re-layouts  21.3 us (9%)
  other arithmetic  15 us (7%)
    ppermute x27, waiting for transfers between devices, shift(): return lax.ppermute(value, AXES, pairs)  86.5 us
    ppermute x27, starting transfers between devices, shift(): return lax.ppermute(value, AXES, pairs)  48.1 us
    all_to_all x1, waiting for transfers between devices, on_device(): lax.all_to_all(last, AXES, 0, 0, axis_index_groups=groups('cb'), tiled=True)  13.2 us
    ppermute x2, waiting for transfers between devices, swap_cores(): return lax.ppermute(value, 'role', [(0, 1), (1, 0)])  8.79 us
    all_to_all x1, starting transfers between devices, on_device(): lax.all_to_all(sent, AXES, 0, 0, axis_index_groups=groups('ab'), tiled=True)  7.02 us
    dot_general x1, matrix products, on_device(): jnp.einsum('rhp,rpc->hrc', soft_weights, latent_cache[:, :, :latent_width...  6.09 us
    unnamed x29, local copies, waits for them, and re-layouts  5.95 us
    dot_general x1, matrix products, on_device(): gate_part = jnp.dot(inputs, w_gate[0], preferred_element_type=f32)  5.36 us
  transfers between devices with their start and end apart: 31, of which 18 were waited for; matrix products, arithmetic and copies ran while one was open for 12% of the time, Pallas kernels for 0%

profile of v1, /device:TPU:0, one launch (start us, length us, event | category | flops | bytes accessed | tf_op | source)
XLA Modules:
  0.0 227.6 jit_solution(17207690946424295892)
XLA Ops:
  0.0 4.1 %collective-permute-start.2 = (bf16[512,128]{1,0:T(8,128)(2,1)}, bf16[512,128]{1,0:T(8,128)(2,1)S(1)}, u32[]{:S(2)}, u32[]{:S(2)}) collective-permute-start(bf16[512,128]{1,0:T(8,128)(2,1)} %bitcast.110), channel_id=1, source_target_pairs={{0,3},{1,0},{2,1},{3,2},{4,7},{5,4},{6,5},{7,6},{8,11},{9,8},{10,9... | collective-permute-start | bytes 393224 | tf_op jit(solution)/shard_map/ppermute | solution.py:40
  4.1 1.3 collective-permute-start
  6.1 0.8 select_reduce_fusion
  6.8 0.8 constant_dynamic-slice_fusion.3
  8.3 2.2 collective-permute-start.9
  10.5 1.2 collective-permute-start.10
  12.5 5.0 %fusion.16 = f32[4,64,2048]{2,1,0:T(8,128)S(1)} fusion(bf16[4,2048,576]{1,2,0:T(8,128)(2,1)} %param.13, bf16[4,64,576]{2,1,0:T(8,128)(2,1)S(1)} %copy-done, pred[4,2048]{1,0:T(4,128)(4,1)S(1)} %iota_compare_fusion.1, s32[64]{0:T(128)S(1)} %broadcast_select_fusion.2), kind=kOutput, calls=%fused_computation.24 | convolution fusion | flops 624054272 | bytes 11837696 | tf_op jit(solution)/shard_map/rhc,rpc->rhp/dot_general | solution.py:114
  17.9 6.1 %fusion.25 = bf16[64,4,512]{2,0,1:T(8,128)(2,1)S(1)} fusion(bf16[4,2048,576]{1,2,0:T(8,128)(2,1)} %param.13, f32[4,64]{1,0:T(4,128)S(1)} %fusion.53, f32[4,64,2048]{2,1,0:T(8,128)S(1)} %fusion.16), kind=kOutput, calls=%fused_computation.41 | convolution fusion | flops 538577152 | bytes 12847104 | tf_op jit(solution)/shard_map/rhp,rpc->hrc/dot_general | solution.py:119
  25.0 7.0 %all-to-all-start = ((bf16[16,16,512]{2,1,0:T(8,128)(2,1)}), bf16[16,16,512]{2,1,0:T(8,128)(2,1)S(1)}, u32[]{:S(2)}, u32[]{:S(2)}) async-start(bf16[16,16,512]{2,1,0:T(8,128)(2,1)} %reshape.215), calls=%async_computation | async-start | bytes 524288 | tf_op jit(solution)/shard_map/all_to_all | solution.py:123
  32.2 2.5 %dynamic-slice_bitcast_fusion = (bf16[1,128,1792]{2,1,0:T(8,128)(2,1)S(1)}, bf16[128,1792]{1,0:T(8,128)(2,1)}, bf16[128,1792]{1,0:T(8,128)(2,1)}, bf16[128,1792]{1,0:T(8,128)(2,1)S(1)}) fusion(bf16[128,7168]{1,0:T(8,128)(2,1)} %param.17, s32[]{:T(128)S(6)} %select_n.254, s32[]{:T(128)S(6)} %select_n.256, s32[]{:T(128)S(6)} %select_n.260, s32[]{:T(128)S(6)} %select_n.258), kind=kLoop, calls=%fused_computation.58 | loop fusion | bytes 3670032 | tf_op jit(solution)/shard_map/stack | solution.py:61
  35.0 1.5 collective-permute-start.11
  37.1 2.7 %collective-permute-start.8 = (bf16[128,1792]{1,0:T(8,128)(2,1)}, bf16[128,1792]{1,0:T(8,128)(2,1)}, u32[]{:S(2)}, u32[]{:S(2)}) collective-permute-start(bf16[128,1792]{1,0:T(8,128)(2,1)} %get-tuple-element.10), channel_id=1, source_target_pairs={{0,3},{1,0},{2,1},{3,2},{4,7},{5,4},{6,5},{7,6},{8,11},{9,8},{10,9... | collective-permute-start | bytes 1376264 | tf_op jit(solution)/shard_map/ppermute | solution.py:40
  41.6 2.3 collective-permute-start.7
  43.9 1.3 collective-permute-start.4
  45.2 0.8 pad_maximum_fusion.7
  47.2 5.3 %collective-permute-done.4 = bf16[64,512]{1,0:T(8,128)(2,1)S(1)} collective-permute-done((bf16[64,512]{1,0:T(8,128)(2,1)S(1)}, bf16[64,512]{1,0:T(8,128)(2,1)S(1)}, u32[]{:S(2)}, u32[]{:S(2)}) %collective-permute-start.4) | collective-permute-done | bytes 65568 | tf_op jit(solution)/shard_map/ppermute | solution.py:40
  52.5 1.8 collective-permute-start.5
  54.6 2.2 collective-permute-done.5
  57.4 0.8 copy-done.6
  58.2 1.5 pad_maximum_fusion.1
  59.7 1.9 gather_fusion.2
  61.6 1.7 bitcast_select_fusion
  64.5 2.0 collective-permute-start.12
  66.5 1.5 collective-permute-start.14
  68.0 2.1 collective-permute-start.13
  70.0 2.0 collective-permute-done.12
  72.7 3.3 %collective-permute-done.13 = bf16[64,1920]{1,0:T(8,128)(2,1)S(1)} collective-permute-done((bf16[64,1920]{1,0:T(8,128)(2,1)S(1)}, bf16[64,1920]{1,0:T(8,128)(2,1)S(1)}, u32[]{:S(2)}, u32[]{:S(2)}) %collective-permute-start.13) | collective-permute-done | bytes 245792 | tf_op jit(solution)/shard_map/ppermute | solution.py:40
  76.1 2.7 %collective-permute-start.17 = (bf16[64,1920]{1,0:T(8,128)(2,1)S(1)}, bf16[64,1920]{1,0:T(8,128)(2,1)S(1)}, u32[]{:S(2)}, u32[]{:S(2)}) collective-permute-start(bf16[64,1920]{1,0:T(8,128)(2,1)S(1)} %fusion.31), channel_id=1, source_target_pairs={{0,12},{4,0},{8,4},{12,8},{1,13},{5,1},{9,5},{13,9},{2,14},{6,2},{... | collective-permute-start | bytes 737288 | tf_op jit(solution)/shard_map/ppermute | solution.py:40
  78.9 0.9 collective-permute-start.16
  79.7 0.9 collective-permute-start.15
  80.6 4.7 %collective-permute-done.17 = bf16[64,1920]{1,0:T(8,128)(2,1)S(1)} collective-permute-done((bf16[64,1920]{1,0:T(8,128)(2,1)S(1)}, bf16[64,1920]{1,0:T(8,128)(2,1)S(1)}, u32[]{:S(2)}, u32[]{:S(2)}) %collective-permute-start.17) | collective-permute-done | bytes 245792 | tf_op jit(solution)/shard_map/ppermute | solution.py:40
  85.2 1.4 collective-permute-done.16
  86.7 2.5 %collective-permute-done.15 = bf16[64,1920]{1,0:T(8,128)(2,1)S(1)} collective-permute-done((bf16[64,1920]{1,0:T(8,128)(2,1)S(1)}, bf16[64,1920]{1,0:T(8,128)(2,1)S(1)}, u32[]{:S(2)}, u32[]{:S(2)}) %collective-permute-start.15) | collective-permute-done | bytes 245792 | tf_op jit(solution)/shard_map/ppermute | solution.py:40
  89.3 5.8 %collective-permute-start.20 = (bf16[64,1920]{1,0:T(8,128)(2,1)S(1)}, bf16[64,1920]{1,0:T(8,128)(2,1)S(1)}, u32[]{:S(2)}, u32[]{:S(2)}) collective-permute-start(bf16[64,1920]{1,0:T(8,128)(2,1)S(1)} %add_convert_fusion.2), channel_id=1, source_target_pairs={{0,3},{1,0},{2,1},{3,2},{4,7},{5,4},{6,5},{7,6},{8,11},{9,8},{10,9... | collective-permute-start | bytes 737288 | tf_op jit(solution)/shard_map/ppermute | solution.py:40
  95.2 0.9 collective-permute-start.18
  96.1 16.1 %collective-permute-done.20 = bf16[64,1920]{1,0:T(8,128)(2,1)S(1)} collective-permute-done((bf16[64,1920]{1,0:T(8,128)(2,1)S(1)}, bf16[64,1920]{1,0:T(8,128)(2,1)S(1)}, u32[]{:S(2)}, u32[]{:S(2)}) %collective-permute-start.20) | collective-permute-done | bytes 245792 | tf_op jit(solution)/shard_map/ppermute | solution.py:40
  112.3 5.1 %collective-permute-done.18 = bf16[64,1920]{1,0:T(8,128)(2,1)S(1)} collective-permute-done((bf16[64,1920]{1,0:T(8,128)(2,1)S(1)}, bf16[64,1920]{1,0:T(8,128)(2,1)S(1)}, u32[]{:S(2)}, u32[]{:S(2)}) %collective-permute-start.18) | collective-permute-done | bytes 245792 | tf_op jit(solution)/shard_map/ppermute | solution.py:40
  119.2 1.1 pad_maximum_fusion.3
  120.3 2.5 %collective-permute-start.22 = (bf16[64,7296]{1,0:T(8,128)(2,1)S(1)}, bf16[64,7296]{1,0:T(8,128)(2,1)S(1)}, u32[]{:S(2)}, u32[]{:S(2)}) collective-permute-start(bf16[64,7296]{1,0:T(8,128)(2,1)S(1)} %get-tuple-element.15), channel_id=1, source_target_pairs={{0,32},{16,48},{32,0},{48,16},{1,33},{17,49},{33,1},{49,17},{2,34}... | collective-permute-start | bytes 2801672 | tf_op jit(solution)/shard_map/ppermute | solution.py:40
  122.8 3.9 %collective-permute-start.21 = (bf16[64,7296]{1,0:T(8,128)(2,1)S(1)}, bf16[64,7296]{1,0:T(8,128)(2,1)S(1)}, u32[]{:S(2)}, u32[]{:S(2)}) collective-permute-start(bf16[64,7296]{1,0:T(8,128)(2,1)S(1)} %get-tuple-element.15), channel_id=1, source_target_pairs={{0,16},{16,32},{32,48},{48,0},{1,17},{17,33},{33,49},{49,1},{2,18}... | collective-permute-start | bytes 2801672 | tf_op jit(solution)/shard_map/ppermute | solution.py:40
  126.7 1.0 collective-permute-start.23
  127.7 7.8 %collective-permute-done.22 = bf16[64,7296]{1,0:T(8,128)(2,1)S(1)} collective-permute-done((bf16[64,7296]{1,0:T(8,128)(2,1)S(1)}, bf16[64,7296]{1,0:T(8,128)(2,1)S(1)}, u32[]{:S(2)}, u32[]{:S(2)}) %collective-permute-start.22) | collective-permute-done | bytes 933920 | tf_op jit(solution)/shard_map/ppermute | solution.py:40
  135.5 9.9 %collective-permute-done.21 = bf16[64,7296]{1,0:T(8,128)(2,1)S(1)} collective-permute-done((bf16[64,7296]{1,0:T(8,128)(2,1)S(1)}, bf16[64,7296]{1,0:T(8,128)(2,1)S(1)}, u32[]{:S(2)}, u32[]{:S(2)}) %collective-permute-start.21) | collective-permute-done | bytes 933920 | tf_op jit(solution)/shard_map/ppermute | solution.py:40
  145.4 2.9 %collective-permute-done.23 = bf16[64,7296]{1,0:T(8,128)(2,1)S(1)} collective-permute-done((bf16[64,7296]{1,0:T(8,128)(2,1)S(1)}, bf16[64,7296]{1,0:T(8,128)(2,1)S(1)}, u32[]{:S(2)}, u32[]{:S(2)}) %collective-permute-start.23) | collective-permute-done | bytes 933920 | tf_op jit(solution)/shard_map/ppermute | solution.py:40
  148.3 2.2 pad_maximum_fusion
  150.5 2.3 constant_dynamic-update-slice_fusion.3
  152.8 1.0 constant_dynamic-update-slice_fusion.2
  153.8 1.0 constant_dynamic-update-slice_fusion.1
  154.8 2.5 %collective-permute-done.24 = bf16[256,7296]{1,0:T(8,128)(2,1)} collective-permute-done((bf16[256,7296]{1,0:T(8,128)(2,1)}, bf16[256,7296]{1,0:T(8,128)(2,1)}, u32[]{:S(2)}, u32[]{:S(2)}) %collective-permute-start.24) | collective-permute-done | bytes 3735584 | tf_op jit(solution)/shard_map/ppermute | solution.py:44
  157.3 4.1 %constant_dynamic-update-slice_fusion = bf16[512,7296]{1,0:T(8,128)(2,1)} fusion(bf16[512,7296]{1,0:T(8,128)(2,1)} %constant_dynamic-update-slice_fusion.1, bf16[256,7296]{1,0:T(8,128)(2,1)} %collective-permute-done.24), kind=kLoop, calls=%fused_computation.91 | loop fusion | bytes 7471104 | tf_op jit(solution)/shard_map/concatenate | solution.py:164
  161.5 1.0 multiply_reduce_fusion
  162.6 5.4 %fusion.6 = f32[512,256]{1,0:T(8,128)S(1)} fusion(bf16[512,7296]{1,0:T(8,128)(2,1)} %constant_dynamic-update-slice_fusion, bf16[1,7168,256]{2,1,0:T(8,128)(2,1)S(1)} %copy-done.11), kind=kOutput, calls=%fused_computation.14 | convolution fusion | flops 1879048192 | bytes 11534336 | tf_op jit(solution)/shard_map/dot_general | solution.py:170
  167.9 0.9 copy-done.12
  168.8 2.1 multiply_convert_fusion.1
  170.9 1.1 fusion.1
  172.4 6.3 %collective-permute-done.25 = bf16[256,7168]{1,0:T(8,128)(2,1)S(1)} collective-permute-done((bf16[256,7168]{1,0:T(8,128)(2,1)S(1)}, bf16[256,7168]{1,0:T(8,128)(2,1)S(1)}, u32[]{:S(2)}, u32[]{:S(2)}) %collective-permute-start.25) | collective-permute-done | bytes 3670048 | tf_op jit(solution)/shard_map/ppermute | solution.py:44
  178.7 1.3 add_convert_fusion
  180.2 2.7 %collective-permute-start.26 = (bf16[64,7168]{1,0:T(8,128)(2,1)S(1)}, bf16[64,7168]{1,0:T(8,128)(2,1)S(1)}, u32[]{:S(2)}, u32[]{:S(2)}) collective-permute-start(bf16[64,7168]{1,0:T(8,128)(2,1)S(1)} %get-tuple-element.5), channel_id=1, source_target_pairs={{0,48},{16,0},{32,16},{48,32},{1,49},{17,1},{33,17},{49,33},{2,50}... | collective-permute-start | bytes 2752520 | tf_op jit(solution)/shard_map/ppermute | solution.py:40
  182.9 1.8 collective-permute-start.27
  184.7 19.0 %collective-permute-done.26 = bf16[64,7168]{1,0:T(8,128)(2,1)S(1)} collective-permute-done((bf16[64,7168]{1,0:T(8,128)(2,1)S(1)}, bf16[64,7168]{1,0:T(8,128)(2,1)S(1)}, u32[]{:S(2)}, u32[]{:S(2)}) %collective-permute-start.26) | collective-permute-done | bytes 917536 | tf_op jit(solution)/shard_map/ppermute | solution.py:40
  203.7 3.7 %collective-permute-done.28 = bf16[64,7168]{1,0:T(8,128)(2,1)S(1)} collective-permute-done((bf16[64,7168]{1,0:T(8,128)(2,1)S(1)}, bf16[64,7168]{1,0:T(8,128)(2,1)S(1)}, u32[]{:S(2)}, u32[]{:S(2)}) %collective-permute-start.28) | collective-permute-done | bytes 917536 | tf_op jit(solution)/shard_map/ppermute | solution.py:40
  207.8 1.3 reshape.218
  209.1 4.2 %all-to-all-start.1 = ((bf16[16,4,7168]{2,1,0:T(4,128)(2,1)}), bf16[16,4,7168]{2,1,0:T(4,128)(2,1)S(1)}, u32[]{:S(2)}, u32[]{:S(2)}) async-start(bf16[16,4,7168]{2,1,0:T(4,128)(2,1)} %reshape.218), calls=%async_computation.1 | async-start | bytes 1835008 | tf_op jit(solution)/shard_map/all_to_all | solution.py:185
  213.3 13.2 %all-to-all-done.1 = bf16[16,4,7168]{2,1,0:T(4,128)(2,1)S(1)} async-done(((bf16[16,4,7168]{2,1,0:T(4,128)(2,1)}), bf16[16,4,7168]{2,1,0:T(4,128)(2,1)S(1)}, u32[]{:S(2)}, u32[]{:S(2)}) %all-to-all-start.1) | async-done | bytes 917536 | tf_op jit(solution)/shard_map/all_to_all | solution.py:185
  (102 shorter events, 14.4 us)
Async XLA Ops:
  0.0 12.5 %copy-start = (bf16[4,64,576]{2,1,0:T(8,128)(2,1)S(1)}, bf16[4,64,576]{2,1,0:T(8,128)(2,1)}, u32[]{:S(2)}) copy-start(bf16[4,64,576]{2,1,0:T(8,128)(2,1)} %param.12) | copy-start | bytes 884740
  0.0 35.0 %collective-permute-start.2 = (bf16[512,128]{1,0:T(8,128)(2,1)}, bf16[512,128]{1,0:T(8,128)(2,1)S(1)}, u32[]{:S(2)}, u32[]{:S(2)}) collective-permute-start(bf16[512,128]{1,0:T(8,128)(2,1)} %bitcast.110), channel_id=1, source_target_pairs={{0,3},{1,0},{2,1},{3,2},{4,7},{5,4},{6,5},{7,6},{8,11},{9,8},{10,9... | collective-permute-start | bytes 393224 | tf_op jit(solution)/shard_map/ppermute | solution.py:40
  4.1 32.4 %collective-permute-start.1 = (bf16[512,128]{1,0:T(8,128)(2,1)}, bf16[512,128]{1,0:T(8,128)(2,1)S(1)}, u32[]{:S(2)}, u32[]{:S(2)}) collective-permute-start(bf16[512,128]{1,0:T(8,128)(2,1)} %bitcast.111), channel_id=1, source_target_pairs={{0,2},{1,3},{2,0},{3,1},{4,6},{5,7},{6,4},{7,5},{8,10},{9,11},{10,... | collective-permute-start | bytes 393224 | tf_op jit(solution)/shard_map/ppermute | solution.py:40
  4.1 33.0 %collective-permute-start = (bf16[512,128]{1,0:T(8,128)(2,1)}, bf16[512,128]{1,0:T(8,128)(2,1)S(1)}, u32[]{:S(2)}, u32[]{:S(2)}) collective-permute-start(bf16[512,128]{1,0:T(8,128)(2,1)} %bitcast.112), channel_id=1, source_target_pairs={{0,1},{1,2},{2,3},{3,0},{4,5},{5,6},{6,7},{7,4},{8,9},{9,10},{10,1... | collective-permute-start | bytes 393224 | tf_op jit(solution)/shard_map/ppermute | solution.py:40
  8.3 33.3 %collective-permute-start.9 = (bf16[4,1920]{1,0:T(4,128)(2,1)}, bf16[4,1920]{1,0:T(4,128)(2,1)S(1)}, u32[]{:S(2)}, u32[]{:S(2)}) collective-permute-start(bf16[4,1920]{1,0:T(4,128)(2,1)} %get-tuple-element.30), channel_id=1, source_target_pairs={{0,1},{1,2},{2,3},{3,0},{4,5},{5,6},{6,7},{7,4},{8,9},{9,10},{10,1... | collective-permute-start | bytes 46088 | tf_op jit(solution)/shard_map/ppermute | solution.py:40
  10.5 33.4 %collective-permute-start.10 = (bf16[4,1920]{1,0:T(4,128)(2,1)}, bf16[4,1920]{1,0:T(4,128)(2,1)}, u32[]{:S(2)}, u32[]{:S(2)}) collective-permute-start(bf16[4,1920]{1,0:T(4,128)(2,1)} %get-tuple-element.31), channel_id=1, source_target_pairs={{0,2},{1,3},{2,0},{3,1},{4,6},{5,7},{6,4},{7,5},{8,10},{9,11},{10,... | collective-permute-start | bytes 46088 | tf_op jit(solution)/shard_map/ppermute | solution.py:40
  24.0 11.0 %copy-start.9 = (bf16[4,1920]{1,0:T(4,128)(2,1)S(1)}, bf16[4,1920]{1,0:T(4,128)(2,1)}, u32[]{:S(2)}) copy-start(bf16[4,1920]{1,0:T(4,128)(2,1)} %get-tuple-element.32) | copy-start | bytes 46084
  24.0 15.8 %copy-start.8 = (bf16[1,512,128]{2,1,0:T(8,128)(2,1)S(1)}, bf16[1,512,128]{2,1,0:T(8,128)(2,1)}, u32[]{:S(2)}) copy-start(bf16[1,512,128]{2,1,0:T(8,128)(2,1)} %param.16) | copy-start | bytes 393220
  25.0 15.7 %all-to-all-start = ((bf16[16,16,512]{2,1,0:T(8,128)(2,1)}), bf16[16,16,512]{2,1,0:T(8,128)(2,1)S(1)}, u32[]{:S(2)}, u32[]{:S(2)}) async-start(bf16[16,16,512]{2,1,0:T(8,128)(2,1)} %reshape.215), calls=%async_computation | async-start | bytes 524288 | tf_op jit(solution)/shard_map/all_to_all | solution.py:123
  35.0 10.2 %collective-permute-start.11 = (bf16[4,1920]{1,0:T(4,128)(2,1)S(1)}, bf16[4,1920]{1,0:T(4,128)(2,1)S(1)}, u32[]{:S(2)}, u32[]{:S(2)}) collective-permute-start(bf16[4,1920]{1,0:T(4,128)(2,1)S(1)} %copy-done.9), channel_id=1, source_target_pairs={{0,3},{1,0},{2,1},{3,2},{4,7},{5,4},{6,5},{7,6},{8,11},{9,8},{10,9... | collective-permute-start | bytes 46088 | tf_op jit(solution)/shard_map/ppermute | solution.py:40
  36.6 20.8 %collective-permute-start.6 = (bf16[128,1792]{1,0:T(8,128)(2,1)}, bf16[128,1792]{1,0:T(8,128)(2,1)}, u32[]{:S(2)}, u32[]{:S(2)}) collective-permute-start(bf16[128,1792]{1,0:T(8,128)(2,1)} %get-tuple-element.9), channel_id=1, source_target_pairs={{0,1},{1,2},{2,3},{3,0},{4,5},{5,6},{6,7},{7,4},{8,9},{9,10},{10,1... | collective-permute-start | bytes 1376264 | tf_op jit(solution)/shard_map/ppermute | solution.py:40
  37.1 20.2 %collective-permute-start.8 = (bf16[128,1792]{1,0:T(8,128)(2,1)}, bf16[128,1792]{1,0:T(8,128)(2,1)}, u32[]{:S(2)}, u32[]{:S(2)}) collective-permute-start(bf16[128,1792]{1,0:T(8,128)(2,1)} %get-tuple-element.10), channel_id=1, source_target_pairs={{0,3},{1,0},{2,1},{3,2},{4,7},{5,4},{6,5},{7,6},{8,11},{9,8},{10,9... | collective-permute-start | bytes 1376264 | tf_op jit(solution)/shard_map/ppermute | solution.py:40
  41.6 15.8 %collective-permute-start.7 = (bf16[128,1792]{1,0:T(8,128)(2,1)S(1)}, bf16[128,1792]{1,0:T(8,128)(2,1)S(1)}, u32[]{:S(2)}, u32[]{:S(2)}) collective-permute-start(bf16[128,1792]{1,0:T(8,128)(2,1)S(1)} %get-tuple-element.11), channel_id=1, source_target_pairs={{0,2},{1,3},{2,0},{3,1},{4,6},{5,7},{6,4},{7,5},{8,10},{9,11},{10,... | collective-permute-start | bytes 1376264 | tf_op jit(solution)/shard_map/ppermute | solution.py:40
  43.9 8.6 %collective-permute-start.4 = (bf16[64,512]{1,0:T(8,128)(2,1)S(1)}, bf16[64,512]{1,0:T(8,128)(2,1)S(1)}, u32[]{:S(2)}, u32[]{:S(2)}) collective-permute-start(bf16[64,512]{1,0:T(8,128)(2,1)S(1)} %get-tuple-element.22), channel_id=1, source_target_pairs={{0,2},{1,3},{2,0},{3,1},{4,6},{5,7},{6,4},{7,5},{8,10},{9,11},{10,... | collective-permute-start | bytes 196616 | tf_op jit(solution)/shard_map/ppermute | solution.py:40
  46.6 8.0 %collective-permute-start.3 = (bf16[64,512]{1,0:T(8,128)(2,1)S(1)}, bf16[64,512]{1,0:T(8,128)(2,1)S(1)}, u32[]{:S(2)}, u32[]{:S(2)}) collective-permute-start(bf16[64,512]{1,0:T(8,128)(2,1)S(1)} %get-tuple-element.22), channel_id=1, source_target_pairs={{0,1},{1,2},{2,3},{3,0},{4,5},{5,6},{6,7},{7,4},{8,9},{9,10},{10,1... | collective-permute-start | bytes 196616 | tf_op jit(solution)/shard_map/ppermute | solution.py:40
  52.5 4.3 %collective-permute-start.5 = (bf16[64,512]{1,0:T(8,128)(2,1)S(1)}, bf16[64,512]{1,0:T(8,128)(2,1)S(1)}, u32[]{:S(2)}, u32[]{:S(2)}) collective-permute-start(bf16[64,512]{1,0:T(8,128)(2,1)S(1)} %get-tuple-element.22), channel_id=1, source_target_pairs={{0,3},{1,0},{2,1},{3,2},{4,7},{5,4},{6,5},{7,6},{8,11},{9,8},{10,9... | collective-permute-start | bytes 196616 | tf_op jit(solution)/shard_map/ppermute | solution.py:40
  57.4 0.8 copy-start.6
  64.2 31.9 %copy-start.10 = (bf16[7168]{0:T(1024)(128)(2,1)S(1)}, bf16[7168]{0:T(1024)(128)(2,1)}, u32[]{:S(2)}) copy-start(bf16[7168]{0:T(1024)(128)(2,1)} %param.18) | copy-start | bytes 43012
  64.5 7.5 %collective-permute-start.12 = (bf16[64,1920]{1,0:T(8,128)(2,1)S(1)}, bf16[64,1920]{1,0:T(8,128)(2,1)S(1)}, u32[]{:S(2)}, u32[]{:S(2)}) collective-permute-start(bf16[64,1920]{1,0:T(8,128)(2,1)S(1)} %get-tuple-element.12), channel_id=1, source_target_pairs={{0,16},{16,32},{32,48},{48,0},{1,17},{17,33},{33,49},{49,1},{2,18}... | collective-permute-start | bytes 737288 | tf_op jit(solution)/shard_map/ppermute | solution.py:40
  66.5 6.2 %collective-permute-start.14 = (bf16[64,1920]{1,0:T(8,128)(2,1)S(1)}, bf16[64,1920]{1,0:T(8,128)(2,1)S(1)}, u32[]{:S(2)}, u32[]{:S(2)}) collective-permute-start(bf16[64,1920]{1,0:T(8,128)(2,1)S(1)} %get-tuple-element.13), channel_id=1, source_target_pairs={{0,48},{16,0},{32,16},{48,32},{1,49},{17,1},{33,17},{49,33},{2,50}... | collective-permute-start | bytes 737288 | tf_op jit(solution)/shard_map/ppermute | solution.py:40
  68.0 8.0 %collective-permute-start.13 = (bf16[64,1920]{1,0:T(8,128)(2,1)S(1)}, bf16[64,1920]{1,0:T(8,128)(2,1)S(1)}, u32[]{:S(2)}, u32[]{:S(2)}) collective-permute-start(bf16[64,1920]{1,0:T(8,128)(2,1)S(1)} %get-tuple-element.14), channel_id=1, source_target_pairs={{0,32},{16,48},{32,0},{48,16},{1,33},{17,49},{33,1},{49,17},{2,34}... | collective-permute-start | bytes 737288 | tf_op jit(solution)/shard_map/ppermute | solution.py:40
  76.1 9.1 %collective-permute-start.17 = (bf16[64,1920]{1,0:T(8,128)(2,1)S(1)}, bf16[64,1920]{1,0:T(8,128)(2,1)S(1)}, u32[]{:S(2)}, u32[]{:S(2)}) collective-permute-start(bf16[64,1920]{1,0:T(8,128)(2,1)S(1)} %fusion.31), channel_id=1, source_target_pairs={{0,12},{4,0},{8,4},{12,8},{1,13},{5,1},{9,5},{13,9},{2,14},{6,2},{... | collective-permute-start | bytes 737288 | tf_op jit(solution)/shard_map/ppermute | solution.py:40
  78.9 7.8 %collective-permute-start.16 = (bf16[64,1920]{1,0:T(8,128)(2,1)S(1)}, bf16[64,1920]{1,0:T(8,128)(2,1)S(1)}, u32[]{:S(2)}, u32[]{:S(2)}) collective-permute-start(bf16[64,1920]{1,0:T(8,128)(2,1)S(1)} %fusion.31), channel_id=1, source_target_pairs={{0,8},{4,12},{8,0},{12,4},{1,9},{5,13},{9,1},{13,5},{2,10},{6,14},... | collective-permute-start | bytes 737288 | tf_op jit(solution)/shard_map/ppermute | solution.py:40
  79.7 9.5 %collective-permute-start.15 = (bf16[64,1920]{1,0:T(8,128)(2,1)S(1)}, bf16[64,1920]{1,0:T(8,128)(2,1)S(1)}, u32[]{:S(2)}, u32[]{:S(2)}) collective-permute-start(bf16[64,1920]{1,0:T(8,128)(2,1)S(1)} %fusion.31), channel_id=1, source_target_pairs={{0,4},{4,8},{8,12},{12,0},{1,5},{5,9},{9,13},{13,1},{2,6},{6,10},{... | collective-permute-start | bytes 737288 | tf_op jit(solution)/shard_map/ppermute | solution.py:40
  89.3 22.9 %collective-permute-start.20 = (bf16[64,1920]{1,0:T(8,128)(2,1)S(1)}, bf16[64,1920]{1,0:T(8,128)(2,1)S(1)}, u32[]{:S(2)}, u32[]{:S(2)}) collective-permute-start(bf16[64,1920]{1,0:T(8,128)(2,1)S(1)} %add_convert_fusion.2), channel_id=1, source_target_pairs={{0,3},{1,0},{2,1},{3,2},{4,7},{5,4},{6,5},{7,6},{8,11},{9,8},{10,9... | collective-permute-start | bytes 737288 | tf_op jit(solution)/shard_map/ppermute | solution.py:40
  95.2 17.1 %collective-permute-start.19 = (bf16[64,1920]{1,0:T(8,128)(2,1)S(1)}, bf16[64,1920]{1,0:T(8,128)(2,1)S(1)}, u32[]{:S(2)}, u32[]{:S(2)}) collective-permute-start(bf16[64,1920]{1,0:T(8,128)(2,1)S(1)} %add_convert_fusion.2), channel_id=1, source_target_pairs={{0,2},{1,3},{2,0},{3,1},{4,6},{5,7},{6,4},{7,5},{8,10},{9,11},{10,... | collective-permute-start | bytes 737288 | tf_op jit(solution)/shard_map/ppermute | solution.py:40
  95.2 22.2 %collective-permute-start.18 = (bf16[64,1920]{1,0:T(8,128)(2,1)S(1)}, bf16[64,1920]{1,0:T(8,128)(2,1)S(1)}, u32[]{:S(2)}, u32[]{:S(2)}) collective-permute-start(bf16[64,1920]{1,0:T(8,128)(2,1)S(1)} %add_convert_fusion.2), channel_id=1, source_target_pairs={{0,1},{1,2},{2,3},{3,0},{4,5},{5,6},{6,7},{7,4},{8,9},{9,10},{10,1... | collective-permute-start | bytes 737288 | tf_op jit(solution)/shard_map/ppermute | solution.py:40
  120.3 15.2 %collective-permute-start.22 = (bf16[64,7296]{1,0:T(8,128)(2,1)S(1)}, bf16[64,7296]{1,0:T(8,128)(2,1)S(1)}, u32[]{:S(2)}, u32[]{:S(2)}) collective-permute-start(bf16[64,7296]{1,0:T(8,128)(2,1)S(1)} %get-tuple-element.15), channel_id=1, source_target_pairs={{0,32},{16,48},{32,0},{48,16},{1,33},{17,49},{33,1},{49,17},{2,34}... | collective-permute-start | bytes 2801672 | tf_op jit(solution)/shard_map/ppermute | solution.py:40
  122.8 22.6 %collective-permute-start.21 = (bf16[64,7296]{1,0:T(8,128)(2,1)S(1)}, bf16[64,7296]{1,0:T(8,128)(2,1)S(1)}, u32[]{:S(2)}, u32[]{:S(2)}) collective-permute-start(bf16[64,7296]{1,0:T(8,128)(2,1)S(1)} %get-tuple-element.15), channel_id=1, source_target_pairs={{0,16},{16,32},{32,48},{48,0},{1,17},{17,33},{33,49},{49,1},{2,18}... | collective-permute-start | bytes 2801672 | tf_op jit(solution)/shard_map/ppermute | solution.py:40
  126.7 21.6 %collective-permute-start.23 = (bf16[64,7296]{1,0:T(8,128)(2,1)S(1)}, bf16[64,7296]{1,0:T(8,128)(2,1)S(1)}, u32[]{:S(2)}, u32[]{:S(2)}) collective-permute-start(bf16[64,7296]{1,0:T(8,128)(2,1)S(1)} %get-tuple-element.15), channel_id=1, source_target_pairs={{0,48},{16,0},{32,16},{48,32},{1,49},{17,1},{33,17},{49,33},{2,50}... | collective-permute-start | bytes 2801672 | tf_op jit(solution)/shard_map/ppermute | solution.py:40
  145.4 5.1 %copy-start.5 = (bf16[64,7296]{1,0:T(8,128)(2,1)}, bf16[64,7296]{1,0:T(8,128)(2,1)S(1)}, u32[]{:S(2)}) copy-start(bf16[64,7296]{1,0:T(8,128)(2,1)S(1)} %collective-permute-done.21) | copy-start | bytes 2801668
  148.3 2.2 copy-start.3
  150.5 6.8 %collective-permute-start.24 = (bf16[256,7296]{1,0:T(8,128)(2,1)}, bf16[256,7296]{1,0:T(8,128)(2,1)}, u32[]{:S(2)}, u32[]{:S(2)}) collective-permute-start(bf16[256,7296]{1,0:T(8,128)(2,1)} %pad_maximum_fusion), channel_id=1, source_target_pairs={{0,64},{64,0},{1,65},{65,1},{2,66},{66,2},{3,67},{67,3},{4,68},{68... | collective-permute-start | bytes 11206664 | tf_op jit(solution)/shard_map/ppermute | solution.py:44
  150.5 3.3 %copy-start.4 = (bf16[64,7296]{1,0:T(8,128)(2,1)S(1)}, bf16[64,7296]{1,0:T(8,128)(2,1)}, u32[]{:S(2)}) copy-start(bf16[64,7296]{1,0:T(8,128)(2,1)} %copy-done.3) | copy-start | bytes 2801668
  154.8 7.7 %copy-start.11 = (bf16[1,7168,256]{2,1,0:T(8,128)(2,1)S(1)}, bf16[1,7168,256]{2,1,0:T(8,128)(2,1)}, u32[]{:S(2)}) copy-start(bf16[1,7168,256]{2,1,0:T(8,128)(2,1)} %param.21) | copy-start | bytes 11010052
  162.5 5.4 %copy-start.7 = (bf16[512,7296]{1,0:T(8,128)(2,1)S(1)}, bf16[512,7296]{1,0:T(8,128)(2,1)}, u32[]{:S(2)}) copy-start(bf16[512,7296]{1,0:T(8,128)(2,1)} %constant_dynamic-update-slice_fusion) | copy-start | bytes 22413316
  162.6 6.2 %copy-start.12 = (bf16[1,7168,256]{2,1,0:T(8,128)(2,1)S(1)}, bf16[1,7168,256]{2,1,0:T(8,128)(2,1)}, u32[]{:S(2)}) copy-start(bf16[1,7168,256]{2,1,0:T(8,128)(2,1)} %param.22) | copy-start | bytes 11010052
  168.8 2.1 copy-start.2
  172.0 6.7 %collective-permute-start.25 = (bf16[256,7168]{1,0:T(8,128)(2,1)S(1)}, bf16[256,7168]{1,0:T(8,128)(2,1)S(1)}, u32[]{:S(2)}, u32[]{:S(2)}) collective-permute-start(bf16[256,7168]{1,0:T(8,128)(2,1)S(1)} %fusion.1), channel_id=1, source_target_pairs={{0,64},{64,0},{1,65},{65,1},{2,66},{66,2},{3,67},{67,3},{4,68},{68... | collective-permute-start | bytes 11010056 | tf_op jit(solution)/shard_map/ppermute | solution.py:44
  180.2 23.5 %collective-permute-start.26 = (bf16[64,7168]{1,0:T(8,128)(2,1)S(1)}, bf16[64,7168]{1,0:T(8,128)(2,1)S(1)}, u32[]{:S(2)}, u32[]{:S(2)}) collective-permute-start(bf16[64,7168]{1,0:T(8,128)(2,1)S(1)} %get-tuple-element.5), channel_id=1, source_target_pairs={{0,48},{16,0},{32,16},{48,32},{1,49},{17,1},{33,17},{49,33},{2,50}... | collective-permute-start | bytes 2752520 | tf_op jit(solution)/shard_map/ppermute | solution.py:40
  182.9 24.4 %collective-permute-start.28 = (bf16[64,7168]{1,0:T(8,128)(2,1)S(1)}, bf16[64,7168]{1,0:T(8,128)(2,1)S(1)}, u32[]{:S(2)}, u32[]{:S(2)}) collective-permute-start(bf16[64,7168]{1,0:T(8,128)(2,1)S(1)} %get-tuple-element.6), channel_id=1, source_target_pairs={{0,16},{16,32},{32,48},{48,0},{1,17},{17,33},{33,49},{49,1},{2,18}... | collective-permute-start | bytes 2752520 | tf_op jit(solution)/shard_map/ppermute | solution.py:40
  182.9 44.7 %copy-start.1 = (bf16[4,64,576]{2,1,0:T(8,128)(2,1)S(1)}, bf16[4,64,576]{2,1,0:T(8,128)(2,1)}, u32[]{:S(2)}) copy-start(bf16[4,64,576]{2,1,0:T(8,128)(2,1)} %param.12) | copy-start | bytes 884740
  182.9 24.4 %collective-permute-start.27 = (bf16[64,7168]{1,0:T(8,128)(2,1)S(1)}, bf16[64,7168]{1,0:T(8,128)(2,1)S(1)}, u32[]{:S(2)}, u32[]{:S(2)}) collective-permute-start(bf16[64,7168]{1,0:T(8,128)(2,1)S(1)} %get-tuple-element.7), channel_id=1, source_target_pairs={{0,32},{16,48},{32,0},{48,16},{1,33},{17,49},{33,1},{49,17},{2,34}... | collective-permute-start | bytes 2752520 | tf_op jit(solution)/shard_map/ppermute | solution.py:40
  209.1 17.5 %all-to-all-start.1 = ((bf16[16,4,7168]{2,1,0:T(4,128)(2,1)}), bf16[16,4,7168]{2,1,0:T(4,128)(2,1)S(1)}, u32[]{:S(2)}, u32[]{:S(2)}) async-start(bf16[16,4,7168]{2,1,0:T(4,128)(2,1)} %reshape.218), calls=%async_computation.1 | async-start | bytes 1835008 | tf_op jit(solution)/shard_map/all_to_all | solution.py:185

commit v2 on v0

v2 whole, which is shorter than its diff:
```python
import functools
import itertools

import jax
import jax.numpy as jnp
from jax import lax
from jax.experimental import pallas as pl
from jax.experimental.pallas import tpu as pltpu
from jax.sharding import PartitionSpec as P

EXPERTS = 16
AXES = ("role", "dev")
SIDE = 4
EXTRA = 128
GROUP = 16
CHUNK = 512

score_scale = 192.0 ** (-0.5)
epsilon = 1e-06
bf16, f32 = jnp.bfloat16, jnp.float32


def device_at(role, a, b, c):
    x, y, z = (a, b, c) if role == 0 else (c, a, b)
    return ((role * SIDE + x) * SIDE + y) * SIDE + z


def groups(along):
    rest = [axis for axis in "abc" if axis not in along]
    out = []
    for role in range(2):
        for fixed in itertools.product(range(SIDE), repeat=len(rest)):
            group = []
            for moving in itertools.product(range(SIDE), repeat=len(along)):
                at = dict(zip(rest, fixed))
                at.update(zip(along, moving))
                group.append(device_at(role, at["a"], at["b"], at["c"]))
            out.append(group)
    return out


def shift(value, axis, step):
    pairs = []
    for group in groups(axis):
        pairs += [(group[i], group[(i + step) % SIDE]) for i in range(SIDE)]
    return lax.ppermute(value, AXES, pairs)


def shifts(value, axis):
    got = {step: shift(value, axis, step) for step in (2, 1, 3)}
    return [value] + [got[step] for step in (1, 2, 3)]


def swap_cores(value):
    return lax.ppermute(value, "role", [(0, 1), (1, 0)])


def call(body, out_shape, args, flops, limit, **given):
    smem = pl.BlockSpec(memory_space=pltpu.SMEM)
    vmem = pl.BlockSpec(memory_space=pltpu.VMEM)
    if "grid" not in given and "grid_spec" not in given:
        given["in_specs"] = [smem] + [vmem] * (len(args) - 1)
        given["out_specs"] = jax.tree.map(lambda _: vmem, out_shape)
    moved = sum(x.size * x.dtype.itemsize for x in [*args, *jax.tree.leaves(out_shape)])
    return pl.pallas_call(
        body,
        out_shape=out_shape,
        compiler_params=pltpu.CompilerParams(vmem_limit_bytes=limit * 2**20),
        cost_estimate=pl.CostEstimate(flops=flops, bytes_accessed=moved, transcendentals=0),
        **given,
    )(*args)


def back(mine, step):
    return lax.rem(mine - step + SIDE, SIDE)


def ahead(mine, step):
    return lax.rem(mine + step, SIDE)


def lanes(at, width):
    return pl.ds(pl.multiple_of(at * width, width), width)


def iota(shape, axis):
    return lax.broadcasted_iota(jnp.int32, shape, axis)


def bundle_kernel(at, w_out, w_uv, residual, ids, gates, *outs):
    c = at[3]
    latent, depth = w_uv.shape[1], w_out.shape[0]
    rows, width = residual.shape
    block = width // SIDE
    weights = jnp.zeros((rows, EXTRA), f32)
    for k in range(ids.shape[1]):
        named = ids[:, k : k + 1] == iota((rows, EXTRA), 1)
        weights = weights + jnp.where(named, gates[:, k : k + 1].astype(f32), 0.0)
    spread = (iota((GROUP, rows), 0) == iota((GROUP, rows), 1)).astype(f32).astype(bf16)

    def place(value):
        return jnp.dot(spread, value, preferred_element_type=f32).astype(bf16)

    weights = place(weights.astype(bf16))
    for step, out in enumerate(outs):
        to = lanes(ahead(c, step), block)
        for k in range(latent // depth):
            out[:depth, k * depth : (k + 1) * depth] = w_uv[0, k * depth : (k + 1) * depth, :]
        out[:depth, latent:] = w_out[:, to]
        out[depth:, :block] = place(residual[:, to])
        out[depth:, block : block + EXTRA] = weights
        if latent > EXTRA:
            out[depth:, block + EXTRA :] = jnp.zeros((GROUP, latent - EXTRA), bf16)


def attend_kernel(lengths, at, query, cache, out, most, norm, mixed, placed):
    row, chunk = pl.program_id(0), pl.program_id(1)
    length = lengths[row]
    heads, latent = mixed.shape
    size = cache.shape[1]

    @pl.when((row == 0) & (chunk == 0))
    def _():
        placed[...] = jnp.zeros_like(placed)

    @pl.when(chunk == 0)
    def _():
        most[...] = jnp.full_like(most, -jnp.inf)
        norm[...] = jnp.zeros_like(norm)
        mixed[...] = jnp.zeros_like(mixed)

    @pl.when(chunk * size < length)
    def _():
        keys = cache[0]
        scores = score_scale * lax.dot_general(
            query[0], keys, (((1,), (1,)), ((), ())), preferred_element_type=f32
        )
        scores = jnp.where(chunk * size + iota(scores.shape, 1) < length, scores, -jnp.inf)
        highest = jnp.maximum(most[...], jnp.max(scores, axis=1, keepdims=True))
        fade = jnp.exp(most[...] - highest)
        shares = jnp.exp(scores - highest)
        most[...] = highest
        norm[...] = norm[...] * fade + jnp.sum(shares, axis=1, keepdims=True)
        mixed[...] = mixed[...] * fade + jnp.dot(
            shares.astype(bf16), keys[:, :latent], preferred_element_type=f32
        )

    @pl.when(chunk == pl.num_programs(1) - 1)
    def _():
        done = (mixed[...] / norm[...]).astype(bf16)
        line, head = iota((placed.shape[0], heads), 0), iota((placed.shape[0], heads), 1)
        a, b, c = line >> 6, (line >> 4) & 3, line & 3
        wanted = jnp.where(at[0] == 0, a * 16 + b * 4 + c, c * 16 + a * 4 + b)
        pick = ((wanted == head) & (((line >> 2) & 3) == row)).astype(f32).astype(bf16)
        placed[...] += jnp.dot(pick, done, preferred_element_type=f32)

        @pl.when(row == pl.num_programs(0) - 1)
        def _():
            out[...] = placed[...].astype(bf16)


def attend(lengths, at, queries, cache):
    rows, heads, width = queries.shape
    cache_length = cache.shape[1]
    size = min(CHUNK, cache_length)
    latent = width - 64
    lines = rows * heads
    grid_spec = pltpu.PrefetchScalarGridSpec(
        num_scalar_prefetch=2,
        grid=(rows, cache_length // size),
        in_specs=[
            pl.BlockSpec((1, heads, width), lambda r, k, lengths, at: (r, 0, 0)),
            pl.BlockSpec(
                (1, size, width),
                lambda r, k, lengths, at: (r, jnp.minimum(k, (lengths[r] - 1) // size), 0),
            ),
        ],
        out_specs=pl.BlockSpec((lines, latent), lambda r, k, lengths, at: (0, 0)),
        scratch_shapes=[
            pltpu.VMEM((heads, 1), f32),
            pltpu.VMEM((heads, 1), f32),
            pltpu.VMEM((heads, latent), f32),
            pltpu.VMEM((lines, latent), f32),
        ],
    )
    return call(
        attend_kernel,
        jax.ShapeDtypeStruct((lines, latent), bf16),
        (lengths, at, queries, cache),
        2 * lines * cache_length * (width + latent),
        16,
        grid_spec=grid_spec,
    )


def heads_kernel(at, latents, w0, w1, w2, w3, out):
    lines = latents.shape[0]
    depth, latent = w0.shape
    line = iota((lines, depth), 0)
    count = lines // SIDE
    gather = (iota((count, lines), 0) == (iota((count, lines), 1) >> 2)).astype(f32).astype(bf16)
    for step, w in enumerate((w0, w1, w2, w3)):
        head = back(at[3], step)
        value = jnp.zeros((lines, depth), f32)
        for k in range(latent // depth):
            span = slice(k * depth, (k + 1) * depth)
            value = value + jnp.dot(latents[:, span], w[:, span], preferred_element_type=f32)
        value = jnp.where((line & 3) == head, value, 0.0).astype(bf16)
        out[head] = jnp.dot(gather, value, preferred_element_type=f32).astype(bf16)


def project_kernel(at, h0, h1, h2, h3, p0, p1, p2, p3, o0, o1, o2, o3, lines):
    packs = (p0, p1, p2, p3)
    heads, _, depth = h0.shape
    block = o0.shape[1] - EXTRA
    latent = p0.shape[1] - block
    a, b, c = at[1], at[2], at[3]
    for step in range(SIDE):
        rows = pl.ds(pl.multiple_of(ahead(a, step) * GROUP, GROUP), GROUP)
        for j, h in enumerate((h0, h1, h2, h3)):
            for k in range(heads):
                lines[step, back(c, j), :, k * depth : (k + 1) * depth] = h[back(c, k), rows, :]
    for step, out in enumerate((o0, o1, o2, o3)):
        left = lines[step].reshape(SIDE * GROUP, heads * depth)
        total = jnp.zeros((SIDE * GROUP, block), f32)
        for k, pack in enumerate(packs):
            total = total + jnp.dot(
                left[:, k * depth : (k + 1) * depth],
                pack[:depth, latent:],
                preferred_element_type=f32,
            )
        out[:, :block] = total.astype(bf16)
        out[:, block:] = jnp.zeros((SIDE * GROUP, EXTRA), bf16)
    move = iota((GROUP, GROUP), 0) == b * 4 + iota((GROUP, GROUP), 1)
    move = (move & (iota((GROUP, GROUP), 1) < 4)).astype(f32).astype(bf16)
    for j, pack in enumerate(packs):
        rows = pl.ds(pl.multiple_of(back(c, j) * GROUP, GROUP), GROUP)
        own = jnp.dot(move, pack[depth:, : block + EXTRA], preferred_element_type=f32)
        o0[rows, :] = (o0[rows, :].astype(f32) + own).astype(bf16)


def norm_kernel(at, s0, s1, s2, s3, gain, out, mine):
    slots = (s0, s1, s2, s3)
    width = gain.shape[1]
    block = width // SIDE
    squares = 0.0
    for slot in slots:
        value = slot[:, :block].astype(f32)
        squares = squares + jnp.sum(value * value, axis=1, keepdims=True)
    factor = lax.rsqrt(squares * (1.0 / width) + epsilon)
    rows = pl.ds(pl.multiple_of(at[3] * GROUP, GROUP), GROUP)
    for step, slot in enumerate(slots):
        to = lanes(back(at[3], step), block)
        out[:, to] = (slot[:, :block].astype(f32) * factor * gain[:, to]).astype(bf16)
        mine[:, to] = slot[rows, :block]
    out[:, width:] = s0[:, block:]


def experts_kernel(count, parts, at, *refs):
    xs, ws, refs = refs[:count], refs[count : 2 * count], refs[2 * count :]
    gates, ups, downs, refs = refs[0:2], refs[2:4], refs[4:6], refs[6:]
    outs, (gate_sum, up_sum, hidden, weights) = refs[:count], refs[count:]
    step = pl.program_id(0)
    units = gates[0].shape[2]
    rows = xs[0].shape[0]

    def joined(refs):
        return refs[0][...] if count == 1 else jnp.concatenate([r[...] for r in refs], axis=0)

    @pl.when(step < parts)
    def _():
        x = joined(xs)
        for k in range(2):
            span = slice(k * units, (k + 1) * units)
            gate = jnp.dot(x, gates[k][0], preferred_element_type=f32)
            up = jnp.dot(x, ups[k][0], preferred_element_type=f32)

            @pl.when(step == 0)
            def _():
                gate_sum[:, span] = gate
                up_sum[:, span] = up

            @pl.when(step > 0)
            def _():
                gate_sum[:, span] += gate
                up_sum[:, span] += up

    @pl.when(step == parts - 1)
    def _():
        gate = gate_sum[...]
        hidden[...] = (gate * (1.0 / (1.0 + jnp.exp(-gate))) * up_sum[...]).astype(bf16)
        told = joined(ws).astype(f32)
        for k in range(2):
            chosen = iota(told.shape, 1) == at[4 + k]
            weight = jnp.sum(jnp.where(chosen, told, 0.0), axis=1, keepdims=True)
            weights[k] = jnp.broadcast_to(weight, told.shape)

    @pl.when(step >= parts)
    def _():
        total = 0.0
        for k in range(2):
            value = jnp.dot(
                hidden[:, k * units : (k + 1) * units], downs[k][0], preferred_element_type=f32
            )
            total = total + value * weights[k][:, 0:1]
        for k, out in enumerate(outs):
            out[...] = total[k * rows : (k + 1) * rows].astype(bf16)


def experts(at, slots, gates, ups, downs):
    count, parts = len(slots), SIDE
    rows = slots[0].shape[0]
    width, units = gates[0].shape[1:]
    block = width // parts

    def first(i):
        return jnp.minimum(i, parts - 1)

    def second(i):
        return jnp.maximum(i - parts, 0)

    in_specs = [pl.BlockSpec(memory_space=pltpu.SMEM)]
    in_specs += [pl.BlockSpec((rows, block), lambda i: (0, first(i)))] * count
    in_specs += [pl.BlockSpec((rows, EXTRA), lambda i: (0, width // EXTRA))] * count
    in_specs += [pl.BlockSpec((1, block, units), lambda i: (0, first(i), 0))] * 4
    in_specs += [pl.BlockSpec((1, units, block), lambda i: (0, 0, second(i)))] * 2
    return call(
        functools.partial(experts_kernel, count, parts),
        [jax.ShapeDtypeStruct((rows, width), bf16)] * count,
        (at, *slots, *slots, *gates, *ups, *downs),
        12 * count * rows * width * units,
        24,
        grid=(2 * parts,),
        in_specs=in_specs,
        out_specs=[pl.BlockSpec((rows, block), lambda i: (0, second(i)))] * count,
        scratch_shapes=[
            pltpu.VMEM((count * rows, 2 * units), f32),
            pltpu.VMEM((count * rows, 2 * units), f32),
            pltpu.VMEM((count * rows, 2 * units), bf16),
            pltpu.VMEM((2, count * rows, EXTRA), f32),
        ],
    )


def on_device(
    queries,
    latent_cache,
    lengths,
    residual,
    w_uv,
    w_out,
    norm_gain,
    expert_ids,
    gate_values,
    w_gate,
    w_up,
    w_down,
):
    role, dev = lax.axis_index("role"), lax.axis_index("dev")
    x, y, z = dev // 16, dev // 4 % 4, dev % 4
    first = role == 0
    a, b, c = jnp.where(first, x, y), jnp.where(first, y, z), jnp.where(first, z, x)
    per_expert = 128 // EXPERTS
    experts_here = [(role * 64 + dev) // per_expert, ((1 - role) * 64 + dev) // per_expert]
    at = jnp.stack([role, a, b, c, *experts_here, role, role]).astype(jnp.int32)
    rows, width = residual.shape
    latent, depth = w_uv.shape[1:]
    block = width // SIDE
    count = GROUP * SIDE

    shape = jax.ShapeDtypeStruct((depth + GROUP, latent + block), bf16)
    packs = call(
        bundle_kernel,
        [shape] * SIDE,
        (at, w_out, w_uv, residual, expert_ids, gate_values),
        0,
        16,
    )
    packs = [packs[0]] + [shift(packs[s], "c", s) for s in (1, 2, 3)]
    gates, ups, downs = [(w, swap_cores(w)) for w in (w_gate, w_up, w_down)]

    sent = attend(lengths, at, queries, latent_cache).reshape(16, SIDE * rows, latent)
    got = lax.all_to_all(sent, AXES, 0, 0, axis_index_groups=groups("ab"), tiled=True)
    got = got.reshape(-1, latent)
    vmem = pl.BlockSpec(memory_space=pltpu.VMEM)
    head_out = call(
        heads_kernel,
        jax.ShapeDtypeStruct((SIDE, count, depth), bf16),
        (at, got, *packs),
        2 * SIDE * got.size * depth,
        16,
        grid=(1,),
        in_specs=[pl.BlockSpec(memory_space=pltpu.SMEM), vmem]
        + [pl.BlockSpec((depth, latent), lambda i: (0, 0))] * SIDE,
        out_specs=vmem,
    )
    gathered = shifts(head_out, "c")
    partial = call(
        project_kernel,
        [jax.ShapeDtypeStruct((count, block + EXTRA), bf16)] * SIDE,
        (at, *gathered, *packs),
        2 * SIDE * count * SIDE * depth * block,
        24,
        scratch_shapes=[pltpu.VMEM((SIDE, SIDE, GROUP, SIDE * depth), bf16)],
    )

    def added(parts):
        return functools.reduce(lambda u, v: u + v, [p.astype(f32) for p in parts]).astype(bf16)

    total = added([partial[0]] + [shift(partial[s], "a", s) for s in (2, 1, 3)])
    attended = added(shifts(total, "b"))
    columns = shifts(attended, "c")
    normed, mine = call(
        norm_kernel,
        [
            jax.ShapeDtypeStruct((count, width + EXTRA), bf16),
            jax.ShapeDtypeStruct((GROUP, width), bf16),
        ],
        (at, *columns, norm_gain.astype(f32).reshape(1, width)),
        0,
        16,
    )

    near = [shift(normed, "a", s) for s in (1, 3)]
    far = shift(normed, "a", 2)
    run = functools.partial(experts, at, gates=gates, ups=ups, downs=downs)
    (own_sum,) = run([normed])
    near_sums = run(near)
    (far_sum,) = run([far])
    sums = [shift(near_sums[0], "a", -1), shift(near_sums[1], "a", -3), shift(far_sum, "a", -2)]
    last = added([own_sum] + sums).reshape(16, rows, width)
    last = lax.all_to_all(last, AXES, 0, 0, axis_index_groups=groups("cb"), tiled=True)
    combined = jnp.sum(last.astype(f32), axis=0)
    mine = lax.dynamic_slice_in_dim(mine, b * rows, rows, 0)
    return (mine.astype(f32) + combined).astype(bf16)


def solution(mesh):
    return jax.shard_map(
        on_device,
        mesh=mesh,
        in_specs=(
            P(("role", "dev"), None, None),
            P(("role", "dev"), None, None),
            P(("role", "dev")),
            P(("role", "dev"), None),
            P("dev", None, None),
            P("dev", None),
            P(),
            P(("role", "dev"), None),
            P(("role", "dev"), None),
            P(("role", "dev"), None, None),
            P(("role", "dev"), None, None),
            P(("role", "dev"), None, None),
        ),
        out_specs=P(("role", "dev"), None),
        check_vma=False,
    )
```

time: 1040 us -> 178 us (0.17)
  blocking collectives: 648 us -> 14.4 us
  waiting for transfers between devices: 318 us -> 64 us
  matrix products: 41.8 us -> 0 us
  starting transfers between devices: 0.09 us -> 37.5 us
  Pallas kernels: 0 us -> 34.8 us
  between operations: 13.9 us -> 0.17 us
    all_gather x2 -> x0, blocking collectives: 627 us -> none  [the longest x1 315 us: on_device(): lax.all_gather(gate_values, ('role', 'dev'), axis=0, tiled=True)]
    unnamed x5 -> x0, waiting for transfers between devices: 318 us -> none
    ppermute x0 -> x24, waiting for transfers between devices: none -> 51.6 us  [the longest x21 51.6 us: shift(): return lax.ppermute(value, AXES, pairs)]
    dot_general x5 -> x0, matrix products: 41.8 us -> none  [the longest x1 18.2 us: on_device(): jnp.dot(hidden, down_local, preferred_element_type=jnp.float32)]
    pallas_call x0 -> x8, Pallas kernels: none -> 34.8 us  [call(): pl.pallas_call(body, out_shape=out_shape, compiler_params=pltpu.CompilerP...]
    ppermute x0 -> x24, starting transfers between devices: none -> 33.6 us  [the longest x21 33.1 us: shift(): return lax.ppermute(value, AXES, pairs)]
    all_to_all x0 -> x1, waiting for transfers between devices: none -> 12.5 us  [on_device(): lax.all_to_all(last, AXES, 0, 0, axis_index_groups=groups('cb'), tiled=True)]
    unnamed x20 -> x25, local copies, waits for them, and re-layouts: 14.7 us -> 22.8 us
  transfers between devices with their start and end apart: 3 -> 25, of which waited for: 2 -> 13; matrix products, arithmetic and copies ran while one was open for 0% -> 8% of each run, Pallas kernels for 0% -> 16%
where the time goes in v2:
time: 178 us; the launch traced here: 177 us
  waiting for transfers between devices  64 us (36%)
  starting transfers between devices  37.5 us (21%)
  Pallas kernels  34.8 us (20%)
  local copies, waits for them, and re-layouts  24.1 us (14%)
  blocking collectives  14.4 us (8%)
    ppermute x21, waiting for transfers between devices, shift(): return lax.ppermute(value, AXES, pairs)  51.6 us
    pallas_call x8, Pallas kernels, call(): pl.pallas_call(body, out_shape=out_shape, compiler_params=pltpu.CompilerP...  34.8 us
    ppermute x21, starting transfers between devices, shift(): return lax.ppermute(value, AXES, pairs)  33.1 us
    unnamed x25, local copies, waits for them, and re-layouts  22.8 us
    all_to_all x1, blocking collectives, on_device(): lax.all_to_all(sent, AXES, 0, 0, axis_index_groups=groups('ab'), tiled=True)  14.4 us
    all_to_all x1, waiting for transfers between devices, on_device(): lax.all_to_all(last, AXES, 0, 0, axis_index_groups=groups('cb'), tiled=True)  12.5 us
    all_to_all x1, starting transfers between devices, on_device(): lax.all_to_all(last, AXES, 0, 0, axis_index_groups=groups('cb'), tiled=True)  3.86 us
  transfers between devices with their start and end apart: 25, of which 13 were waited for; matrix products, arithmetic and copies ran while one was open for 8% of the time, Pallas kernels for 16%

profile of v2, /device:TPU:0, one launch (start us, length us, event | category | flops | bytes accessed | tf_op | source)
XLA Modules:
  0.0 176.8 jit_solution(17822598347609595702)
XLA Ops:
  0.0 0.1 stack.29.at
  0.1 1.5 copy-done.4
  1.6 0.9 copy-done.6
  2.5 0.8 copy-done.7
  3.3 0.7 copy-done.8
  4.0 0.7 copy-done.9
  4.7 2.2 %shard_map.119 = (bf16[144,2304]{1,0:T(8,128)(2,1)S(1)}, bf16[144,2304]{1,0:T(8,128)(2,1)}, bf16[144,2304]{1,0:T(8,128)(2,1)}, bf16[144,2304]{1,0:T(8,128)(2,1)}) custom-call(s32[8]{0:T(128)S(1)} %stack.29.at, bf16[128,7168]{1,0:T(8,128)(2,1)S(1)} %copy-done.4, bf16[1,512,128]{2,1,0:T(8,128)(2,1)S(1)} %copy-done.6, bf16[4,7168]{1,0:T(4,128)(2,1)S(1)} %copy-done.7, ...), custom_call_target="tpu_custom_call" | custom-call | bytes 4677856 | tf_op jit(solution)/shard_map/pallas_call | solution.py:65
  6.8 2.0 %collective-permute-start = (bf16[144,2304]{1,0:T(8,128)(2,1)}, bf16[144,2304]{1,0:T(8,128)(2,1)S(1)}, u32[]{:S(2)}, u32[]{:S(2)}) collective-permute-start(bf16[144,2304]{1,0:T(8,128)(2,1)} %get-tuple-element.18), channel_id=1, source_target_pairs={{0,1},{1,2},{2,3},{3,0},{4,5},{5,6},{6,7},{7,4},{8,9},{9,10},{10,1... | collective-permute-start | bytes 1990664 | tf_op jit(solution)/shard_map/ppermute | solution.py:46
  8.8 3.6 %collective-permute-start.1 = (bf16[144,2304]{1,0:T(8,128)(2,1)}, bf16[144,2304]{1,0:T(8,128)(2,1)S(1)}, u32[]{:S(2)}, u32[]{:S(2)}) collective-permute-start(bf16[144,2304]{1,0:T(8,128)(2,1)} %get-tuple-element.19), channel_id=1, source_target_pairs={{0,2},{1,3},{2,0},{3,1},{4,6},{5,7},{6,4},{7,5},{8,10},{9,11},{10,... | collective-permute-start | bytes 1990664 | tf_op jit(solution)/shard_map/ppermute | solution.py:46
  12.4 1.0 collective-permute-start.2
  13.4 14.2 %copy.13.cache = bf16[4,2048,576]{2,1,0:T(8,128)(2,1)} copy(bf16[4,2048,576]{1,2,0:T(8,128)(2,1)} %param.13) | data formatting | bytes 18874368 | tf_op args[1]
  27.6 4.0 %copy-done = bf16[4,2048,576]{2,1,0:T(8,128)(2,1)S(1)} copy-done((bf16[4,2048,576]{2,1,0:T(8,128)(2,1)S(1)}, bf16[4,2048,576]{2,1,0:T(8,128)(2,1)}, u32[]{:S(2)}) %copy-start) | copy-done | bytes 9437208
  31.6 6.4 %shard_map.118 = bf16[256,512]{1,0:T(8,128)(2,1)S(1)} custom-call(s32[4]{0:T(128)S(1)} %copy-done.10, s32[8]{0:T(128)S(1)} %stack.29.at, bf16[4,64,576]{2,1,0:T(8,128)(2,1)S(1)} %copy-done.5, bf16[4,2048,576]{2,1,0:T(8,128)(2,1)S(1)} %copy-done), custom_call_target="tpu_custom_call" | custom-call | flops 1140850688 | bytes 9994288 | tf_op jit(solution)/shard_map/pallas_call | solution.py:65
  38.0 14.4 %all_to_all.10 = bf16[16,16,512]{2,1,0:T(8,128)(2,1)S(1)} all-to-all(bf16[16,16,512]{2,1,0:T(8,128)(2,1)S(1)} %bitcast.10), channel_id=1, replica_groups={{0,4,8,12,16,20,24,28,32,36,40,44,48,52,56,60},{1,5,9,13,17,21,25,29,33..., dimensions={0} | all-to-all | bytes 524288 | tf_op jit(solution)/shard_map/all_to_all | solution.py:383
  52.5 0.0 collective-permute-done.w1.p1
  52.5 0.0 collective-permute-done.1.w2.p2
  52.5 0.0 copy-start.1
  52.5 1.7 shard_map.120.h0
  54.2 3.3 %collective-permute-start.3 = (bf16[4,64,128]{2,1,0:T(8,128)(2,1)S(1)}, bf16[4,64,128]{2,1,0:T(8,128)(2,1)S(1)}, u32[]{:S(2)}, u32[]{:S(2)}) collective-permute-start(bf16[4,64,128]{2,1,0:T(8,128)(2,1)S(1)} %shard_map.120.h0), channel_id=1, source_target_pairs={{0,1},{1,2},{2,3},{3,0},{4,5},{5,6},{6,7},{7,4},{8,9},{9,10},{10,1... | collective-permute-start | bytes 196616 | tf_op jit(solution)/shard_map/ppermute | solution.py:46
  57.5 1.0 collective-permute-start.4
  58.5 1.7 collective-permute-start.5
  60.3 0.0 collective-permute-done.3.h1
  60.3 3.0 %collective-permute-done.4.h2 = bf16[4,64,128]{2,1,0:T(8,128)(2,1)S(1)} collective-permute-done((bf16[4,64,128]{2,1,0:T(8,128)(2,1)S(1)}, bf16[4,64,128]{2,1,0:T(8,128)(2,1)S(1)}, u32[]{:S(2)}, u32[]{:S(2)}) %collective-permute-start.4) | collective-permute-done | bytes 65568 | tf_op jit(solution)/shard_map/ppermute | solution.py:46
  63.3 1.7 shard_map.121
  65.0 0.0 copy-start.11
  65.0 1.4 collective-permute-start.6
  66.5 0.6 collective-permute-start.7
  67.1 2.6 %collective-permute-start.8 = (bf16[64,1920]{1,0:T(8,128)(2,1)S(1)}, bf16[64,1920]{1,0:T(8,128)(2,1)S(1)}, u32[]{:S(2)}, u32[]{:S(2)}) collective-permute-start(bf16[64,1920]{1,0:T(8,128)(2,1)S(1)} %get-tuple-element.24), channel_id=1, source_target_pairs={{0,48},{16,0},{32,16},{48,32},{1,49},{17,1},{33,17},{49,33},{2,50}... | collective-permute-start | bytes 737288 | tf_op jit(solution)/shard_map/ppermute | solution.py:46
  69.7 0.5 collective-permute-start.16
  70.2 2.7 %collective-permute-done.6 = bf16[64,1920]{1,0:T(8,128)(2,1)S(1)} collective-permute-done((bf16[64,1920]{1,0:T(8,128)(2,1)S(1)}, bf16[64,1920]{1,0:T(8,128)(2,1)S(1)}, u32[]{:S(2)}, u32[]{:S(2)}) %collective-permute-start.6) | collective-permute-done | bytes 245792 | tf_op jit(solution)/shard_map/ppermute | solution.py:46
  72.9 0.0 collective-permute-start.17
  72.9 2.5 %collective-permute-done.7 = bf16[64,1920]{1,0:T(8,128)(2,1)S(1)} collective-permute-done((bf16[64,1920]{1,0:T(8,128)(2,1)S(1)}, bf16[64,1920]{1,0:T(8,128)(2,1)S(1)}, u32[]{:S(2)}, u32[]{:S(2)}) %collective-permute-start.7) | collective-permute-done | bytes 245792 | tf_op jit(solution)/shard_map/ppermute | solution.py:46
  75.5 0.1 add_convert_fusion.2
  75.6 1.6 collective-permute-start.10
  77.2 1.6 collective-permute-start.11
  78.8 4.6 %collective-permute-done.10 = bf16[64,1920]{1,0:T(8,128)(2,1)S(1)} collective-permute-done((bf16[64,1920]{1,0:T(8,128)(2,1)S(1)}, bf16[64,1920]{1,0:T(8,128)(2,1)S(1)}, u32[]{:S(2)}, u32[]{:S(2)}) %collective-permute-start.10) | collective-permute-done | bytes 245792 | tf_op jit(solution)/shard_map/ppermute | solution.py:46
  83.4 0.5 collective-permute-start.9
  83.9 0.5 collective-permute-done.11
  84.4 6.4 %collective-permute-done.9 = bf16[64,1920]{1,0:T(8,128)(2,1)S(1)} collective-permute-done((bf16[64,1920]{1,0:T(8,128)(2,1)S(1)}, bf16[64,1920]{1,0:T(8,128)(2,1)S(1)}, u32[]{:S(2)}, u32[]{:S(2)}) %collective-permute-start.9) | collective-permute-done | bytes 245792 | tf_op jit(solution)/shard_map/ppermute | solution.py:46
  90.8 0.1 add_convert_fusion.1.s0
  90.9 0.7 collective-permute-start.12
  91.6 3.3 %collective-permute-start.13 = (bf16[64,1920]{1,0:T(8,128)(2,1)S(1)}, bf16[64,1920]{1,0:T(8,128)(2,1)S(1)}, u32[]{:S(2)}, u32[]{:S(2)}) collective-permute-start(bf16[64,1920]{1,0:T(8,128)(2,1)S(1)} %add_convert_fusion.1.s0), channel_id=1, source_target_pairs={{0,2},{1,3},{2,0},{3,1},{4,6},{5,7},{6,4},{7,5},{8,10},{9,11},{10,... | collective-permute-start | bytes 737288 | tf_op jit(solution)/shard_map/ppermute | solution.py:46
  94.9 3.5 %collective-permute-done.12.s1 = bf16[64,1920]{1,0:T(8,128)(2,1)S(1)} collective-permute-done((bf16[64,1920]{1,0:T(8,128)(2,1)S(1)}, bf16[64,1920]{1,0:T(8,128)(2,1)S(1)}, u32[]{:S(2)}, u32[]{:S(2)}) %collective-permute-start.12) | collective-permute-done | bytes 245792 | tf_op jit(solution)/shard_map/ppermute | solution.py:46
  98.4 1.3 collective-permute-start.14
  99.6 2.1 %collective-permute-done.13.s2 = bf16[64,1920]{1,0:T(8,128)(2,1)S(1)} collective-permute-done((bf16[64,1920]{1,0:T(8,128)(2,1)S(1)}, bf16[64,1920]{1,0:T(8,128)(2,1)S(1)}, u32[]{:S(2)}, u32[]{:S(2)}) %collective-permute-start.13) | collective-permute-done | bytes 245792 | tf_op jit(solution)/shard_map/ppermute | solution.py:46
  101.7 2.9 %collective-permute-done.14.s3 = bf16[64,1920]{1,0:T(8,128)(2,1)S(1)} collective-permute-done((bf16[64,1920]{1,0:T(8,128)(2,1)S(1)}, bf16[64,1920]{1,0:T(8,128)(2,1)S(1)}, u32[]{:S(2)}, u32[]{:S(2)}) %collective-permute-start.14) | collective-permute-done | bytes 245792 | tf_op jit(solution)/shard_map/ppermute | solution.py:46
  104.6 1.0 shard_map.122
  105.6 0.3 collective-permute-start.18
  105.9 3.0 %collective-permute-start.19 = (bf16[64,7296]{1,0:T(8,128)(2,1)S(1)}, bf16[64,7296]{1,0:T(8,128)(2,1)S(1)}, u32[]{:S(2)}, u32[]{:S(2)}) collective-permute-start(bf16[64,7296]{1,0:T(8,128)(2,1)S(1)} %get-tuple-element.26.refs_0_.refs_1_), channel_id=1, source_target_pairs={{0,48},{16,0},{32,16},{48,32},{1,49},{17,1},{33,17},{49,33},{2,50}... | collective-permute-start | bytes 2801672 | tf_op jit(solution)/shard_map/ppermute | solution.py:46
  108.9 11.5 %collective-permute-done.18.refs_0_.refs_2_ = bf16[64,7296]{1,0:T(8,128)(2,1)S(1)} collective-permute-done((bf16[64,7296]{1,0:T(8,128)(2,1)S(1)}, bf16[64,7296]{1,0:T(8,128)(2,1)S(1)}, u32[]{:S(2)}, u32[]{:S(2)}) %collective-permute-start.18) | collective-permute-done | bytes 933920 | tf_op jit(solution)/shard_map/ppermute | solution.py:46
  120.4 0.1 collective-permute-start.22
  120.6 7.3 %shard_map.124 = (bf16[64,7168]{1,0:T(8,128)(2,1)S(1)}, bf16[64,7168]{1,0:T(8,128)(2,1)S(1)}) custom-call(s32[8]{0:T(128)S(1)} %stack.29.at, bf16[64,7296]{1,0:T(8,128)(2,1)S(1)} %collective-permute-done.18.refs_0_.refs_2_, bf16[64,7296]{1,0:T(8,128)(2,1)S(1)} %collective-permute-done.19.refs_1_.refs_3_, ...), custom_call_target="tpu_custom_call" | custom-call | flops 2818572288 | bytes 27590688 | tf_op jit(solution)/shard_map/pallas_call | solution.py:65
  127.9 3.2 %collective-permute-start.20 = (bf16[64,7168]{1,0:T(8,128)(2,1)S(1)}, bf16[64,7168]{1,0:T(8,128)(2,1)S(1)}, u32[]{:S(2)}, u32[]{:S(2)}) collective-permute-start(bf16[64,7168]{1,0:T(8,128)(2,1)S(1)} %get-tuple-element.27), channel_id=1, source_target_pairs={{0,48},{16,0},{32,16},{48,32},{1,49},{17,1},{33,17},{49,33},{2,50}... | collective-permute-start | bytes 2752520 | tf_op jit(solution)/shard_map/ppermute | solution.py:46
  131.1 4.4 %collective-permute-done.22.refs_0_.refs_1_ = bf16[64,7296]{1,0:T(8,128)(2,1)S(1)} collective-permute-done((bf16[64,7296]{1,0:T(8,128)(2,1)S(1)}, bf16[64,7296]{1,0:T(8,128)(2,1)S(1)}, u32[]{:S(2)}, u32[]{:S(2)}) %collective-permute-start.22) | collective-permute-done | bytes 933920 | tf_op jit(solution)/shard_map/ppermute | solution.py:46
  135.5 7.2 %shard_map.125 = bf16[64,7168]{1,0:T(8,128)(2,1)S(1)} custom-call(s32[8]{0:T(128)S(1)} %stack.29.at, bf16[64,7296]{1,0:T(8,128)(2,1)S(1)} %collective-permute-done.22.refs_0_.refs_1_, bf16[64,7296]{1,0:T(8,128)(2,1)S(1)} %collective-permute-done.22.refs_0_.refs_1_, bf16[1,7168,256]{2,1,0:T(8,128)(2,1)S(1)} %copy-done.1, ...), custom_call_target="tpu_custom_call" | custom-call | flops 1409286144 | bytes 24805408 | tf_op jit(solution)/shard_map/pallas_call | solution.py:65
  142.7 0.3 collective-permute-start.23
  143.0 7.2 %shard_map.123 = bf16[64,7168]{1,0:T(8,128)(2,1)S(1)} custom-call(s32[8]{0:T(128)S(1)} %stack.29.at, bf16[64,7296]{1,0:T(8,128)(2,1)S(1)} %get-tuple-element.26.refs_0_.refs_1_, bf16[64,7296]{1,0:T(8,128)(2,1)S(1)} %get-tuple-element.26.refs_0_.refs_1_, bf16[1,7168,256]{2,1,0:T(8,128)(2,1)S(1)} %copy-done.1, ...), custom_call_target="tpu_custom_call" | custom-call | flops 1409286144 | bytes 24805408 | tf_op jit(solution)/shard_map/pallas_call | solution.py:65
  150.2 7.5 %collective-permute-done.23 = bf16[64,7168]{1,0:T(8,128)(2,1)S(1)} collective-permute-done((bf16[64,7168]{1,0:T(8,128)(2,1)S(1)}, bf16[64,7168]{1,0:T(8,128)(2,1)S(1)}, u32[]{:S(2)}, u32[]{:S(2)}) %collective-permute-start.23) | collective-permute-done | bytes 917536 | tf_op jit(solution)/shard_map/ppermute | solution.py:46
  157.7 0.5 add_convert_fusion
  158.1 1.3 reshape.18
  159.4 3.9 %all-to-all-start.1 = ((bf16[16,4,7168]{2,1,0:T(4,128)(2,1)}), bf16[16,4,7168]{2,1,0:T(4,128)(2,1)S(1)}, u32[]{:S(2)}, u32[]{:S(2)}) async-start(bf16[16,4,7168]{2,1,0:T(4,128)(2,1)} %reshape.18), calls=%async_computation.1 | async-start | bytes 1835008 | tf_op jit(solution)/shard_map/all_to_all | solution.py:432
  163.3 12.5 %all-to-all-done.1 = bf16[16,4,7168]{2,1,0:T(4,128)(2,1)S(1)} async-done(((bf16[16,4,7168]{2,1,0:T(4,128)(2,1)}), bf16[16,4,7168]{2,1,0:T(4,128)(2,1)S(1)}, u32[]{:S(2)}, u32[]{:S(2)}) %all-to-all-start.1) | async-done | bytes 917536 | tf_op jit(solution)/shard_map/all_to_all | solution.py:432
  175.8 0.4 convert_reduce_fusion
  176.1 0.7 add_convert_fusion.3
  (28 shorter events, 0.1 us)
Async XLA Ops:
  0.1 1.5 copy-start.4
  1.6 0.9 copy-start.6
  2.5 0.8 copy-start.7
  3.3 0.7 copy-start.8
  4.0 0.7 copy-start.9
  6.8 45.6 %collective-permute-start = (bf16[144,2304]{1,0:T(8,128)(2,1)}, bf16[144,2304]{1,0:T(8,128)(2,1)S(1)}, u32[]{:S(2)}, u32[]{:S(2)}) collective-permute-start(bf16[144,2304]{1,0:T(8,128)(2,1)} %get-tuple-element.18), channel_id=1, source_target_pairs={{0,1},{1,2},{2,3},{3,0},{4,5},{5,6},{6,7},{7,4},{8,9},{9,10},{10,1... | collective-permute-start | bytes 1990664 | tf_op jit(solution)/shard_map/ppermute | solution.py:46
  8.8 43.6 %collective-permute-start.1 = (bf16[144,2304]{1,0:T(8,128)(2,1)}, bf16[144,2304]{1,0:T(8,128)(2,1)S(1)}, u32[]{:S(2)}, u32[]{:S(2)}) collective-permute-start(bf16[144,2304]{1,0:T(8,128)(2,1)} %get-tuple-element.19), channel_id=1, source_target_pairs={{0,2},{1,3},{2,0},{3,1},{4,6},{5,7},{6,4},{7,5},{8,10},{9,11},{10,... | collective-permute-start | bytes 1990664 | tf_op jit(solution)/shard_map/ppermute | solution.py:46
  12.4 15.2 %copy-start.5 = (bf16[4,64,576]{2,1,0:T(8,128)(2,1)S(1)}, bf16[4,64,576]{2,1,0:T(8,128)(2,1)}, u32[]{:S(2)}) copy-start(bf16[4,64,576]{2,1,0:T(8,128)(2,1)} %query.1) | copy-start | bytes 884740
  12.4 15.2 %copy-start.10 = (s32[4]{0:T(128)S(1)}, s32[4]{0:T(128)}, u32[]{:S(2)}) copy-start(s32[4]{0:T(128)} %lengths.1) | copy-start | bytes 52
  12.4 40.0 %collective-permute-start.2 = (bf16[144,2304]{1,0:T(8,128)(2,1)}, bf16[144,2304]{1,0:T(8,128)(2,1)S(1)}, u32[]{:S(2)}, u32[]{:S(2)}) collective-permute-start(bf16[144,2304]{1,0:T(8,128)(2,1)} %get-tuple-element.20), channel_id=1, source_target_pairs={{0,3},{1,0},{2,1},{3,2},{4,7},{5,4},{6,5},{7,6},{8,11},{9,8},{10,9... | collective-permute-start | bytes 1990664 | tf_op jit(solution)/shard_map/ppermute | solution.py:46
  27.6 4.0 %copy-start = (bf16[4,2048,576]{2,1,0:T(8,128)(2,1)S(1)}, bf16[4,2048,576]{2,1,0:T(8,128)(2,1)}, u32[]{:S(2)}) copy-start(bf16[4,2048,576]{2,1,0:T(8,128)(2,1)} %copy.13.cache) | copy-start | bytes 28311556
  31.6 38.1 %copy-start.2 = (bf16[1,7168,256]{2,1,0:T(8,128)(2,1)S(1)}, bf16[1,7168,256]{2,1,0:T(8,128)(2,1)}, u32[]{:S(2)}) copy-start(bf16[1,7168,256]{2,1,0:T(8,128)(2,1)} %refs_4_.5) | copy-start | bytes 11010052
  31.6 41.3 %copy-start.3 = (bf16[1,256,7168]{2,1,0:T(8,128)(2,1)S(1)}, bf16[1,256,7168]{2,1,0:T(8,128)(2,1)}, u32[]{:S(2)}) copy-start(bf16[1,256,7168]{2,1,0:T(8,128)(2,1)} %refs_6_.5) | copy-start | bytes 11010052
  52.5 17.2 %copy-start.1 = (bf16[1,7168,256]{2,1,0:T(8,128)(2,1)S(1)}, bf16[1,7168,256]{2,1,0:T(8,128)(2,1)}, u32[]{:S(2)}) copy-start(bf16[1,7168,256]{2,1,0:T(8,128)(2,1)} %refs_2_.3) | copy-start | bytes 11010052
  54.2 6.0 %collective-permute-start.3 = (bf16[4,64,128]{2,1,0:T(8,128)(2,1)S(1)}, bf16[4,64,128]{2,1,0:T(8,128)(2,1)S(1)}, u32[]{:S(2)}, u32[]{:S(2)}) collective-permute-start(bf16[4,64,128]{2,1,0:T(8,128)(2,1)S(1)} %shard_map.120.h0), channel_id=1, source_target_pairs={{0,1},{1,2},{2,3},{3,0},{4,5},{5,6},{6,7},{7,4},{8,9},{9,10},{10,1... | collective-permute-start | bytes 196616 | tf_op jit(solution)/shard_map/ppermute | solution.py:46
  57.5 5.8 %collective-permute-start.4 = (bf16[4,64,128]{2,1,0:T(8,128)(2,1)S(1)}, bf16[4,64,128]{2,1,0:T(8,128)(2,1)S(1)}, u32[]{:S(2)}, u32[]{:S(2)}) collective-permute-start(bf16[4,64,128]{2,1,0:T(8,128)(2,1)S(1)} %shard_map.120.h0), channel_id=1, source_target_pairs={{0,2},{1,3},{2,0},{3,1},{4,6},{5,7},{6,4},{7,5},{8,10},{9,11},{10,... | collective-permute-start | bytes 196616 | tf_op jit(solution)/shard_map/ppermute | solution.py:46
  58.5 4.7 %collective-permute-start.5 = (bf16[4,64,128]{2,1,0:T(8,128)(2,1)S(1)}, bf16[4,64,128]{2,1,0:T(8,128)(2,1)S(1)}, u32[]{:S(2)}, u32[]{:S(2)}) collective-permute-start(bf16[4,64,128]{2,1,0:T(8,128)(2,1)S(1)} %shard_map.120.h0), channel_id=1, source_target_pairs={{0,3},{1,0},{2,1},{3,2},{4,7},{5,4},{6,5},{7,6},{8,11},{9,8},{10,9... | collective-permute-start | bytes 196616 | tf_op jit(solution)/shard_map/ppermute | solution.py:46
  65.0 34.6 %copy-start.11 = (bf16[7168]{0:T(1024)(128)(2,1)S(1)}, bf16[7168]{0:T(1024)(128)(2,1)}, u32[]{:S(2)}) copy-start(bf16[7168]{0:T(1024)(128)(2,1)} %param.18) | copy-start | bytes 43012
  65.0 7.9 %collective-permute-start.6 = (bf16[64,1920]{1,0:T(8,128)(2,1)S(1)}, bf16[64,1920]{1,0:T(8,128)(2,1)S(1)}, u32[]{:S(2)}, u32[]{:S(2)}) collective-permute-start(bf16[64,1920]{1,0:T(8,128)(2,1)S(1)} %get-tuple-element.22), channel_id=1, source_target_pairs={{0,32},{16,48},{32,0},{48,16},{1,33},{17,49},{33,1},{49,17},{2,34}... | collective-permute-start | bytes 737288 | tf_op jit(solution)/shard_map/ppermute | solution.py:46
  66.5 9.0 %collective-permute-start.7 = (bf16[64,1920]{1,0:T(8,128)(2,1)S(1)}, bf16[64,1920]{1,0:T(8,128)(2,1)S(1)}, u32[]{:S(2)}, u32[]{:S(2)}) collective-permute-start(bf16[64,1920]{1,0:T(8,128)(2,1)S(1)} %get-tuple-element.23), channel_id=1, source_target_pairs={{0,16},{16,32},{32,48},{48,0},{1,17},{17,33},{33,49},{49,1},{2,18}... | collective-permute-start | bytes 737288 | tf_op jit(solution)/shard_map/ppermute | solution.py:46
  67.1 8.4 %collective-permute-start.8 = (bf16[64,1920]{1,0:T(8,128)(2,1)S(1)}, bf16[64,1920]{1,0:T(8,128)(2,1)S(1)}, u32[]{:S(2)}, u32[]{:S(2)}) collective-permute-start(bf16[64,1920]{1,0:T(8,128)(2,1)S(1)} %get-tuple-element.24), channel_id=1, source_target_pairs={{0,48},{16,0},{32,16},{48,32},{1,49},{17,1},{33,17},{49,33},{2,50}... | collective-permute-start | bytes 737288 | tf_op jit(solution)/shard_map/ppermute | solution.py:46
  69.7 50.9 %collective-permute-start.15 = (bf16[1,7168,256]{2,1,0:T(8,128)(2,1)S(1)}, bf16[1,7168,256]{2,1,0:T(8,128)(2,1)S(1)}, u32[]{:S(2)}, u32[]{:S(2)}) collective-permute-start(bf16[1,7168,256]{2,1,0:T(8,128)(2,1)S(1)} %copy-done.1), channel_id=1, source_target_pairs={{0,64},{64,0},{1,65},{65,1},{2,66},{66,2},{3,67},{67,3},{4,68},{68... | collective-permute-start | bytes 11010056 | tf_op jit(solution)/shard_map/ppermute | solution.py:55
  69.7 50.9 %collective-permute-start.16 = (bf16[1,7168,256]{2,1,0:T(8,128)(2,1)S(1)}, bf16[1,7168,256]{2,1,0:T(8,128)(2,1)S(1)}, u32[]{:S(2)}, u32[]{:S(2)}) collective-permute-start(bf16[1,7168,256]{2,1,0:T(8,128)(2,1)S(1)} %copy-done.2), channel_id=1, source_target_pairs={{0,64},{64,0},{1,65},{65,1},{2,66},{66,2},{3,67},{67,3},{4,68},{68... | collective-permute-start | bytes 11010056 | tf_op jit(solution)/shard_map/ppermute | solution.py:55
  72.9 47.6 %collective-permute-start.17 = (bf16[1,256,7168]{2,1,0:T(8,128)(2,1)S(1)}, bf16[1,256,7168]{2,1,0:T(8,128)(2,1)S(1)}, u32[]{:S(2)}, u32[]{:S(2)}) collective-permute-start(bf16[1,256,7168]{2,1,0:T(8,128)(2,1)S(1)} %copy-done.3), channel_id=1, source_target_pairs={{0,64},{64,0},{1,65},{65,1},{2,66},{66,2},{3,67},{67,3},{4,68},{68... | collective-permute-start | bytes 11010056 | tf_op jit(solution)/shard_map/ppermute | solution.py:55
  75.6 7.8 %collective-permute-start.10 = (bf16[64,1920]{1,0:T(8,128)(2,1)S(1)}, bf16[64,1920]{1,0:T(8,128)(2,1)S(1)}, u32[]{:S(2)}, u32[]{:S(2)}) collective-permute-start(bf16[64,1920]{1,0:T(8,128)(2,1)S(1)} %add_convert_fusion.2), channel_id=1, source_target_pairs={{0,8},{4,12},{8,0},{12,4},{1,9},{5,13},{9,1},{13,5},{2,10},{6,14},... | collective-permute-start | bytes 737288 | tf_op jit(solution)/shard_map/ppermute | solution.py:46
  77.2 7.2 %collective-permute-start.11 = (bf16[64,1920]{1,0:T(8,128)(2,1)S(1)}, bf16[64,1920]{1,0:T(8,128)(2,1)S(1)}, u32[]{:S(2)}, u32[]{:S(2)}) collective-permute-start(bf16[64,1920]{1,0:T(8,128)(2,1)S(1)} %add_convert_fusion.2), channel_id=1, source_target_pairs={{0,12},{4,0},{8,4},{12,8},{1,13},{5,1},{9,5},{13,9},{2,14},{6,2},{... | collective-permute-start | bytes 737288 | tf_op jit(solution)/shard_map/ppermute | solution.py:46
  83.4 7.4 %collective-permute-start.9 = (bf16[64,1920]{1,0:T(8,128)(2,1)S(1)}, bf16[64,1920]{1,0:T(8,128)(2,1)S(1)}, u32[]{:S(2)}, u32[]{:S(2)}) collective-permute-start(bf16[64,1920]{1,0:T(8,128)(2,1)S(1)} %add_convert_fusion.2), channel_id=1, source_target_pairs={{0,4},{4,8},{8,12},{12,0},{1,5},{5,9},{9,13},{13,1},{2,6},{6,10},{... | collective-permute-start | bytes 737288 | tf_op jit(solution)/shard_map/ppermute | solution.py:46
  90.9 7.5 %collective-permute-start.12 = (bf16[64,1920]{1,0:T(8,128)(2,1)S(1)}, bf16[64,1920]{1,0:T(8,128)(2,1)S(1)}, u32[]{:S(2)}, u32[]{:S(2)}) collective-permute-start(bf16[64,1920]{1,0:T(8,128)(2,1)S(1)} %add_convert_fusion.1.s0), channel_id=1, source_target_pairs={{0,1},{1,2},{2,3},{3,0},{4,5},{5,6},{6,7},{7,4},{8,9},{9,10},{10,1... | collective-permute-start | bytes 737288 | tf_op jit(solution)/shard_map/ppermute | solution.py:46
  91.6 10.1 %collective-permute-start.13 = (bf16[64,1920]{1,0:T(8,128)(2,1)S(1)}, bf16[64,1920]{1,0:T(8,128)(2,1)S(1)}, u32[]{:S(2)}, u32[]{:S(2)}) collective-permute-start(bf16[64,1920]{1,0:T(8,128)(2,1)S(1)} %add_convert_fusion.1.s0), channel_id=1, source_target_pairs={{0,2},{1,3},{2,0},{3,1},{4,6},{5,7},{6,4},{7,5},{8,10},{9,11},{10,... | collective-permute-start | bytes 737288 | tf_op jit(solution)/shard_map/ppermute | solution.py:46
  98.4 6.2 %collective-permute-start.14 = (bf16[64,1920]{1,0:T(8,128)(2,1)S(1)}, bf16[64,1920]{1,0:T(8,128)(2,1)S(1)}, u32[]{:S(2)}, u32[]{:S(2)}) collective-permute-start(bf16[64,1920]{1,0:T(8,128)(2,1)S(1)} %add_convert_fusion.1.s0), channel_id=1, source_target_pairs={{0,3},{1,0},{2,1},{3,2},{4,7},{5,4},{6,5},{7,6},{8,11},{9,8},{10,9... | collective-permute-start | bytes 737288 | tf_op jit(solution)/shard_map/ppermute | solution.py:46
  105.6 14.8 %collective-permute-start.18 = (bf16[64,7296]{1,0:T(8,128)(2,1)S(1)}, bf16[64,7296]{1,0:T(8,128)(2,1)S(1)}, u32[]{:S(2)}, u32[]{:S(2)}) collective-permute-start(bf16[64,7296]{1,0:T(8,128)(2,1)S(1)} %get-tuple-element.26.refs_0_.refs_1_), channel_id=1, source_target_pairs={{0,16},{16,32},{32,48},{48,0},{1,17},{17,33},{33,49},{49,1},{2,18}... | collective-permute-start | bytes 2801672 | tf_op jit(solution)/shard_map/ppermute | solution.py:46
  105.9 14.7 %collective-permute-start.19 = (bf16[64,7296]{1,0:T(8,128)(2,1)S(1)}, bf16[64,7296]{1,0:T(8,128)(2,1)S(1)}, u32[]{:S(2)}, u32[]{:S(2)}) collective-permute-start(bf16[64,7296]{1,0:T(8,128)(2,1)S(1)} %get-tuple-element.26.refs_0_.refs_1_), channel_id=1, source_target_pairs={{0,48},{16,0},{32,16},{48,32},{1,49},{17,1},{33,17},{49,33},{2,50}... | collective-permute-start | bytes 2801672 | tf_op jit(solution)/shard_map/ppermute | solution.py:46
  120.4 15.1 %collective-permute-start.22 = (bf16[64,7296]{1,0:T(8,128)(2,1)S(1)}, bf16[64,7296]{1,0:T(8,128)(2,1)S(1)}, u32[]{:S(2)}, u32[]{:S(2)}) collective-permute-start(bf16[64,7296]{1,0:T(8,128)(2,1)S(1)} %get-tuple-element.26.refs_0_.refs_1_), channel_id=1, source_target_pairs={{0,32},{16,48},{32,0},{48,16},{1,33},{17,49},{33,1},{49,17},{2,34}... | collective-permute-start | bytes 2801672 | tf_op jit(solution)/shard_map/ppermute | solution.py:46
  127.9 22.3 %collective-permute-start.20 = (bf16[64,7168]{1,0:T(8,128)(2,1)S(1)}, bf16[64,7168]{1,0:T(8,128)(2,1)S(1)}, u32[]{:S(2)}, u32[]{:S(2)}) collective-permute-start(bf16[64,7168]{1,0:T(8,128)(2,1)S(1)} %get-tuple-element.27), channel_id=1, source_target_pairs={{0,48},{16,0},{32,16},{48,32},{1,49},{17,1},{33,17},{49,33},{2,50}... | collective-permute-start | bytes 2752520 | tf_op jit(solution)/shard_map/ppermute | solution.py:46
  131.1 19.1 %collective-permute-start.21 = (bf16[64,7168]{1,0:T(8,128)(2,1)S(1)}, bf16[64,7168]{1,0:T(8,128)(2,1)S(1)}, u32[]{:S(2)}, u32[]{:S(2)}) collective-permute-start(bf16[64,7168]{1,0:T(8,128)(2,1)S(1)} %get-tuple-element.28), channel_id=1, source_target_pairs={{0,16},{16,32},{32,48},{48,0},{1,17},{17,33},{33,49},{49,1},{2,18}... | collective-permute-start | bytes 2752520 | tf_op jit(solution)/shard_map/ppermute | solution.py:46
  142.7 15.0 %collective-permute-start.23 = (bf16[64,7168]{1,0:T(8,128)(2,1)S(1)}, bf16[64,7168]{1,0:T(8,128)(2,1)S(1)}, u32[]{:S(2)}, u32[]{:S(2)}) collective-permute-start(bf16[64,7168]{1,0:T(8,128)(2,1)S(1)} %shard_map.125), channel_id=1, source_target_pairs={{0,32},{16,48},{32,0},{48,16},{1,33},{17,49},{33,1},{49,17},{2,34}... | collective-permute-start | bytes 2752520 | tf_op jit(solution)/shard_map/ppermute | solution.py:46
  159.4 16.3 %all-to-all-start.1 = ((bf16[16,4,7168]{2,1,0:T(4,128)(2,1)}), bf16[16,4,7168]{2,1,0:T(4,128)(2,1)S(1)}, u32[]{:S(2)}, u32[]{:S(2)}) async-start(bf16[16,4,7168]{2,1,0:T(4,128)(2,1)} %reshape.18), calls=%async_computation.1 | async-start | bytes 1835008 | tf_op jit(solution)/shard_map/all_to_all | solution.py:432

commit v3 on v2

--- a/solution.py
+++ b/solution.py
@@ -13,7 +13,7 @@
 SIDE = 4
 EXTRA = 128
 GROUP = 16
-CHUNK = 512
+CHUNK = 1024
 
 score_scale = 192.0 ** (-0.5)
 epsilon = 1e-06
@@ -58,7 +58,7 @@
 def call(body, out_shape, args, flops, limit, **given):
     smem = pl.BlockSpec(memory_space=pltpu.SMEM)
     vmem = pl.BlockSpec(memory_space=pltpu.VMEM)
-    if "grid" not in given and "grid_spec" not in given:
+    if "in_specs" not in given:
         given["in_specs"] = [smem] + [vmem] * (len(args) - 1)
         given["out_specs"] = jax.tree.map(lambda _: vmem, out_shape)
     moved = sum(x.size * x.dtype.itemsize for x in [*args, *jax.tree.leaves(out_shape)])
@@ -66,7 +66,9 @@
         body,
         out_shape=out_shape,
         compiler_params=pltpu.CompilerParams(vmem_limit_bytes=limit * 2**20),
-        cost_estimate=pl.CostEstimate(flops=flops, bytes_accessed=moved, transcendentals=0),
+        cost_estimate=pl.CostEstimate(
+            flops=flops, bytes_accessed=moved if flops else 0, transcendentals=0
+        ),
         **given,
     )(*args)
 
@@ -113,83 +115,89 @@
             out[depth:, block + EXTRA :] = jnp.zeros((GROUP, latent - EXTRA), bf16)
 
 
-def attend_kernel(lengths, at, query, cache, out, most, norm, mixed, placed):
-    row, chunk = pl.program_id(0), pl.program_id(1)
-    length = lengths[row]
-    heads, latent = mixed.shape
-    size = cache.shape[1]
-
-    @pl.when((row == 0) & (chunk == 0))
-    def _():
-        placed[...] = jnp.zeros_like(placed)
-
-    @pl.when(chunk == 0)
-    def _():
-        most[...] = jnp.full_like(most, -jnp.inf)
-        norm[...] = jnp.zeros_like(norm)
-        mixed[...] = jnp.zeros_like(mixed)
-
-    @pl.when(chunk * size < length)
-    def _():
-        keys = cache[0]
-        scores = score_scale * lax.dot_general(
-            query[0], keys, (((1,), (1,)), ((), ())), preferred_element_type=f32
+def attend_kernel(lengths, at, query, cache, out, held, scores, most, norm, mixed, sems):
+    rows, heads, _ = query.shape
+    latent = mixed.shape[2]
+    size = most.shape[2]
+    parts = cache.shape[2] // size
+
+    def copy(row, part):
+        span = pl.ds(part * size, size)
+        return pltpu.make_async_copy(
+            cache.at[row, :, span], held.at[row, :, span], sems.at[row, part]
         )
-        scores = jnp.where(chunk * size + iota(scores.shape, 1) < length, scores, -jnp.inf)
-        highest = jnp.maximum(most[...], jnp.max(scores, axis=1, keepdims=True))
-        fade = jnp.exp(most[...] - highest)
-        shares = jnp.exp(scores - highest)
-        most[...] = highest
-        norm[...] = norm[...] * fade + jnp.sum(shares, axis=1, keepdims=True)
-        mixed[...] = mixed[...] * fade + jnp.dot(
-            shares.astype(bf16), keys[:, :latent], preferred_element_type=f32
+
+    def where_live(step):
+        for row in range(rows):
+            for part in range(parts):
+                act = functools.partial(step, row, part)
+                if part:
+                    pl.when(part * size < lengths[row])(act)
+                else:
+                    act()
+
+    def score(row, part):
+        span = slice(part * size, (part + 1) * size)
+        copy(row, part).wait()
+        value = score_scale * jnp.dot(query[row], held[row, :, span], preferred_element_type=f32)
+        live = part * size + iota(value.shape, 1) < lengths[row]
+        value = jnp.where(live, value, -jnp.inf)
+        scores[row, :, span] = value
+        most[row] = jnp.maximum(most[row], value) if part else value
+
+    where_live(lambda row, part: copy(row, part).start())
+    where_live(score)
+    tops = [jnp.max(most[row], axis=1, keepdims=True) for row in range(rows)]
+
+    def mix(row, part):
+        span = slice(part * size, (part + 1) * size)
+        shares = jnp.exp(scores[row, :, span] - tops[row])
+        norm[row] = norm[row] + shares if part else shares
+        value = lax.dot_general(
+            shares.astype(bf16),
+            held[row, :latent, span],
+            (((1,), (1,)), ((), ())),
+            preferred_element_type=f32,
         )
-
-    @pl.when(chunk == pl.num_programs(1) - 1)
-    def _():
-        done = (mixed[...] / norm[...]).astype(bf16)
-        line, head = iota((placed.shape[0], heads), 0), iota((placed.shape[0], heads), 1)
-        a, b, c = line >> 6, (line >> 4) & 3, line & 3
-        wanted = jnp.where(at[0] == 0, a * 16 + b * 4 + c, c * 16 + a * 4 + b)
+        mixed[row] = mixed[row] + value if part else value
+
+    where_live(mix)
+    lines = out.shape[0]
+    line, head = iota((lines, heads), 0), iota((lines, heads), 1)
+    a, b, c = line >> 6, (line >> 4) & 3, line & 3
+    wanted = jnp.where(at[0] == 0, a * 16 + b * 4 + c, c * 16 + a * 4 + b)
+    placed = jnp.zeros((lines, latent), f32)
+    for row in range(rows):
+        done = (mixed[row] / jnp.sum(norm[row], axis=1, keepdims=True)).astype(bf16)
         pick = ((wanted == head) & (((line >> 2) & 3) == row)).astype(f32).astype(bf16)
-        placed[...] += jnp.dot(pick, done, preferred_element_type=f32)
-
-        @pl.when(row == pl.num_programs(0) - 1)
-        def _():
-            out[...] = placed[...].astype(bf16)
+        placed = placed + jnp.dot(pick, done, preferred_element_type=f32)
+    out[...] = placed.astype(bf16)
 
 
 def attend(lengths, at, queries, cache):
     rows, heads, width = queries.shape
-    cache_length = cache.shape[1]
+    cache_length = cache.shape[2]
     size = min(CHUNK, cache_length)
     latent = width - 64
     lines = rows * heads
-    grid_spec = pltpu.PrefetchScalarGridSpec(
-        num_scalar_prefetch=2,
-        grid=(rows, cache_length // size),
-        in_specs=[
-            pl.BlockSpec((1, heads, width), lambda r, k, lengths, at: (r, 0, 0)),
-            pl.BlockSpec(
-                (1, size, width),
-                lambda r, k, lengths, at: (r, jnp.minimum(k, (lengths[r] - 1) // size), 0),
-            ),
-        ],
-        out_specs=pl.BlockSpec((lines, latent), lambda r, k, lengths, at: (0, 0)),
-        scratch_shapes=[
-            pltpu.VMEM((heads, 1), f32),
-            pltpu.VMEM((heads, 1), f32),
-            pltpu.VMEM((heads, latent), f32),
-            pltpu.VMEM((lines, latent), f32),
-        ],
-    )
+    smem = pl.BlockSpec(memory_space=pltpu.SMEM)
+    vmem = pl.BlockSpec(memory_space=pltpu.VMEM)
     return call(
         attend_kernel,
         jax.ShapeDtypeStruct((lines, latent), bf16),
         (lengths, at, queries, cache),
         2 * lines * cache_length * (width + latent),
-        16,
-        grid_spec=grid_spec,
+        56,
+        in_specs=[smem, smem, vmem, pl.BlockSpec(memory_space=pltpu.HBM)],
+        out_specs=vmem,
+        scratch_shapes=[
+            pltpu.VMEM(cache.shape, bf16),
+            pltpu.VMEM((rows, heads, cache_length), f32),
+            pltpu.VMEM((rows, heads, size), f32),
+            pltpu.VMEM((rows, heads, size), f32),
+            pltpu.VMEM((rows, heads, latent), f32),
+            pltpu.SemaphoreType.DMA((rows, cache_length // size)),
+        ],
     )
 
 
@@ -374,13 +382,21 @@
         [shape] * SIDE,
         (at, w_out, w_uv, residual, expert_ids, gate_values),
         0,
-        16,
+        60,
+        grid=(1,),
+        in_specs=[pl.BlockSpec(memory_space=pltpu.SMEM)]
+        + [
+            pl.BlockSpec(v.shape, lambda i, n=v.ndim: (0,) * n)
+            for v in (w_out, w_uv, residual, expert_ids, gate_values)
+        ],
+        out_specs=[pl.BlockSpec(shape.shape, lambda i: (0, 0))] * SIDE,
     )
     packs = [packs[0]] + [shift(packs[s], "c", s) for s in (1, 2, 3)]
     gates, ups, downs = [(w, swap_cores(w)) for w in (w_gate, w_up, w_down)]
 
-    sent = attend(lengths, at, queries, latent_cache).reshape(16, SIDE * rows, latent)
+    sent = attend(lengths, at, queries, latent_cache.swapaxes(1, 2)).reshape(16, SIDE * rows, latent)
     got = lax.all_to_all(sent, AXES, 0, 0, axis_index_groups=groups("ab"), tiled=True)
+    got, gates, ups, downs = lax.optimization_barrier((got, gates, ups, downs))
     got = got.reshape(-1, latent)
     vmem = pl.BlockSpec(memory_space=pltpu.VMEM)
     head_out = call(

time: 178 us -> 155 us (0.87)
  local copies, waits for them, and re-layouts: 24.1 us -> 1.97 us
  Pallas kernels: 34.8 us -> 45.4 us
  waiting for transfers between devices: 64 us -> 56.8 us
  starting transfers between devices: 37.5 us -> 31.4 us
  blocking collectives: 14.4 us -> 16.3 us
    unnamed x25 -> x12, local copies, waits for them, and re-layouts: 22.8 us -> 0.03 us
    pallas_call x8, Pallas kernels: 34.8 us -> 45.4 us  [call(): pl.pallas_call(body, out_shape=out_shape, compiler_params=pltpu.CompilerP...]
    ppermute x21, waiting for transfers between devices: 51.6 us -> 44.3 us  [shift(): return lax.ppermute(value, AXES, pairs)]
    ppermute x21, starting transfers between devices: 33.1 us -> 27.1 us  [shift(): return lax.ppermute(value, AXES, pairs)]
    all_to_all x1, blocking collectives: 14.4 us -> 16.3 us  [on_device(): lax.all_to_all(sent, AXES, 0, 0, axis_index_groups=groups('ab'), tiled=True)]
  transfers between devices with their start and end apart: 25 -> 25, of which waited for: 13 -> 15; matrix products, arithmetic and copies ran while one was open for 8% -> 0% of each run, Pallas kernels for 16% -> 27%
where the time goes in v3:
time: 155 us; the launch traced here: 154 us
  waiting for transfers between devices  56.8 us (37%)
  Pallas kernels  45.4 us (29%)
  starting transfers between devices  31.4 us (20%)
  blocking collectives  16.3 us (11%)
  local copies, waits for them, and re-layouts  1.97 us (1%)
  other arithmetic  1.76 us (1%)
    pallas_call x8, Pallas kernels, call(): pl.pallas_call(body, out_shape=out_shape, compiler_params=pltpu.CompilerP...  45.4 us
    ppermute x21, waiting for transfers between devices, shift(): return lax.ppermute(value, AXES, pairs)  44.3 us
    ppermute x21, starting transfers between devices, shift(): return lax.ppermute(value, AXES, pairs)  27.1 us
    all_to_all x1, blocking collectives, on_device(): lax.all_to_all(sent, AXES, 0, 0, axis_index_groups=groups('ab'), tiled=True)  16.3 us
    all_to_all x1, waiting for transfers between devices, on_device(): lax.all_to_all(last, AXES, 0, 0, axis_index_groups=groups('cb'), tiled=True)  12.5 us
    all_to_all x1, starting transfers between devices, on_device(): lax.all_to_all(last, AXES, 0, 0, axis_index_groups=groups('cb'), tiled=True)  3.73 us
  transfers between devices with their start and end apart: 25, of which 15 were waited for; matrix products, arithmetic and copies ran while one was open for 0% of the time, Pallas kernels for 27%

profile of v3, /device:TPU:0, one launch (start us, length us, event | category | flops | bytes accessed | tf_op | source)
XLA Modules:
  0.0 153.7 jit_solution(7355747022344007238)
XLA Ops:
  0.0 0.0 collective-permute-start
  0.0 0.5 collective-permute-start.1
  0.5 0.0 collective-permute-start.2
  0.5 0.7 stack.29.at
  1.2 3.4 %shard_map.119 = (bf16[144,2304]{1,0:T(8,128)(2,1)}, bf16[144,2304]{1,0:T(8,128)(2,1)}, bf16[144,2304]{1,0:T(8,128)(2,1)}, bf16[144,2304]{1,0:T(8,128)(2,1)}) custom-call(s32[8]{0:T(128)} %stack.29.at, bf16[128,7168]{1,0:T(8,128)(2,1)} %w_out.1, bf16[1,512,128]{2,1,0:T(8,128)(2,1)} %w_uv.1, bf16[4,7168]{1,0:T(4,128)(2,1)} %residual.1, s32[4,8]{1,0:T(4,128)} %ids.1, ...), custom_call_target="tpu_custom_call" | custom-call | tf_op jit(solution)/shard_map/pallas_call | solution.py:65
  4.6 2.0 %collective-permute-start.3 = (bf16[144,2304]{1,0:T(8,128)(2,1)}, bf16[144,2304]{1,0:T(8,128)(2,1)S(1)}, u32[]{:S(2)}, u32[]{:S(2)}) collective-permute-start(bf16[144,2304]{1,0:T(8,128)(2,1)} %get-tuple-element.26), channel_id=1, source_target_pairs={{0,1},{1,2},{2,3},{3,0},{4,5},{5,6},{6,7},{7,4},{8,9},{9,10},{10,1... | collective-permute-start | bytes 1990664 | tf_op jit(solution)/shard_map/ppermute | solution.py:46
  6.6 3.6 %collective-permute-start.4 = (bf16[144,2304]{1,0:T(8,128)(2,1)}, bf16[144,2304]{1,0:T(8,128)(2,1)S(1)}, u32[]{:S(2)}, u32[]{:S(2)}) collective-permute-start(bf16[144,2304]{1,0:T(8,128)(2,1)} %get-tuple-element.27), channel_id=1, source_target_pairs={{0,2},{1,3},{2,0},{3,1},{4,6},{5,7},{6,4},{7,5},{8,10},{9,11},{10,... | collective-permute-start | bytes 1990664 | tf_op jit(solution)/shard_map/ppermute | solution.py:46
  10.2 0.0 collective-permute-done.refs_3_.refs_5_
  10.2 1.0 collective-permute-start.5
  11.2 7.2 %shard_map.118 = bf16[256,512]{1,0:T(8,128)(2,1)} custom-call(s32[4]{0:T(128)} %lengths.1, s32[8]{0:T(128)} %stack.29.at, bf16[4,64,576]{2,1,0:T(8,128)(2,1)} %query.1, bf16[4,576,2048]{2,1,0:T(8,128)(2,1)} %bitcast.12), custom_call_target="tpu_custom_call" | custom-call | flops 1140850688 | bytes 9994288 | tf_op jit(solution)/shard_map/pallas_call | solution.py:65
  18.4 16.3 %all_to_all.10 = bf16[16,16,512]{2,1,0:T(8,128)(2,1)S(1)} all-to-all(bf16[16,16,512]{2,1,0:T(8,128)(2,1)} %bitcast.13), channel_id=1, replica_groups={{0,4,8,12,16,20,24,28,32,36,40,44,48,52,56,60},{1,5,9,13,17,21,25,29,33..., dimensions={0} | all-to-all | bytes 524288 | tf_op jit(solution)/shard_map/all_to_all | solution.py:398
  34.7 0.0 collective-permute-done.1.refs_5_.refs_7_
  34.7 0.0 collective-permute-done.4.w2.p2
  34.8 0.0 copy-start.1
  34.8 1.8 %shard_map.120.h0 = bf16[4,64,128]{2,1,0:T(8,128)(2,1)S(1)} custom-call(s32[8]{0:T(128)S(1)} %copy-done.4, bf16[256,512]{1,0:T(8,128)(2,1)S(1)} %bitcast.10, bf16[144,2304]{1,0:T(8,128)(2,1)S(1)} %copy-done.3, bf16[144,2304]{1,0:T(8,128)(2,1)S(1)} %collective-permute-done.3.w1.p1, bf16[144,2304]{1,0:T(8,128)(2,1)S(1)} %collective-permute-done.4.w2.p2, ...), custom_call_target="tpu_custom_call" | custom-call | flops 134217728 | bytes 2981920 | tf_op jit(solution)/shard_map/pallas_call | solution.py:65
  36.6 0.9 collective-permute-start.8
  37.4 3.0 %collective-permute-start.7 = (bf16[4,64,128]{2,1,0:T(8,128)(2,1)S(1)}, bf16[4,64,128]{2,1,0:T(8,128)(2,1)S(1)}, u32[]{:S(2)}, u32[]{:S(2)}) collective-permute-start(bf16[4,64,128]{2,1,0:T(8,128)(2,1)S(1)} %shard_map.120.h0), channel_id=1, source_target_pairs={{0,2},{1,3},{2,0},{3,1},{4,6},{5,7},{6,4},{7,5},{8,10},{9,11},{10,... | collective-permute-start | bytes 196616 | tf_op jit(solution)/shard_map/ppermute | solution.py:46
  40.5 0.4 collective-permute-done.8.h3
  40.9 2.3 %collective-permute-done.7.h2 = bf16[4,64,128]{2,1,0:T(8,128)(2,1)S(1)} collective-permute-done((bf16[4,64,128]{2,1,0:T(8,128)(2,1)S(1)}, bf16[4,64,128]{2,1,0:T(8,128)(2,1)S(1)}, u32[]{:S(2)}, u32[]{:S(2)}) %collective-permute-start.7) | collective-permute-done | bytes 65568 | tf_op jit(solution)/shard_map/ppermute | solution.py:46
  43.2 2.8 %collective-permute-done.6.h1 = bf16[4,64,128]{2,1,0:T(8,128)(2,1)S(1)} collective-permute-done((bf16[4,64,128]{2,1,0:T(8,128)(2,1)S(1)}, bf16[4,64,128]{2,1,0:T(8,128)(2,1)S(1)}, u32[]{:S(2)}, u32[]{:S(2)}) %collective-permute-start.6) | collective-permute-done | bytes 65568 | tf_op jit(solution)/shard_map/ppermute | solution.py:46
  46.0 1.7 %shard_map.121 = (bf16[64,1920]{1,0:T(8,128)(2,1)S(1)}, bf16[64,1920]{1,0:T(8,128)(2,1)S(1)}, bf16[64,1920]{1,0:T(8,128)(2,1)S(1)}, bf16[64,1920]{1,0:T(8,128)(2,1)S(1)}) custom-call(s32[8]{0:T(128)S(1)} %copy-done.4, bf16[4,64,128]{2,1,0:T(8,128)(2,1)S(1)} %shard_map.120.h0, bf16[4,64,128]{2,1,0:T(8,128)(2,1)S(1)} %collective-permute-done.6.h1, ...), custom_call_target="tpu_custom_call" | custom-call | flops 469762048 | bytes 3899424 | tf_op jit(solution)/shard_map/pallas_call | solution.py:65
  47.7 0.0 copy-start.5
  47.7 1.4 collective-permute-start.9
  49.1 0.6 collective-permute-start.10
  49.7 2.6 %collective-permute-start.11 = (bf16[64,1920]{1,0:T(8,128)(2,1)S(1)}, bf16[64,1920]{1,0:T(8,128)(2,1)S(1)}, u32[]{:S(2)}, u32[]{:S(2)}) collective-permute-start(bf16[64,1920]{1,0:T(8,128)(2,1)S(1)} %get-tuple-element.32), channel_id=1, source_target_pairs={{0,48},{16,0},{32,16},{48,32},{1,49},{17,1},{33,17},{49,33},{2,50}... | collective-permute-start | bytes 737288 | tf_op jit(solution)/shard_map/ppermute | solution.py:46
  52.4 3.2 %collective-permute-done.9 = bf16[64,1920]{1,0:T(8,128)(2,1)S(1)} collective-permute-done((bf16[64,1920]{1,0:T(8,128)(2,1)S(1)}, bf16[64,1920]{1,0:T(8,128)(2,1)S(1)}, u32[]{:S(2)}, u32[]{:S(2)}) %collective-permute-start.9) | collective-permute-done | bytes 245792 | tf_op jit(solution)/shard_map/ppermute | solution.py:46
  55.6 2.5 %collective-permute-done.10 = bf16[64,1920]{1,0:T(8,128)(2,1)S(1)} collective-permute-done((bf16[64,1920]{1,0:T(8,128)(2,1)S(1)}, bf16[64,1920]{1,0:T(8,128)(2,1)S(1)}, u32[]{:S(2)}, u32[]{:S(2)}) %collective-permute-start.10) | collective-permute-done | bytes 245792 | tf_op jit(solution)/shard_map/ppermute | solution.py:46
  58.1 0.0 collective-permute-done.11
  58.1 0.1 add_convert_fusion.2
  58.3 1.1 collective-permute-start.14
  59.4 1.5 collective-permute-start.13
  60.9 0.4 collective-permute-start.12
  61.3 3.3 %collective-permute-done.14 = bf16[64,1920]{1,0:T(8,128)(2,1)S(1)} collective-permute-done((bf16[64,1920]{1,0:T(8,128)(2,1)S(1)}, bf16[64,1920]{1,0:T(8,128)(2,1)S(1)}, u32[]{:S(2)}, u32[]{:S(2)}) %collective-permute-start.14) | collective-permute-done | bytes 245792 | tf_op jit(solution)/shard_map/ppermute | solution.py:46
  64.6 2.6 %collective-permute-done.13 = bf16[64,1920]{1,0:T(8,128)(2,1)S(1)} collective-permute-done((bf16[64,1920]{1,0:T(8,128)(2,1)S(1)}, bf16[64,1920]{1,0:T(8,128)(2,1)S(1)}, u32[]{:S(2)}, u32[]{:S(2)}) %collective-permute-start.13) | collective-permute-done | bytes 245792 | tf_op jit(solution)/shard_map/ppermute | solution.py:46
  67.2 2.5 %collective-permute-done.12 = bf16[64,1920]{1,0:T(8,128)(2,1)S(1)} collective-permute-done((bf16[64,1920]{1,0:T(8,128)(2,1)S(1)}, bf16[64,1920]{1,0:T(8,128)(2,1)S(1)}, u32[]{:S(2)}, u32[]{:S(2)}) %collective-permute-start.12) | collective-permute-done | bytes 245792 | tf_op jit(solution)/shard_map/ppermute | solution.py:46
  69.7 0.1 add_convert_fusion.1.s0
  69.9 0.3 collective-permute-start.17
  70.1 1.5 %collective-permute-start.16 = (bf16[64,1920]{1,0:T(8,128)(2,1)S(1)}, bf16[64,1920]{1,0:T(8,128)(2,1)S(1)}, u32[]{:S(2)}, u32[]{:S(2)}) collective-permute-start(bf16[64,1920]{1,0:T(8,128)(2,1)S(1)} %add_convert_fusion.1.s0), channel_id=1, source_target_pairs={{0,2},{1,3},{2,0},{3,1},{4,6},{5,7},{6,4},{7,5},{8,10},{9,11},{10,... | collective-permute-start | bytes 737288 | tf_op jit(solution)/shard_map/ppermute | solution.py:46
  71.7 0.5 collective-permute-start.15
  72.1 4.2 %collective-permute-done.17.s3 = bf16[64,1920]{1,0:T(8,128)(2,1)S(1)} collective-permute-done((bf16[64,1920]{1,0:T(8,128)(2,1)S(1)}, bf16[64,1920]{1,0:T(8,128)(2,1)S(1)}, u32[]{:S(2)}, u32[]{:S(2)}) %collective-permute-start.17) | collective-permute-done | bytes 245792 | tf_op jit(solution)/shard_map/ppermute | solution.py:46
  76.3 1.7 %collective-permute-done.16.s2 = bf16[64,1920]{1,0:T(8,128)(2,1)S(1)} collective-permute-done((bf16[64,1920]{1,0:T(8,128)(2,1)S(1)}, bf16[64,1920]{1,0:T(8,128)(2,1)S(1)}, u32[]{:S(2)}, u32[]{:S(2)}) %collective-permute-start.16) | collective-permute-done | bytes 245792 | tf_op jit(solution)/shard_map/ppermute | solution.py:46
  78.0 2.5 %collective-permute-done.15.s1 = bf16[64,1920]{1,0:T(8,128)(2,1)S(1)} collective-permute-done((bf16[64,1920]{1,0:T(8,128)(2,1)S(1)}, bf16[64,1920]{1,0:T(8,128)(2,1)S(1)}, u32[]{:S(2)}, u32[]{:S(2)}) %collective-permute-start.15) | collective-permute-done | bytes 245792 | tf_op jit(solution)/shard_map/ppermute | solution.py:46
  80.5 1.0 shard_map.122
  81.5 1.3 collective-permute-start.22
  82.8 1.7 %collective-permute-start.19 = (bf16[64,7296]{1,0:T(8,128)(2,1)S(1)}, bf16[64,7296]{1,0:T(8,128)(2,1)S(1)}, u32[]{:S(2)}, u32[]{:S(2)}) collective-permute-start(bf16[64,7296]{1,0:T(8,128)(2,1)S(1)} %get-tuple-element.34.refs_0_.refs_1_), channel_id=1, source_target_pairs={{0,48},{16,0},{32,16},{48,32},{1,49},{17,1},{33,17},{49,33},{2,50}... | collective-permute-start | bytes 2801672 | tf_op jit(solution)/shard_map/ppermute | solution.py:46
  84.5 0.3 collective-permute-start.18
  84.9 11.9 %collective-permute-done.22.refs_0_.refs_1_ = bf16[64,7296]{1,0:T(8,128)(2,1)S(1)} collective-permute-done((bf16[64,7296]{1,0:T(8,128)(2,1)S(1)}, bf16[64,7296]{1,0:T(8,128)(2,1)S(1)}, u32[]{:S(2)}, u32[]{:S(2)}) %collective-permute-start.22) | collective-permute-done | bytes 933920 | tf_op jit(solution)/shard_map/ppermute | solution.py:46
  96.8 10.1 %shard_map.125 = bf16[64,7168]{1,0:T(8,128)(2,1)S(1)} custom-call(s32[8]{0:T(128)S(1)} %copy-done.4, bf16[64,7296]{1,0:T(8,128)(2,1)S(1)} %collective-permute-done.22.refs_0_.refs_1_, bf16[64,7296]{1,0:T(8,128)(2,1)S(1)} %collective-permute-done.22.refs_0_.refs_1_, bf16[1,7168,256]{2,1,0:T(8,128)(2,1)S(1)} %copy-done, ...), custom_call_target="tpu_custom_call" | custom-call | flops 1409286144 | bytes 24805408 | tf_op jit(solution)/shard_map/pallas_call | solution.py:65
  106.9 1.3 collective-permute-start.23
  108.2 0.0 collective-permute-done.19.refs_1_.refs_3_
  108.2 0.0 collective-permute-done.18.refs_0_.refs_2_
  108.2 10.2 %shard_map.124 = (bf16[64,7168]{1,0:T(8,128)(2,1)S(1)}, bf16[64,7168]{1,0:T(8,128)(2,1)S(1)}) custom-call(s32[8]{0:T(128)S(1)} %copy-done.4, bf16[64,7296]{1,0:T(8,128)(2,1)S(1)} %collective-permute-done.18.refs_0_.refs_2_, bf16[64,7296]{1,0:T(8,128)(2,1)S(1)} %collective-permute-done.19.refs_1_.refs_3_, ...), custom_call_target="tpu_custom_call" | custom-call | flops 2818572288 | bytes 27590688 | tf_op jit(solution)/shard_map/pallas_call | solution.py:65
  118.4 1.8 %collective-permute-start.20 = (bf16[64,7168]{1,0:T(8,128)(2,1)S(1)}, bf16[64,7168]{1,0:T(8,128)(2,1)S(1)}, u32[]{:S(2)}, u32[]{:S(2)}) collective-permute-start(bf16[64,7168]{1,0:T(8,128)(2,1)S(1)} %get-tuple-element.41), channel_id=1, source_target_pairs={{0,48},{16,0},{32,16},{48,32},{1,49},{17,1},{33,17},{49,33},{2,50}... | collective-permute-start | bytes 2752520 | tf_op jit(solution)/shard_map/ppermute | solution.py:46
  120.2 0.3 collective-permute-start.21
  120.5 10.0 %shard_map.123 = bf16[64,7168]{1,0:T(8,128)(2,1)S(1)} custom-call(s32[8]{0:T(128)S(1)} %copy-done.4, bf16[64,7296]{1,0:T(8,128)(2,1)S(1)} %get-tuple-element.34.refs_0_.refs_1_, bf16[64,7296]{1,0:T(8,128)(2,1)S(1)} %get-tuple-element.34.refs_0_.refs_1_, bf16[1,7168,256]{2,1,0:T(8,128)(2,1)S(1)} %copy-done, ...), custom_call_target="tpu_custom_call" | custom-call | flops 1409286144 | bytes 24805408 | tf_op jit(solution)/shard_map/pallas_call | solution.py:65
  130.5 0.0 collective-permute-done.23
  130.5 1.3 collective-permute-done.20
  131.8 2.9 %collective-permute-done.21 = bf16[64,7168]{1,0:T(8,128)(2,1)S(1)} collective-permute-done((bf16[64,7168]{1,0:T(8,128)(2,1)S(1)}, bf16[64,7168]{1,0:T(8,128)(2,1)S(1)}, u32[]{:S(2)}, u32[]{:S(2)}) %collective-permute-start.21) | collective-permute-done | bytes 917536 | tf_op jit(solution)/shard_map/ppermute | solution.py:46
  134.8 0.5 add_convert_fusion
  135.2 1.3 reshape.18
  136.5 3.7 %all-to-all-start.1 = ((bf16[16,4,7168]{2,1,0:T(4,128)(2,1)}), bf16[16,4,7168]{2,1,0:T(4,128)(2,1)S(1)}, u32[]{:S(2)}, u32[]{:S(2)}) async-start(bf16[16,4,7168]{2,1,0:T(4,128)(2,1)} %reshape.18), calls=%async_computation.1 | async-start | bytes 1835008 | tf_op jit(solution)/shard_map/all_to_all | solution.py:448
  140.2 12.5 %all-to-all-done.1 = bf16[16,4,7168]{2,1,0:T(4,128)(2,1)S(1)} async-done(((bf16[16,4,7168]{2,1,0:T(4,128)(2,1)}), bf16[16,4,7168]{2,1,0:T(4,128)(2,1)S(1)}, u32[]{:S(2)}, u32[]{:S(2)}) %all-to-all-start.1) | async-done | bytes 917536 | tf_op jit(solution)/shard_map/all_to_all | solution.py:448
  152.7 0.4 convert_reduce_fusion
  153.1 0.7 add_convert_fusion.3
  (15 shorter events, 0.0 us)
Async XLA Ops:
  0.0 10.2 %collective-permute-start = (bf16[1,7168,256]{2,1,0:T(8,128)(2,1)}, bf16[1,7168,256]{2,1,0:T(8,128)(2,1)}, u32[]{:S(2)}, u32[]{:S(2)}) collective-permute-start(bf16[1,7168,256]{2,1,0:T(8,128)(2,1)} %refs_2_.1), channel_id=1, source_target_pairs={{0,64},{64,0},{1,65},{65,1},{2,66},{66,2},{3,67},{67,3},{4,68},{68... | collective-permute-start | bytes 11010056 | tf_op jit(solution)/shard_map/ppermute | solution.py:55
  0.0 34.7 %collective-permute-start.1 = (bf16[1,7168,256]{2,1,0:T(8,128)(2,1)}, bf16[1,7168,256]{2,1,0:T(8,128)(2,1)}, u32[]{:S(2)}, u32[]{:S(2)}) collective-permute-start(bf16[1,7168,256]{2,1,0:T(8,128)(2,1)} %refs_4_.2), channel_id=1, source_target_pairs={{0,64},{64,0},{1,65},{65,1},{2,66},{66,2},{3,67},{67,3},{4,68},{68... | collective-permute-start | bytes 11010056 | tf_op jit(solution)/shard_map/ppermute | solution.py:55
  0.5 34.2 %collective-permute-start.2 = (bf16[1,256,7168]{2,1,0:T(8,128)(2,1)}, bf16[1,256,7168]{2,1,0:T(8,128)(2,1)}, u32[]{:S(2)}, u32[]{:S(2)}) collective-permute-start(bf16[1,256,7168]{2,1,0:T(8,128)(2,1)} %refs_6_.2), channel_id=1, source_target_pairs={{0,64},{64,0},{1,65},{65,1},{2,66},{66,2},{3,67},{67,3},{4,68},{68... | collective-permute-start | bytes 11010056 | tf_op jit(solution)/shard_map/ppermute | solution.py:55
  4.6 30.1 %collective-permute-start.3 = (bf16[144,2304]{1,0:T(8,128)(2,1)}, bf16[144,2304]{1,0:T(8,128)(2,1)S(1)}, u32[]{:S(2)}, u32[]{:S(2)}) collective-permute-start(bf16[144,2304]{1,0:T(8,128)(2,1)} %get-tuple-element.26), channel_id=1, source_target_pairs={{0,1},{1,2},{2,3},{3,0},{4,5},{5,6},{6,7},{7,4},{8,9},{9,10},{10,1... | collective-permute-start | bytes 1990664 | tf_op jit(solution)/shard_map/ppermute | solution.py:46
  6.6 28.1 %collective-permute-start.4 = (bf16[144,2304]{1,0:T(8,128)(2,1)}, bf16[144,2304]{1,0:T(8,128)(2,1)S(1)}, u32[]{:S(2)}, u32[]{:S(2)}) collective-permute-start(bf16[144,2304]{1,0:T(8,128)(2,1)} %get-tuple-element.27), channel_id=1, source_target_pairs={{0,2},{1,3},{2,0},{3,1},{4,6},{5,7},{6,4},{7,5},{8,10},{9,11},{10,... | collective-permute-start | bytes 1990664 | tf_op jit(solution)/shard_map/ppermute | solution.py:46
  10.2 24.5 %collective-permute-start.5 = (bf16[144,2304]{1,0:T(8,128)(2,1)}, bf16[144,2304]{1,0:T(8,128)(2,1)S(1)}, u32[]{:S(2)}, u32[]{:S(2)}) collective-permute-start(bf16[144,2304]{1,0:T(8,128)(2,1)} %get-tuple-element.28), channel_id=1, source_target_pairs={{0,3},{1,0},{2,1},{3,2},{4,7},{5,4},{6,5},{7,6},{8,11},{9,8},{10,9... | collective-permute-start | bytes 1990664 | tf_op jit(solution)/shard_map/ppermute | solution.py:46
  11.2 23.5 %copy-start.3 = (bf16[144,2304]{1,0:T(8,128)(2,1)S(1)}, bf16[144,2304]{1,0:T(8,128)(2,1)}, u32[]{:S(2)}) copy-start(bf16[144,2304]{1,0:T(8,128)(2,1)} %get-tuple-element.25.w0.p0) | copy-start | bytes 1990660
  11.2 23.5 %copy-start.4 = (s32[8]{0:T(128)S(1)}, s32[8]{0:T(128)}, u32[]{:S(2)}) copy-start(s32[8]{0:T(128)} %stack.29.at) | copy-start | bytes 100
  11.2 85.6 %copy-start.2 = (bf16[1,256,7168]{2,1,0:T(8,128)(2,1)S(1)}, bf16[1,256,7168]{2,1,0:T(8,128)(2,1)}, u32[]{:S(2)}) copy-start(bf16[1,256,7168]{2,1,0:T(8,128)(2,1)} %refs_6_.2) | copy-start | bytes 11010052
  34.8 62.0 %copy-start.1 = (bf16[1,7168,256]{2,1,0:T(8,128)(2,1)S(1)}, bf16[1,7168,256]{2,1,0:T(8,128)(2,1)}, u32[]{:S(2)}) copy-start(bf16[1,7168,256]{2,1,0:T(8,128)(2,1)} %refs_4_.2) | copy-start | bytes 11010052
  36.6 4.3 %collective-permute-start.8 = (bf16[4,64,128]{2,1,0:T(8,128)(2,1)S(1)}, bf16[4,64,128]{2,1,0:T(8,128)(2,1)S(1)}, u32[]{:S(2)}, u32[]{:S(2)}) collective-permute-start(bf16[4,64,128]{2,1,0:T(8,128)(2,1)S(1)} %shard_map.120.h0), channel_id=1, source_target_pairs={{0,3},{1,0},{2,1},{3,2},{4,7},{5,4},{6,5},{7,6},{8,11},{9,8},{10,9... | collective-permute-start | bytes 196616 | tf_op jit(solution)/shard_map/ppermute | solution.py:46
  37.4 5.8 %collective-permute-start.7 = (bf16[4,64,128]{2,1,0:T(8,128)(2,1)S(1)}, bf16[4,64,128]{2,1,0:T(8,128)(2,1)S(1)}, u32[]{:S(2)}, u32[]{:S(2)}) collective-permute-start(bf16[4,64,128]{2,1,0:T(8,128)(2,1)S(1)} %shard_map.120.h0), channel_id=1, source_target_pairs={{0,2},{1,3},{2,0},{3,1},{4,6},{5,7},{6,4},{7,5},{8,10},{9,11},{10,... | collective-permute-start | bytes 196616 | tf_op jit(solution)/shard_map/ppermute | solution.py:46
  40.5 5.5 %collective-permute-start.6 = (bf16[4,64,128]{2,1,0:T(8,128)(2,1)S(1)}, bf16[4,64,128]{2,1,0:T(8,128)(2,1)S(1)}, u32[]{:S(2)}, u32[]{:S(2)}) collective-permute-start(bf16[4,64,128]{2,1,0:T(8,128)(2,1)S(1)} %shard_map.120.h0), channel_id=1, source_target_pairs={{0,1},{1,2},{2,3},{3,0},{4,5},{5,6},{6,7},{7,4},{8,9},{9,10},{10,1... | collective-permute-start | bytes 196616 | tf_op jit(solution)/shard_map/ppermute | solution.py:46
  46.0 50.8 %copy-start = (bf16[1,7168,256]{2,1,0:T(8,128)(2,1)S(1)}, bf16[1,7168,256]{2,1,0:T(8,128)(2,1)}, u32[]{:S(2)}) copy-start(bf16[1,7168,256]{2,1,0:T(8,128)(2,1)} %refs_2_.1) | copy-start | bytes 11010052
  47.7 24.4 %copy-start.5 = (bf16[7168]{0:T(1024)(128)(2,1)S(1)}, bf16[7168]{0:T(1024)(128)(2,1)}, u32[]{:S(2)}) copy-start(bf16[7168]{0:T(1024)(128)(2,1)} %param.18) | copy-start | bytes 43012
  47.7 7.9 %collective-permute-start.9 = (bf16[64,1920]{1,0:T(8,128)(2,1)S(1)}, bf16[64,1920]{1,0:T(8,128)(2,1)S(1)}, u32[]{:S(2)}, u32[]{:S(2)}) collective-permute-start(bf16[64,1920]{1,0:T(8,128)(2,1)S(1)} %get-tuple-element.30), channel_id=1, source_target_pairs={{0,32},{16,48},{32,0},{48,16},{1,33},{17,49},{33,1},{49,17},{2,34}... | collective-permute-start | bytes 737288 | tf_op jit(solution)/shard_map/ppermute | solution.py:46
  49.1 9.0 %collective-permute-start.10 = (bf16[64,1920]{1,0:T(8,128)(2,1)S(1)}, bf16[64,1920]{1,0:T(8,128)(2,1)S(1)}, u32[]{:S(2)}, u32[]{:S(2)}) collective-permute-start(bf16[64,1920]{1,0:T(8,128)(2,1)S(1)} %get-tuple-element.31), channel_id=1, source_target_pairs={{0,16},{16,32},{32,48},{48,0},{1,17},{17,33},{33,49},{49,1},{2,18}... | collective-permute-start | bytes 737288 | tf_op jit(solution)/shard_map/ppermute | solution.py:46
  49.7 8.4 %collective-permute-start.11 = (bf16[64,1920]{1,0:T(8,128)(2,1)S(1)}, bf16[64,1920]{1,0:T(8,128)(2,1)S(1)}, u32[]{:S(2)}, u32[]{:S(2)}) collective-permute-start(bf16[64,1920]{1,0:T(8,128)(2,1)S(1)} %get-tuple-element.32), channel_id=1, source_target_pairs={{0,48},{16,0},{32,16},{48,32},{1,49},{17,1},{33,17},{49,33},{2,50}... | collective-permute-start | bytes 737288 | tf_op jit(solution)/shard_map/ppermute | solution.py:46
  58.3 6.3 %collective-permute-start.14 = (bf16[64,1920]{1,0:T(8,128)(2,1)S(1)}, bf16[64,1920]{1,0:T(8,128)(2,1)S(1)}, u32[]{:S(2)}, u32[]{:S(2)}) collective-permute-start(bf16[64,1920]{1,0:T(8,128)(2,1)S(1)} %add_convert_fusion.2), channel_id=1, source_target_pairs={{0,12},{4,0},{8,4},{12,8},{1,13},{5,1},{9,5},{13,9},{2,14},{6,2},{... | collective-permute-start | bytes 737288 | tf_op jit(solution)/shard_map/ppermute | solution.py:46
  59.4 7.8 %collective-permute-start.13 = (bf16[64,1920]{1,0:T(8,128)(2,1)S(1)}, bf16[64,1920]{1,0:T(8,128)(2,1)S(1)}, u32[]{:S(2)}, u32[]{:S(2)}) collective-permute-start(bf16[64,1920]{1,0:T(8,128)(2,1)S(1)} %add_convert_fusion.2), channel_id=1, source_target_pairs={{0,8},{4,12},{8,0},{12,4},{1,9},{5,13},{9,1},{13,5},{2,10},{6,14},... | collective-permute-start | bytes 737288 | tf_op jit(solution)/shard_map/ppermute | solution.py:46
  60.9 8.9 %collective-permute-start.12 = (bf16[64,1920]{1,0:T(8,128)(2,1)S(1)}, bf16[64,1920]{1,0:T(8,128)(2,1)S(1)}, u32[]{:S(2)}, u32[]{:S(2)}) collective-permute-start(bf16[64,1920]{1,0:T(8,128)(2,1)S(1)} %add_convert_fusion.2), channel_id=1, source_target_pairs={{0,4},{4,8},{8,12},{12,0},{1,5},{5,9},{9,13},{13,1},{2,6},{6,10},{... | collective-permute-start | bytes 737288 | tf_op jit(solution)/shard_map/ppermute | solution.py:46
  69.9 6.4 %collective-permute-start.17 = (bf16[64,1920]{1,0:T(8,128)(2,1)S(1)}, bf16[64,1920]{1,0:T(8,128)(2,1)S(1)}, u32[]{:S(2)}, u32[]{:S(2)}) collective-permute-start(bf16[64,1920]{1,0:T(8,128)(2,1)S(1)} %add_convert_fusion.1.s0), channel_id=1, source_target_pairs={{0,3},{1,0},{2,1},{3,2},{4,7},{5,4},{6,5},{7,6},{8,11},{9,8},{10,9... | collective-permute-start | bytes 737288 | tf_op jit(solution)/shard_map/ppermute | solution.py:46
  70.1 7.9 %collective-permute-start.16 = (bf16[64,1920]{1,0:T(8,128)(2,1)S(1)}, bf16[64,1920]{1,0:T(8,128)(2,1)S(1)}, u32[]{:S(2)}, u32[]{:S(2)}) collective-permute-start(bf16[64,1920]{1,0:T(8,128)(2,1)S(1)} %add_convert_fusion.1.s0), channel_id=1, source_target_pairs={{0,2},{1,3},{2,0},{3,1},{4,6},{5,7},{6,4},{7,5},{8,10},{9,11},{10,... | collective-permute-start | bytes 737288 | tf_op jit(solution)/shard_map/ppermute | solution.py:46
  71.7 8.9 %collective-permute-start.15 = (bf16[64,1920]{1,0:T(8,128)(2,1)S(1)}, bf16[64,1920]{1,0:T(8,128)(2,1)S(1)}, u32[]{:S(2)}, u32[]{:S(2)}) collective-permute-start(bf16[64,1920]{1,0:T(8,128)(2,1)S(1)} %add_convert_fusion.1.s0), channel_id=1, source_target_pairs={{0,1},{1,2},{2,3},{3,0},{4,5},{5,6},{6,7},{7,4},{8,9},{9,10},{10,1... | collective-permute-start | bytes 737288 | tf_op jit(solution)/shard_map/ppermute | solution.py:46
  81.5 15.3 %collective-permute-start.22 = (bf16[64,7296]{1,0:T(8,128)(2,1)S(1)}, bf16[64,7296]{1,0:T(8,128)(2,1)S(1)}, u32[]{:S(2)}, u32[]{:S(2)}) collective-permute-start(bf16[64,7296]{1,0:T(8,128)(2,1)S(1)} %get-tuple-element.34.refs_0_.refs_1_), channel_id=1, source_target_pairs={{0,32},{16,48},{32,0},{48,16},{1,33},{17,49},{33,1},{49,17},{2,34}... | collective-permute-start | bytes 2801672 | tf_op jit(solution)/shard_map/ppermute | solution.py:46
  82.8 25.3 %collective-permute-start.19 = (bf16[64,7296]{1,0:T(8,128)(2,1)S(1)}, bf16[64,7296]{1,0:T(8,128)(2,1)S(1)}, u32[]{:S(2)}, u32[]{:S(2)}) collective-permute-start(bf16[64,7296]{1,0:T(8,128)(2,1)S(1)} %get-tuple-element.34.refs_0_.refs_1_), channel_id=1, source_target_pairs={{0,48},{16,0},{32,16},{48,32},{1,49},{17,1},{33,17},{49,33},{2,50}... | collective-permute-start | bytes 2801672 | tf_op jit(solution)/shard_map/ppermute | solution.py:46
  84.5 23.6 %collective-permute-start.18 = (bf16[64,7296]{1,0:T(8,128)(2,1)S(1)}, bf16[64,7296]{1,0:T(8,128)(2,1)S(1)}, u32[]{:S(2)}, u32[]{:S(2)}) collective-permute-start(bf16[64,7296]{1,0:T(8,128)(2,1)S(1)} %get-tuple-element.34.refs_0_.refs_1_), channel_id=1, source_target_pairs={{0,16},{16,32},{32,48},{48,0},{1,17},{17,33},{33,49},{49,1},{2,18}... | collective-permute-start | bytes 2801672 | tf_op jit(solution)/shard_map/ppermute | solution.py:46
  106.9 23.6 %collective-permute-start.23 = (bf16[64,7168]{1,0:T(8,128)(2,1)S(1)}, bf16[64,7168]{1,0:T(8,128)(2,1)S(1)}, u32[]{:S(2)}, u32[]{:S(2)}) collective-permute-start(bf16[64,7168]{1,0:T(8,128)(2,1)S(1)} %shard_map.125), channel_id=1, source_target_pairs={{0,32},{16,48},{32,0},{48,16},{1,33},{17,49},{33,1},{49,17},{2,34}... | collective-permute-start | bytes 2752520 | tf_op jit(solution)/shard_map/ppermute | solution.py:46
  118.4 13.5 %collective-permute-start.20 = (bf16[64,7168]{1,0:T(8,128)(2,1)S(1)}, bf16[64,7168]{1,0:T(8,128)(2,1)S(1)}, u32[]{:S(2)}, u32[]{:S(2)}) collective-permute-start(bf16[64,7168]{1,0:T(8,128)(2,1)S(1)} %get-tuple-element.41), channel_id=1, source_target_pairs={{0,48},{16,0},{32,16},{48,32},{1,49},{17,1},{33,17},{49,33},{2,50}... | collective-permute-start | bytes 2752520 | tf_op jit(solution)/shard_map/ppermute | solution.py:46
  120.2 14.6 %collective-permute-start.21 = (bf16[64,7168]{1,0:T(8,128)(2,1)S(1)}, bf16[64,7168]{1,0:T(8,128)(2,1)S(1)}, u32[]{:S(2)}, u32[]{:S(2)}) collective-permute-start(bf16[64,7168]{1,0:T(8,128)(2,1)S(1)} %get-tuple-element.42), channel_id=1, source_target_pairs={{0,16},{16,32},{32,48},{48,0},{1,17},{17,33},{33,49},{49,1},{2,18}... | collective-permute-start | bytes 2752520 | tf_op jit(solution)/shard_map/ppermute | solution.py:46
  136.5 16.2 %all-to-all-start.1 = ((bf16[16,4,7168]{2,1,0:T(4,128)(2,1)}), bf16[16,4,7168]{2,1,0:T(4,128)(2,1)S(1)}, u32[]{:S(2)}, u32[]{:S(2)}) async-start(bf16[16,4,7168]{2,1,0:T(4,128)(2,1)} %reshape.18), calls=%async_computation.1 | async-start | bytes 1835008 | tf_op jit(solution)/shard_map/all_to_all | solution.py:448

commit v4 on v3

--- a/solution.py
+++ b/solution.py
@@ -267,10 +267,10 @@
 def experts_kernel(count, parts, at, *refs):
     xs, ws, refs = refs[:count], refs[count : 2 * count], refs[2 * count :]
     gates, ups, downs, refs = refs[0:2], refs[2:4], refs[4:6], refs[6:]
-    outs, (gate_sum, up_sum, hidden, weights) = refs[:count], refs[count:]
+    outs, (gate_sum, up_sum, hidden, weights) = refs[:-4], refs[-4:]
     step = pl.program_id(0)
     units = gates[0].shape[2]
-    rows = xs[0].shape[0]
+    rows = outs[0].shape[0]
 
     def joined(refs):
         return refs[0][...] if count == 1 else jnp.concatenate([r[...] for r in refs], axis=0)
@@ -315,8 +315,8 @@
             out[...] = total[k * rows : (k + 1) * rows].astype(bf16)
 
 
-def experts(at, slots, gates, ups, downs):
-    count, parts = len(slots), SIDE
+def experts(at, slots, gates, ups, downs, pieces):
+    count, parts = len(slots), 2
     rows = slots[0].shape[0]
     width, units = gates[0].shape[1:]
     block = width // parts
@@ -334,13 +334,14 @@
     in_specs += [pl.BlockSpec((1, units, block), lambda i: (0, 0, second(i)))] * 2
     return call(
         functools.partial(experts_kernel, count, parts),
-        [jax.ShapeDtypeStruct((rows, width), bf16)] * count,
+        [jax.ShapeDtypeStruct((count * rows // pieces, width), bf16)] * pieces,
         (at, *slots, *slots, *gates, *ups, *downs),
         12 * count * rows * width * units,
-        24,
+        28,
         grid=(2 * parts,),
         in_specs=in_specs,
-        out_specs=[pl.BlockSpec((rows, block), lambda i: (0, second(i)))] * count,
+        out_specs=[pl.BlockSpec((count * rows // pieces, block), lambda i: (0, second(i)))]
+        * pieces,
         scratch_shapes=[
             pltpu.VMEM((count * rows, 2 * units), f32),
             pltpu.VMEM((count * rows, 2 * units), f32),
@@ -348,6 +349,76 @@
             pltpu.VMEM((2, count * rows, EXTRA), f32),
         ],
     )
+
+
+def load_kernel(at, x, *refs):
+    sources, out, held, refs = refs[:6], refs[6], refs[7:13], refs[13:]
+    gate_sum, up_sum, hidden, sems = refs
+    gates, ups, downs = held[0:2], held[2:4], held[4:6]
+    _, width, units = gates[0].shape
+    step = width // SIDE
+
+    def copy(k, i):
+        span = pl.ds(i * step, step)
+        where = (0, span) if k < 4 else (0, slice(None), span)
+        return pltpu.make_async_copy(sources[k].at[where], held[k].at[where], sems.at[k, i])
+
+    for i in range(SIDE):
+        for k in range(4):
+            copy(k, i).start()
+    for i in range(SIDE):
+        for k in (4, 5):
+            copy(k, i).start()
+    for i in range(SIDE):
+        span = slice(i * step, (i + 1) * step)
+        for k in range(4):
+            copy(k, i).wait()
+        for k in range(2):
+            to = slice(k * units, (k + 1) * units)
+            gate = jnp.dot(x[:, span], gates[k][0, span, :], preferred_element_type=f32)
+            up = jnp.dot(x[:, span], ups[k][0, span, :], preferred_element_type=f32)
+            gate_sum[:, to] = gate_sum[:, to] + gate if i else gate
+            up_sum[:, to] = up_sum[:, to] + up if i else up
+    gate = gate_sum[...]
+    hidden[...] = (gate * (1.0 / (1.0 + jnp.exp(-gate))) * up_sum[...]).astype(bf16)
+    told = x[:, width:].astype(f32)
+    weights = []
+    for k in range(2):
+        chosen = iota(told.shape, 1) == at[4 + k]
+        weights.append(jnp.sum(jnp.where(chosen, told, 0.0), axis=1, keepdims=True))
+    for i in range(SIDE):
+        span = slice(i * step, (i + 1) * step)
+        total = 0.0
+        for k in range(2):
+            copy(4 + k, i).wait()
+            left = hidden[:, k * units : (k + 1) * units]
+            value = jnp.dot(left, downs[k][0, :, span], preferred_element_type=f32)
+            total = total + value * weights[k]
+        out[:, span] = total.astype(bf16)
+
+
+def experts_and_load(at, x, gates, ups, downs):
+    rows = x.shape[0]
+    width, units = gates[0].shape[1:]
+    blocks = (*gates, *ups, *downs)
+    smem, vmem = [pl.BlockSpec(memory_space=m) for m in (pltpu.SMEM, pltpu.VMEM)]
+    out, *held = call(
+        load_kernel,
+        [jax.ShapeDtypeStruct((rows, width), bf16)]
+        + [jax.ShapeDtypeStruct(v.shape, bf16) for v in blocks],
+        (at, x, *blocks),
+        12 * rows * width * units,
+        30,
+        in_specs=[smem, vmem] + [pl.BlockSpec(memory_space=pltpu.HBM)] * 6,
+        out_specs=[vmem] * 7,
+        scratch_shapes=[
+            pltpu.VMEM((rows, 2 * units), f32),
+            pltpu.VMEM((rows, 2 * units), f32),
+            pltpu.VMEM((rows, 2 * units), bf16),
+            pltpu.SemaphoreType.DMA((6, SIDE)),
+        ],
+    )
+    return out, held[0:2], held[2:4], held[4:6]
 
 
 def on_device(
@@ -437,12 +508,13 @@
         16,
     )
 
+    own_sum, gates, ups, downs = experts_and_load(at, normed, gates, ups, downs)
     near = [shift(normed, "a", s) for s in (1, 3)]
-    far = shift(normed, "a", 2)
-    run = functools.partial(experts, at, gates=gates, ups=ups, downs=downs)
-    (own_sum,) = run([normed])
-    near_sums = run(near)
-    (far_sum,) = run([far])
+    near, own_sum = lax.optimization_barrier((near, own_sum))
+    half = count // 2
+    far = [shift(near[0][:half], "a", 1), shift(near[1][half:], "a", 3)]
+    near_sums = experts(at, near, gates, ups, downs, 2)
+    (far_sum,) = experts(at, far, gates, ups, downs, 1)
     sums = [shift(near_sums[0], "a", -1), shift(near_sums[1], "a", -3), shift(far_sum, "a", -2)]
     last = added([own_sum] + sums).reshape(16, rows, width)
     last = lax.all_to_all(last, AXES, 0, 0, axis_index_groups=groups("cb"), tiled=True)

time: 155 us -> 152 us (0.981)
  starting transfers between devices: 31.4 us -> 41.1 us
  Pallas kernels: 45.4 us -> 35.8 us
  waiting for transfers between devices: 56.8 us -> 54.5 us
    pallas_call x8, Pallas kernels: 45.4 us -> 35.8 us  [call(): pl.pallas_call(body, out_shape=out_shape, compiler_params=pltpu.CompilerP...]
    ppermute x21 -> x22, starting transfers between devices: 27.1 us -> 34.5 us  [shift(): return lax.ppermute(value, AXES, pairs)]
    all_to_all x1, starting transfers between devices: 3.73 us -> 6.11 us  [on_device(): lax.all_to_all(last, AXES, 0, 0, axis_index_groups=groups('cb'), tiled=True)]
    ppermute x21 -> x22, waiting for transfers between devices: 44.3 us -> 42 us  [shift(): return lax.ppermute(value, AXES, pairs)]
  transfers between devices with their start and end apart: 25 -> 26, of which waited for: 15 -> 14; matrix products, arithmetic and copies ran while one was open for 0% -> 0% of each run, Pallas kernels for 27% -> 21%
where the time goes in v4:
time: 152 us
  waiting for transfers between devices  54.5 us (36%)
  starting transfers between devices  41.1 us (27%)
  Pallas kernels  35.8 us (24%)
  blocking collectives  16.3 us (11%)
  local copies, waits for them, and re-layouts  2.02 us (1%)
  other arithmetic  1.75 us (1%)
    ppermute x22, waiting for transfers between devices, shift(): return lax.ppermute(value, AXES, pairs)  42 us
    pallas_call x8, Pallas kernels, call(): pl.pallas_call(body, out_shape=out_shape, compiler_params=pltpu.CompilerP...  35.8 us
    ppermute x22, starting transfers between devices, shift(): return lax.ppermute(value, AXES, pairs)  34.5 us
    all_to_all x1, blocking collectives, on_device(): lax.all_to_all(sent, AXES, 0, 0, axis_index_groups=groups('ab'), tiled=True)  16.3 us
    all_to_all x1, waiting for transfers between devices, on_device(): lax.all_to_all(last, AXES, 0, 0, axis_index_groups=groups('cb'), tiled=True)  12.5 us
    all_to_all x1, starting transfers between devices, on_device(): lax.all_to_all(last, AXES, 0, 0, axis_index_groups=groups('cb'), tiled=True)  6.11 us
  transfers between devices with their start and end apart: 26, of which 14 were waited for; matrix products, arithmetic and copies ran while one was open for 0% of the time, Pallas kernels for 21%

profile of v4, /device:TPU:0, one launch (start us, length us, event | category | flops | bytes accessed | tf_op | source)
XLA Modules:
  0.0 151.7 jit_solution(8720545921054780560)
XLA Ops:
  0.0 0.0 collective-permute-start
  0.0 0.5 collective-permute-start.1
  0.5 0.0 collective-permute-start.2
  0.5 0.7 stack.29.at
  1.2 3.5 %shard_map.119 = (bf16[144,2304]{1,0:T(8,128)(2,1)}, bf16[144,2304]{1,0:T(8,128)(2,1)}, bf16[144,2304]{1,0:T(8,128)(2,1)}, bf16[144,2304]{1,0:T(8,128)(2,1)}) custom-call(s32[8]{0:T(128)} %stack.29.at, bf16[128,7168]{1,0:T(8,128)(2,1)} %w_out.1, bf16[1,512,128]{2,1,0:T(8,128)(2,1)} %w_uv.1, bf16[4,7168]{1,0:T(4,128)(2,1)} %residual.1, s32[4,8]{1,0:T(4,128)} %ids.1, ...), custom_call_target="tpu_custom_call" | custom-call | tf_op jit(solution)/shard_map/pallas_call | solution.py:65
  4.7 2.0 %collective-permute-start.3 = (bf16[144,2304]{1,0:T(8,128)(2,1)}, bf16[144,2304]{1,0:T(8,128)(2,1)S(1)}, u32[]{:S(2)}, u32[]{:S(2)}) collective-permute-start(bf16[144,2304]{1,0:T(8,128)(2,1)} %get-tuple-element.36), channel_id=1, source_target_pairs={{0,1},{1,2},{2,3},{3,0},{4,5},{5,6},{6,7},{7,4},{8,9},{9,10},{10,1... | collective-permute-start | bytes 1990664 | tf_op jit(solution)/shard_map/ppermute | solution.py:46
  6.7 3.6 %collective-permute-start.4 = (bf16[144,2304]{1,0:T(8,128)(2,1)}, bf16[144,2304]{1,0:T(8,128)(2,1)S(1)}, u32[]{:S(2)}, u32[]{:S(2)}) collective-permute-start(bf16[144,2304]{1,0:T(8,128)(2,1)} %get-tuple-element.37), channel_id=1, source_target_pairs={{0,2},{1,3},{2,0},{3,1},{4,6},{5,7},{6,4},{7,5},{8,10},{9,11},{10,... | collective-permute-start | bytes 1990664 | tf_op jit(solution)/shard_map/ppermute | solution.py:46
  10.2 0.0 collective-permute-done.refs_1_
  10.2 1.0 collective-permute-start.5
  11.3 6.8 %shard_map.118 = bf16[256,512]{1,0:T(8,128)(2,1)} custom-call(s32[4]{0:T(128)} %lengths.1, s32[8]{0:T(128)} %stack.29.at, bf16[4,64,576]{2,1,0:T(8,128)(2,1)} %query.1, bf16[4,576,2048]{2,1,0:T(8,128)(2,1)} %bitcast.12), custom_call_target="tpu_custom_call" | custom-call | flops 1140850688 | bytes 9994288 | tf_op jit(solution)/shard_map/pallas_call | solution.py:65
  18.1 16.3 %all_to_all.10 = bf16[16,16,512]{2,1,0:T(8,128)(2,1)S(1)} all-to-all(bf16[16,16,512]{2,1,0:T(8,128)(2,1)} %bitcast.13), channel_id=1, replica_groups={{0,4,8,12,16,20,24,28,32,36,40,44,48,52,56,60},{1,5,9,13,17,21,25,29,33..., dimensions={0} | all-to-all | bytes 524288 | tf_op jit(solution)/shard_map/all_to_all | solution.py:469
  34.4 0.0 collective-permute-done.1.refs_3_
  34.4 0.0 collective-permute-done.2.refs_5_
  34.4 0.0 collective-permute-done.3.w1.p1
  34.4 0.0 collective-permute-done.4.w2.p2
  34.4 0.0 collective-permute-done.5.w3.p3
  34.5 0.0 copy-start.2
  34.5 1.7 %shard_map.120.h0 = bf16[4,64,128]{2,1,0:T(8,128)(2,1)S(1)} custom-call(s32[8]{0:T(128)S(1)} %copy-done.1, bf16[256,512]{1,0:T(8,128)(2,1)S(1)} %bitcast.10, bf16[144,2304]{1,0:T(8,128)(2,1)S(1)} %copy-done, bf16[144,2304]{1,0:T(8,128)(2,1)S(1)} %collective-permute-done.3.w1.p1, bf16[144,2304]{1,0:T(8,128)(2,1)S(1)} %collective-permute-done.4.w2.p2, ...), custom_call_target="tpu_custom_call" | custom-call | flops 134217728 | bytes 2981920 | tf_op jit(solution)/shard_map/pallas_call | solution.py:65
  36.2 1.6 %collective-permute-start.6 = (bf16[4,64,128]{2,1,0:T(8,128)(2,1)S(1)}, bf16[4,64,128]{2,1,0:T(8,128)(2,1)S(1)}, u32[]{:S(2)}, u32[]{:S(2)}) collective-permute-start(bf16[4,64,128]{2,1,0:T(8,128)(2,1)S(1)} %shard_map.120.h0), channel_id=1, source_target_pairs={{0,1},{1,2},{2,3},{3,0},{4,5},{5,6},{6,7},{7,4},{8,9},{9,10},{10,1... | collective-permute-start | bytes 196616 | tf_op jit(solution)/shard_map/ppermute | solution.py:46
  37.8 1.1 collective-permute-start.7
  38.9 1.7 %collective-permute-start.8 = (bf16[4,64,128]{2,1,0:T(8,128)(2,1)S(1)}, bf16[4,64,128]{2,1,0:T(8,128)(2,1)S(1)}, u32[]{:S(2)}, u32[]{:S(2)}) collective-permute-start(bf16[4,64,128]{2,1,0:T(8,128)(2,1)S(1)} %shard_map.120.h0), channel_id=1, source_target_pairs={{0,3},{1,0},{2,1},{3,2},{4,7},{5,4},{6,5},{7,6},{8,11},{9,8},{10,9... | collective-permute-start | bytes 196616 | tf_op jit(solution)/shard_map/ppermute | solution.py:46
  40.6 1.2 collective-permute-done.6.h1
  41.8 1.8 %collective-permute-done.7.h2 = bf16[4,64,128]{2,1,0:T(8,128)(2,1)S(1)} collective-permute-done((bf16[4,64,128]{2,1,0:T(8,128)(2,1)S(1)}, bf16[4,64,128]{2,1,0:T(8,128)(2,1)S(1)}, u32[]{:S(2)}, u32[]{:S(2)}) %collective-permute-start.7) | collective-permute-done | bytes 65568 | tf_op jit(solution)/shard_map/ppermute | solution.py:46
  43.6 1.7 %shard_map.121 = (bf16[64,1920]{1,0:T(8,128)(2,1)S(1)}, bf16[64,1920]{1,0:T(8,128)(2,1)S(1)}, bf16[64,1920]{1,0:T(8,128)(2,1)S(1)}, bf16[64,1920]{1,0:T(8,128)(2,1)S(1)}) custom-call(s32[8]{0:T(128)S(1)} %copy-done.1, bf16[4,64,128]{2,1,0:T(8,128)(2,1)S(1)} %shard_map.120.h0, bf16[4,64,128]{2,1,0:T(8,128)(2,1)S(1)} %collective-permute-done.6.h1, ...), custom_call_target="tpu_custom_call" | custom-call | flops 469762048 | bytes 3899424 | tf_op jit(solution)/shard_map/pallas_call | solution.py:65
  45.3 0.3 collective-permute-start.10
  45.7 3.0 %collective-permute-start.11 = (bf16[64,1920]{1,0:T(8,128)(2,1)S(1)}, bf16[64,1920]{1,0:T(8,128)(2,1)S(1)}, u32[]{:S(2)}, u32[]{:S(2)}) collective-permute-start(bf16[64,1920]{1,0:T(8,128)(2,1)S(1)} %get-tuple-element.42), channel_id=1, source_target_pairs={{0,48},{16,0},{32,16},{48,32},{1,49},{17,1},{33,17},{49,33},{2,50}... | collective-permute-start | bytes 737288 | tf_op jit(solution)/shard_map/ppermute | solution.py:46
  48.7 0.1 collective-permute-start.9
  48.8 4.0 %collective-permute-done.10 = bf16[64,1920]{1,0:T(8,128)(2,1)S(1)} collective-permute-done((bf16[64,1920]{1,0:T(8,128)(2,1)S(1)}, bf16[64,1920]{1,0:T(8,128)(2,1)S(1)}, u32[]{:S(2)}, u32[]{:S(2)}) %collective-permute-start.10) | collective-permute-done | bytes 245792 | tf_op jit(solution)/shard_map/ppermute | solution.py:46
  52.8 2.2 %collective-permute-done.11 = bf16[64,1920]{1,0:T(8,128)(2,1)S(1)} collective-permute-done((bf16[64,1920]{1,0:T(8,128)(2,1)S(1)}, bf16[64,1920]{1,0:T(8,128)(2,1)S(1)}, u32[]{:S(2)}, u32[]{:S(2)}) %collective-permute-start.11) | collective-permute-done | bytes 245792 | tf_op jit(solution)/shard_map/ppermute | solution.py:46
  55.0 1.4 collective-permute-done.9
  56.4 0.1 add_convert_fusion.2
  56.5 0.5 collective-permute-start.12
  57.0 2.1 %collective-permute-start.13 = (bf16[64,1920]{1,0:T(8,128)(2,1)S(1)}, bf16[64,1920]{1,0:T(8,128)(2,1)S(1)}, u32[]{:S(2)}, u32[]{:S(2)}) collective-permute-start(bf16[64,1920]{1,0:T(8,128)(2,1)S(1)} %add_convert_fusion.2), channel_id=1, source_target_pairs={{0,8},{4,12},{8,0},{12,4},{1,9},{5,13},{9,1},{13,5},{2,10},{6,14},... | collective-permute-start | bytes 737288 | tf_op jit(solution)/shard_map/ppermute | solution.py:46
  59.0 1.6 %collective-permute-start.14 = (bf16[64,1920]{1,0:T(8,128)(2,1)S(1)}, bf16[64,1920]{1,0:T(8,128)(2,1)S(1)}, u32[]{:S(2)}, u32[]{:S(2)}) collective-permute-start(bf16[64,1920]{1,0:T(8,128)(2,1)S(1)} %add_convert_fusion.2), channel_id=1, source_target_pairs={{0,12},{4,0},{8,4},{12,8},{1,13},{5,1},{9,5},{13,9},{2,14},{6,2},{... | collective-permute-start | bytes 737288 | tf_op jit(solution)/shard_map/ppermute | solution.py:46
  60.7 5.9 %collective-permute-done.12 = bf16[64,1920]{1,0:T(8,128)(2,1)S(1)} collective-permute-done((bf16[64,1920]{1,0:T(8,128)(2,1)S(1)}, bf16[64,1920]{1,0:T(8,128)(2,1)S(1)}, u32[]{:S(2)}, u32[]{:S(2)}) %collective-permute-start.12) | collective-permute-done | bytes 245792 | tf_op jit(solution)/shard_map/ppermute | solution.py:46
  66.6 0.0 collective-permute-done.13
  66.6 0.9 collective-permute-done.14
  67.5 0.1 add_convert_fusion.1.s0
  67.6 1.3 collective-permute-start.15
  68.9 2.9 %collective-permute-start.16 = (bf16[64,1920]{1,0:T(8,128)(2,1)S(1)}, bf16[64,1920]{1,0:T(8,128)(2,1)S(1)}, u32[]{:S(2)}, u32[]{:S(2)}) collective-permute-start(bf16[64,1920]{1,0:T(8,128)(2,1)S(1)} %add_convert_fusion.1.s0), channel_id=1, source_target_pairs={{0,2},{1,3},{2,0},{3,1},{4,6},{5,7},{6,4},{7,5},{8,10},{9,11},{10,... | collective-permute-start | bytes 737288 | tf_op jit(solution)/shard_map/ppermute | solution.py:46
  71.8 0.7 collective-permute-start.17
  72.5 2.8 %collective-permute-done.15.s1 = bf16[64,1920]{1,0:T(8,128)(2,1)S(1)} collective-permute-done((bf16[64,1920]{1,0:T(8,128)(2,1)S(1)}, bf16[64,1920]{1,0:T(8,128)(2,1)S(1)}, u32[]{:S(2)}, u32[]{:S(2)}) %collective-permute-start.15) | collective-permute-done | bytes 245792 | tf_op jit(solution)/shard_map/ppermute | solution.py:46
  75.3 3.3 %collective-permute-done.16.s2 = bf16[64,1920]{1,0:T(8,128)(2,1)S(1)} collective-permute-done((bf16[64,1920]{1,0:T(8,128)(2,1)S(1)}, bf16[64,1920]{1,0:T(8,128)(2,1)S(1)}, u32[]{:S(2)}, u32[]{:S(2)}) %collective-permute-start.16) | collective-permute-done | bytes 245792 | tf_op jit(solution)/shard_map/ppermute | solution.py:46
  78.6 0.2 collective-permute-done.17.s3
  78.8 1.0 shard_map.122
  79.8 0.1 collective-permute-start.18
  79.9 3.2 %collective-permute-start.19 = (bf16[64,7296]{1,0:T(8,128)(2,1)S(1)}, bf16[64,7296]{1,0:T(8,128)(2,1)S(1)}, u32[]{:S(2)}, u32[]{:S(2)}) collective-permute-start(bf16[64,7296]{1,0:T(8,128)(2,1)S(1)} %get-tuple-element.44.x), channel_id=1, source_target_pairs={{0,48},{16,0},{32,16},{48,32},{1,49},{17,1},{33,17},{49,33},{2,50}... | collective-permute-start | bytes 2801672 | tf_op jit(solution)/shard_map/ppermute | solution.py:46
  83.1 9.1 %shard_map.123 = (bf16[64,7168]{1,0:T(8,128)(2,1)S(1)}, bf16[1,7168,256]{2,1,0:T(8,128)(2,1)S(1)}, bf16[1,7168,256]{2,1,0:T(8,128)(2,1)S(1)}, bf16[1,7168,256]{2...) custom-call(s32[8]{0:T(128)S(1)} %copy-done.1, ...), custom_call_target="tpu_custom_call" | custom-call | flops 1409286144 | bytes 45891616 | tf_op jit(solution)/shard_map/pallas_call | solution.py:65
  92.2 2.4 %collective-permute-done.18.refs_0_.refs_2_ = bf16[64,7296]{1,0:T(8,128)(2,1)S(1)} collective-permute-done((bf16[64,7296]{1,0:T(8,128)(2,1)S(1)}, bf16[64,7296]{1,0:T(8,128)(2,1)S(1)}, u32[]{:S(2)}, u32[]{:S(2)}) %collective-permute-start.18) | collective-permute-done | bytes 933920 | tf_op jit(solution)/shard_map/ppermute | solution.py:46
  94.7 0.6 collective-permute-start.22
  95.3 2.8 %collective-permute-start.23 = (bf16[32,7296]{1,0:T(8,128)(2,1)S(1)}, bf16[32,7296]{1,0:T(8,128)(2,1)S(1)}, u32[]{:S(2)}, u32[]{:S(2)}) collective-permute-start(bf16[32,7296]{1,0:T(8,128)(2,1)S(1)} %slice.7), channel_id=1, source_target_pairs={{0,48},{16,0},{32,16},{48,32},{1,49},{17,1},{33,17},{49,33},{2,50}... | collective-permute-start | bytes 1400840 | tf_op jit(solution)/shard_map/ppermute | solution.py:46
  98.1 5.7 %shard_map.124 = (bf16[64,7168]{1,0:T(8,128)(2,1)S(1)}, bf16[64,7168]{1,0:T(8,128)(2,1)S(1)}) custom-call(s32[8]{0:T(128)S(1)} %copy-done.1, bf16[64,7296]{1,0:T(8,128)(2,1)S(1)} %collective-permute-done.18.refs_0_.refs_2_, bf16[64,7296]{1,0:T(8,128)(2,1)S(1)} %collective-permute-done.19.refs_1_.refs_3_, ...), custom_call_target="tpu_custom_call" | custom-call | flops 2818572288 | bytes 27590688 | tf_op jit(solution)/shard_map/pallas_call | solution.py:65
  103.8 2.1 %collective-permute-start.20 = (bf16[64,7168]{1,0:T(8,128)(2,1)S(1)}, bf16[64,7168]{1,0:T(8,128)(2,1)S(1)}, u32[]{:S(2)}, u32[]{:S(2)}) collective-permute-start(bf16[64,7168]{1,0:T(8,128)(2,1)S(1)} %get-tuple-element.61), channel_id=1, source_target_pairs={{0,48},{16,0},{32,16},{48,32},{1,49},{17,1},{33,17},{49,33},{2,50}... | collective-permute-start | bytes 2752520 | tf_op jit(solution)/shard_map/ppermute | solution.py:46
  105.9 0.0 collective-permute-start.21
  105.9 6.2 %shard_map.125 = bf16[64,7168]{1,0:T(8,128)(2,1)S(1)} custom-call(s32[8]{0:T(128)S(1)} %copy-done.1, bf16[32,7296]{1,0:T(8,128)(2,1)S(1)} %collective-permute-done.22.refs_0_.refs_2_, bf16[32,7296]{1,0:T(8,128)(2,1)S(1)} %collective-permute-done.23.refs_1_.refs_3_, bf16[32,7296]{1,0:T(8,128)(2,1)S(1)} %collective-permute-done.22.refs_0_.refs_2_, ...), custom_call_target="tpu_custom_call" | custom-call | flops 1409286144 | bytes 24805408 | tf_op jit(solution)/shard_map/pallas_call | solution.py:65
  112.1 2.2 %collective-permute-start.24 = (bf16[64,7168]{1,0:T(8,128)(2,1)S(1)}, bf16[64,7168]{1,0:T(8,128)(2,1)S(1)}, u32[]{:S(2)}, u32[]{:S(2)}) collective-permute-start(bf16[64,7168]{1,0:T(8,128)(2,1)S(1)} %shard_map.125), channel_id=1, source_target_pairs={{0,32},{16,48},{32,0},{48,16},{1,33},{17,49},{33,1},{49,17},{2,34}... | collective-permute-start | bytes 2752520 | tf_op jit(solution)/shard_map/ppermute | solution.py:46
  114.4 2.9 %collective-permute-done.20 = bf16[64,7168]{1,0:T(8,128)(2,1)S(1)} collective-permute-done((bf16[64,7168]{1,0:T(8,128)(2,1)S(1)}, bf16[64,7168]{1,0:T(8,128)(2,1)S(1)}, u32[]{:S(2)}, u32[]{:S(2)}) %collective-permute-start.20) | collective-permute-done | bytes 917536 | tf_op jit(solution)/shard_map/ppermute | solution.py:46
  117.3 13.0 %collective-permute-done.21 = bf16[64,7168]{1,0:T(8,128)(2,1)S(1)} collective-permute-done((bf16[64,7168]{1,0:T(8,128)(2,1)S(1)}, bf16[64,7168]{1,0:T(8,128)(2,1)S(1)}, u32[]{:S(2)}, u32[]{:S(2)}) %collective-permute-start.21) | collective-permute-done | bytes 917536 | tf_op jit(solution)/shard_map/ppermute | solution.py:46
  130.3 0.5 add_convert_fusion
  130.8 1.3 reshape.18
  132.0 6.1 %all-to-all-start.1 = ((bf16[16,4,7168]{2,1,0:T(4,128)(2,1)}), bf16[16,4,7168]{2,1,0:T(4,128)(2,1)S(1)}, u32[]{:S(2)}, u32[]{:S(2)}) async-start(bf16[16,4,7168]{2,1,0:T(4,128)(2,1)} %reshape.18), calls=%async_computation.1 | async-start | bytes 1835008 | tf_op jit(solution)/shard_map/all_to_all | solution.py:520
  138.2 12.5 %all-to-all-done.1 = bf16[16,4,7168]{2,1,0:T(4,128)(2,1)S(1)} async-done(((bf16[16,4,7168]{2,1,0:T(4,128)(2,1)}), bf16[16,4,7168]{2,1,0:T(4,128)(2,1)S(1)}, u32[]{:S(2)}, u32[]{:S(2)}) %all-to-all-start.1) | async-done | bytes 917536 | tf_op jit(solution)/shard_map/all_to_all | solution.py:520
  150.6 0.4 convert_reduce_fusion
  151.0 0.7 add_convert_fusion.3
  (13 shorter events, 0.1 us)
Async XLA Ops:
  0.0 10.2 %collective-permute-start = (bf16[1,7168,256]{2,1,0:T(8,128)(2,1)}, bf16[1,7168,256]{2,1,0:T(8,128)(2,1)}, u32[]{:S(2)}, u32[]{:S(2)}) collective-permute-start(bf16[1,7168,256]{2,1,0:T(8,128)(2,1)} %refs_0_), channel_id=1, source_target_pairs={{0,64},{64,0},{1,65},{65,1},{2,66},{66,2},{3,67},{67,3},{4,68},{68... | collective-permute-start | bytes 11010056 | tf_op jit(solution)/shard_map/ppermute | solution.py:55
  0.0 34.4 %collective-permute-start.1 = (bf16[1,7168,256]{2,1,0:T(8,128)(2,1)}, bf16[1,7168,256]{2,1,0:T(8,128)(2,1)}, u32[]{:S(2)}, u32[]{:S(2)}) collective-permute-start(bf16[1,7168,256]{2,1,0:T(8,128)(2,1)} %refs_2_), channel_id=1, source_target_pairs={{0,64},{64,0},{1,65},{65,1},{2,66},{66,2},{3,67},{67,3},{4,68},{68... | collective-permute-start | bytes 11010056 | tf_op jit(solution)/shard_map/ppermute | solution.py:55
  0.5 33.9 %collective-permute-start.2 = (bf16[1,256,7168]{2,1,0:T(8,128)(2,1)}, bf16[1,256,7168]{2,1,0:T(8,128)(2,1)}, u32[]{:S(2)}, u32[]{:S(2)}) collective-permute-start(bf16[1,256,7168]{2,1,0:T(8,128)(2,1)} %refs_4_), channel_id=1, source_target_pairs={{0,64},{64,0},{1,65},{65,1},{2,66},{66,2},{3,67},{67,3},{4,68},{68... | collective-permute-start | bytes 11010056 | tf_op jit(solution)/shard_map/ppermute | solution.py:55
  4.7 29.8 %collective-permute-start.3 = (bf16[144,2304]{1,0:T(8,128)(2,1)}, bf16[144,2304]{1,0:T(8,128)(2,1)S(1)}, u32[]{:S(2)}, u32[]{:S(2)}) collective-permute-start(bf16[144,2304]{1,0:T(8,128)(2,1)} %get-tuple-element.36), channel_id=1, source_target_pairs={{0,1},{1,2},{2,3},{3,0},{4,5},{5,6},{6,7},{7,4},{8,9},{9,10},{10,1... | collective-permute-start | bytes 1990664 | tf_op jit(solution)/shard_map/ppermute | solution.py:46
  6.7 27.8 %collective-permute-start.4 = (bf16[144,2304]{1,0:T(8,128)(2,1)}, bf16[144,2304]{1,0:T(8,128)(2,1)S(1)}, u32[]{:S(2)}, u32[]{:S(2)}) collective-permute-start(bf16[144,2304]{1,0:T(8,128)(2,1)} %get-tuple-element.37), channel_id=1, source_target_pairs={{0,2},{1,3},{2,0},{3,1},{4,6},{5,7},{6,4},{7,5},{8,10},{9,11},{10,... | collective-permute-start | bytes 1990664 | tf_op jit(solution)/shard_map/ppermute | solution.py:46
  10.2 24.2 %collective-permute-start.5 = (bf16[144,2304]{1,0:T(8,128)(2,1)}, bf16[144,2304]{1,0:T(8,128)(2,1)S(1)}, u32[]{:S(2)}, u32[]{:S(2)}) collective-permute-start(bf16[144,2304]{1,0:T(8,128)(2,1)} %get-tuple-element.38), channel_id=1, source_target_pairs={{0,3},{1,0},{2,1},{3,2},{4,7},{5,4},{6,5},{7,6},{8,11},{9,8},{10,9... | collective-permute-start | bytes 1990664 | tf_op jit(solution)/shard_map/ppermute | solution.py:46
  11.3 23.2 %copy-start = (bf16[144,2304]{1,0:T(8,128)(2,1)S(1)}, bf16[144,2304]{1,0:T(8,128)(2,1)}, u32[]{:S(2)}) copy-start(bf16[144,2304]{1,0:T(8,128)(2,1)} %get-tuple-element.35.w0.p0) | copy-start | bytes 1990660
  11.3 23.2 %copy-start.1 = (s32[8]{0:T(128)S(1)}, s32[8]{0:T(128)}, u32[]{:S(2)}) copy-start(s32[8]{0:T(128)} %stack.29.at) | copy-start | bytes 100
  34.5 38.1 %copy-start.2 = (bf16[7168]{0:T(1024)(128)(2,1)S(1)}, bf16[7168]{0:T(1024)(128)(2,1)}, u32[]{:S(2)}) copy-start(bf16[7168]{0:T(1024)(128)(2,1)} %param.18) | copy-start | bytes 43012
  36.2 5.5 %collective-permute-start.6 = (bf16[4,64,128]{2,1,0:T(8,128)(2,1)S(1)}, bf16[4,64,128]{2,1,0:T(8,128)(2,1)S(1)}, u32[]{:S(2)}, u32[]{:S(2)}) collective-permute-start(bf16[4,64,128]{2,1,0:T(8,128)(2,1)S(1)} %shard_map.120.h0), channel_id=1, source_target_pairs={{0,1},{1,2},{2,3},{3,0},{4,5},{5,6},{6,7},{7,4},{8,9},{9,10},{10,1... | collective-permute-start | bytes 196616 | tf_op jit(solution)/shard_map/ppermute | solution.py:46
  37.8 5.8 %collective-permute-start.7 = (bf16[4,64,128]{2,1,0:T(8,128)(2,1)S(1)}, bf16[4,64,128]{2,1,0:T(8,128)(2,1)S(1)}, u32[]{:S(2)}, u32[]{:S(2)}) collective-permute-start(bf16[4,64,128]{2,1,0:T(8,128)(2,1)S(1)} %shard_map.120.h0), channel_id=1, source_target_pairs={{0,2},{1,3},{2,0},{3,1},{4,6},{5,7},{6,4},{7,5},{8,10},{9,11},{10,... | collective-permute-start | bytes 196616 | tf_op jit(solution)/shard_map/ppermute | solution.py:46
  38.9 4.7 %collective-permute-start.8 = (bf16[4,64,128]{2,1,0:T(8,128)(2,1)S(1)}, bf16[4,64,128]{2,1,0:T(8,128)(2,1)S(1)}, u32[]{:S(2)}, u32[]{:S(2)}) collective-permute-start(bf16[4,64,128]{2,1,0:T(8,128)(2,1)S(1)} %shard_map.120.h0), channel_id=1, source_target_pairs={{0,3},{1,0},{2,1},{3,2},{4,7},{5,4},{6,5},{7,6},{8,11},{9,8},{10,9... | collective-permute-start | bytes 196616 | tf_op jit(solution)/shard_map/ppermute | solution.py:46
  45.3 7.5 %collective-permute-start.10 = (bf16[64,1920]{1,0:T(8,128)(2,1)S(1)}, bf16[64,1920]{1,0:T(8,128)(2,1)S(1)}, u32[]{:S(2)}, u32[]{:S(2)}) collective-permute-start(bf16[64,1920]{1,0:T(8,128)(2,1)S(1)} %get-tuple-element.41), channel_id=1, source_target_pairs={{0,16},{16,32},{32,48},{48,0},{1,17},{17,33},{33,49},{49,1},{2,18}... | collective-permute-start | bytes 737288 | tf_op jit(solution)/shard_map/ppermute | solution.py:46
  45.7 9.3 %collective-permute-start.11 = (bf16[64,1920]{1,0:T(8,128)(2,1)S(1)}, bf16[64,1920]{1,0:T(8,128)(2,1)S(1)}, u32[]{:S(2)}, u32[]{:S(2)}) collective-permute-start(bf16[64,1920]{1,0:T(8,128)(2,1)S(1)} %get-tuple-element.42), channel_id=1, source_target_pairs={{0,48},{16,0},{32,16},{48,32},{1,49},{17,1},{33,17},{49,33},{2,50}... | collective-permute-start | bytes 737288 | tf_op jit(solution)/shard_map/ppermute | solution.py:46
  48.7 7.7 %collective-permute-start.9 = (bf16[64,1920]{1,0:T(8,128)(2,1)S(1)}, bf16[64,1920]{1,0:T(8,128)(2,1)S(1)}, u32[]{:S(2)}, u32[]{:S(2)}) collective-permute-start(bf16[64,1920]{1,0:T(8,128)(2,1)S(1)} %get-tuple-element.40), channel_id=1, source_target_pairs={{0,32},{16,48},{32,0},{48,16},{1,33},{17,49},{33,1},{49,17},{2,34}... | collective-permute-start | bytes 737288 | tf_op jit(solution)/shard_map/ppermute | solution.py:46
  56.5 10.1 %collective-permute-start.12 = (bf16[64,1920]{1,0:T(8,128)(2,1)S(1)}, bf16[64,1920]{1,0:T(8,128)(2,1)S(1)}, u32[]{:S(2)}, u32[]{:S(2)}) collective-permute-start(bf16[64,1920]{1,0:T(8,128)(2,1)S(1)} %add_convert_fusion.2), channel_id=1, source_target_pairs={{0,4},{4,8},{8,12},{12,0},{1,5},{5,9},{9,13},{13,1},{2,6},{6,10},{... | collective-permute-start | bytes 737288 | tf_op jit(solution)/shard_map/ppermute | solution.py:46
  57.0 9.6 %collective-permute-start.13 = (bf16[64,1920]{1,0:T(8,128)(2,1)S(1)}, bf16[64,1920]{1,0:T(8,128)(2,1)S(1)}, u32[]{:S(2)}, u32[]{:S(2)}) collective-permute-start(bf16[64,1920]{1,0:T(8,128)(2,1)S(1)} %add_convert_fusion.2), channel_id=1, source_target_pairs={{0,8},{4,12},{8,0},{12,4},{1,9},{5,13},{9,1},{13,5},{2,10},{6,14},... | collective-permute-start | bytes 737288 | tf_op jit(solution)/shard_map/ppermute | solution.py:46
  59.0 8.4 %collective-permute-start.14 = (bf16[64,1920]{1,0:T(8,128)(2,1)S(1)}, bf16[64,1920]{1,0:T(8,128)(2,1)S(1)}, u32[]{:S(2)}, u32[]{:S(2)}) collective-permute-start(bf16[64,1920]{1,0:T(8,128)(2,1)S(1)} %add_convert_fusion.2), channel_id=1, source_target_pairs={{0,12},{4,0},{8,4},{12,8},{1,13},{5,1},{9,5},{13,9},{2,14},{6,2},{... | collective-permute-start | bytes 737288 | tf_op jit(solution)/shard_map/ppermute | solution.py:46
  67.6 7.7 %collective-permute-start.15 = (bf16[64,1920]{1,0:T(8,128)(2,1)S(1)}, bf16[64,1920]{1,0:T(8,128)(2,1)S(1)}, u32[]{:S(2)}, u32[]{:S(2)}) collective-permute-start(bf16[64,1920]{1,0:T(8,128)(2,1)S(1)} %add_convert_fusion.1.s0), channel_id=1, source_target_pairs={{0,1},{1,2},{2,3},{3,0},{4,5},{5,6},{6,7},{7,4},{8,9},{9,10},{10,1... | collective-permute-start | bytes 737288 | tf_op jit(solution)/shard_map/ppermute | solution.py:46
  68.9 9.7 %collective-permute-start.16 = (bf16[64,1920]{1,0:T(8,128)(2,1)S(1)}, bf16[64,1920]{1,0:T(8,128)(2,1)S(1)}, u32[]{:S(2)}, u32[]{:S(2)}) collective-permute-start(bf16[64,1920]{1,0:T(8,128)(2,1)S(1)} %add_convert_fusion.1.s0), channel_id=1, source_target_pairs={{0,2},{1,3},{2,0},{3,1},{4,6},{5,7},{6,4},{7,5},{8,10},{9,11},{10,... | collective-permute-start | bytes 737288 | tf_op jit(solution)/shard_map/ppermute | solution.py:46
  71.8 7.0 %collective-permute-start.17 = (bf16[64,1920]{1,0:T(8,128)(2,1)S(1)}, bf16[64,1920]{1,0:T(8,128)(2,1)S(1)}, u32[]{:S(2)}, u32[]{:S(2)}) collective-permute-start(bf16[64,1920]{1,0:T(8,128)(2,1)S(1)} %add_convert_fusion.1.s0), channel_id=1, source_target_pairs={{0,3},{1,0},{2,1},{3,2},{4,7},{5,4},{6,5},{7,6},{8,11},{9,8},{10,9... | collective-permute-start | bytes 737288 | tf_op jit(solution)/shard_map/ppermute | solution.py:46
  79.8 14.8 %collective-permute-start.18 = (bf16[64,7296]{1,0:T(8,128)(2,1)S(1)}, bf16[64,7296]{1,0:T(8,128)(2,1)S(1)}, u32[]{:S(2)}, u32[]{:S(2)}) collective-permute-start(bf16[64,7296]{1,0:T(8,128)(2,1)S(1)} %get-tuple-element.44.x), channel_id=1, source_target_pairs={{0,16},{16,32},{32,48},{48,0},{1,17},{17,33},{33,49},{49,1},{2,18}... | collective-permute-start | bytes 2801672 | tf_op jit(solution)/shard_map/ppermute | solution.py:46
  79.9 14.8 %collective-permute-start.19 = (bf16[64,7296]{1,0:T(8,128)(2,1)S(1)}, bf16[64,7296]{1,0:T(8,128)(2,1)S(1)}, u32[]{:S(2)}, u32[]{:S(2)}) collective-permute-start(bf16[64,7296]{1,0:T(8,128)(2,1)S(1)} %get-tuple-element.44.x), channel_id=1, source_target_pairs={{0,48},{16,0},{32,16},{48,32},{1,49},{17,1},{33,17},{49,33},{2,50}... | collective-permute-start | bytes 2801672 | tf_op jit(solution)/shard_map/ppermute | solution.py:46
  94.7 11.2 %collective-permute-start.22 = (bf16[32,7296]{1,0:T(8,128)(2,1)S(1)}, bf16[32,7296]{1,0:T(8,128)(2,1)S(1)}, u32[]{:S(2)}, u32[]{:S(2)}) collective-permute-start(bf16[32,7296]{1,0:T(8,128)(2,1)S(1)} %slice.6), channel_id=1, source_target_pairs={{0,16},{16,32},{32,48},{48,0},{1,17},{17,33},{33,49},{49,1},{2,18}... | collective-permute-start | bytes 1400840 | tf_op jit(solution)/shard_map/ppermute | solution.py:46
  95.3 10.6 %collective-permute-start.23 = (bf16[32,7296]{1,0:T(8,128)(2,1)S(1)}, bf16[32,7296]{1,0:T(8,128)(2,1)S(1)}, u32[]{:S(2)}, u32[]{:S(2)}) collective-permute-start(bf16[32,7296]{1,0:T(8,128)(2,1)S(1)} %slice.7), channel_id=1, source_target_pairs={{0,48},{16,0},{32,16},{48,32},{1,49},{17,1},{33,17},{49,33},{2,50}... | collective-permute-start | bytes 1400840 | tf_op jit(solution)/shard_map/ppermute | solution.py:46
  103.8 13.5 %collective-permute-start.20 = (bf16[64,7168]{1,0:T(8,128)(2,1)S(1)}, bf16[64,7168]{1,0:T(8,128)(2,1)S(1)}, u32[]{:S(2)}, u32[]{:S(2)}) collective-permute-start(bf16[64,7168]{1,0:T(8,128)(2,1)S(1)} %get-tuple-element.61), channel_id=1, source_target_pairs={{0,48},{16,0},{32,16},{48,32},{1,49},{17,1},{33,17},{49,33},{2,50}... | collective-permute-start | bytes 2752520 | tf_op jit(solution)/shard_map/ppermute | solution.py:46
  105.9 24.4 %collective-permute-start.21 = (bf16[64,7168]{1,0:T(8,128)(2,1)S(1)}, bf16[64,7168]{1,0:T(8,128)(2,1)S(1)}, u32[]{:S(2)}, u32[]{:S(2)}) collective-permute-start(bf16[64,7168]{1,0:T(8,128)(2,1)S(1)} %get-tuple-element.62), channel_id=1, source_target_pairs={{0,16},{16,32},{32,48},{48,0},{1,17},{17,33},{33,49},{49,1},{2,18}... | collective-permute-start | bytes 2752520 | tf_op jit(solution)/shard_map/ppermute | solution.py:46
  112.1 18.2 %collective-permute-start.24 = (bf16[64,7168]{1,0:T(8,128)(2,1)S(1)}, bf16[64,7168]{1,0:T(8,128)(2,1)S(1)}, u32[]{:S(2)}, u32[]{:S(2)}) collective-permute-start(bf16[64,7168]{1,0:T(8,128)(2,1)S(1)} %shard_map.125), channel_id=1, source_target_pairs={{0,32},{16,48},{32,0},{48,16},{1,33},{17,49},{33,1},{49,17},{2,34}... | collective-permute-start | bytes 2752520 | tf_op jit(solution)/shard_map/ppermute | solution.py:46
  132.0 18.6 %all-to-all-start.1 = ((bf16[16,4,7168]{2,1,0:T(4,128)(2,1)}), bf16[16,4,7168]{2,1,0:T(4,128)(2,1)S(1)}, u32[]{:S(2)}, u32[]{:S(2)}) async-start(bf16[16,4,7168]{2,1,0:T(4,128)(2,1)} %reshape.18), calls=%async_computation.1 | async-start | bytes 1835008 | tf_op jit(solution)/shard_map/all_to_all | solution.py:520

commit v5 on v4

--- a/solution.py
+++ b/solution.py
@@ -20,9 +20,12 @@
 bf16, f32 = jnp.bfloat16, jnp.float32
 
 
+ORDERS = ("xzy", "zyx")
+PLACE = {"x": 16, "y": 4, "z": 1}
+
+
 def device_at(role, a, b, c):
-    x, y, z = (a, b, c) if role == 0 else (c, a, b)
-    return ((role * SIDE + x) * SIDE + y) * SIDE + z
+    return role * 64 + sum(PLACE[axis] * at for axis, at in zip(ORDERS[role], (a, b, c)))
 
 
 def groups(along):
@@ -115,7 +118,7 @@
             out[depth:, block + EXTRA :] = jnp.zeros((GROUP, latent - EXTRA), bf16)
 
 
-def attend_kernel(lengths, at, query, cache, out, held, scores, most, norm, mixed, sems):
+def attend_kernel(lengths, at, query, cache, out, held, scores, most, norm, mixed, done, sems):
     rows, heads, _ = query.shape
     latent = mixed.shape[2]
     size = most.shape[2]
@@ -163,15 +166,15 @@
 
     where_live(mix)
     lines = out.shape[0]
-    line, head = iota((lines, heads), 0), iota((lines, heads), 1)
+    line = iota((lines, rows * heads), 0)
     a, b, c = line >> 6, (line >> 4) & 3, line & 3
-    wanted = jnp.where(at[0] == 0, a * 16 + b * 4 + c, c * 16 + a * 4 + b)
-    placed = jnp.zeros((lines, latent), f32)
+    orders = [sum(PLACE[axis] * v for axis, v in zip(order, (a, b, c))) for order in ORDERS]
+    wanted = jnp.where(at[0] == 0, *orders) + heads * ((line >> 2) & 3)
+    pick = (wanted == iota((lines, rows * heads), 1)).astype(f32).astype(bf16)
     for row in range(rows):
-        done = (mixed[row] / jnp.sum(norm[row], axis=1, keepdims=True)).astype(bf16)
-        pick = ((wanted == head) & (((line >> 2) & 3) == row)).astype(f32).astype(bf16)
-        placed = placed + jnp.dot(pick, done, preferred_element_type=f32)
-    out[...] = placed.astype(bf16)
+        value = mixed[row] / jnp.sum(norm[row], axis=1, keepdims=True)
+        done[row * heads : (row + 1) * heads, :] = value.astype(bf16)
+    out[...] = jnp.dot(pick, done[...], preferred_element_type=f32).astype(bf16)
 
 
 def attend(lengths, at, queries, cache):
@@ -196,6 +199,7 @@
             pltpu.VMEM((rows, heads, size), f32),
             pltpu.VMEM((rows, heads, size), f32),
             pltpu.VMEM((rows, heads, latent), f32),
+            pltpu.VMEM((lines, latent), bf16),
             pltpu.SemaphoreType.DMA((rows, cache_length // size)),
         ],
     )
@@ -436,9 +440,9 @@
     w_down,
 ):
     role, dev = lax.axis_index("role"), lax.axis_index("dev")
-    x, y, z = dev // 16, dev // 4 % 4, dev % 4
-    first = role == 0
-    a, b, c = jnp.where(first, x, y), jnp.where(first, y, z), jnp.where(first, z, x)
+    a, b, c = [
+        jnp.where(role == 0, *[dev // PLACE[order[i]] % SIDE for order in ORDERS]) for i in range(3)
+    ]
     per_expert = 128 // EXPERTS
     experts_here = [(role * 64 + dev) // per_expert, ((1 - role) * 64 + dev) // per_expert]
     at = jnp.stack([role, a, b, c, *experts_here, role, role]).astype(jnp.int32)

time: 152 us -> 153 us (level); the launches traced: 152 us -> 151 us
  no operation moved by 1% of the time
where the time goes in v5:
time: 153 us; the launch traced here: 151 us
  waiting for transfers between devices  54.2 us (35%)
  starting transfers between devices  40.2 us (26%)
  Pallas kernels  35.6 us (23%)
  blocking collectives  17.2 us (11%)
  local copies, waits for them, and re-layouts  2.02 us (1%)
  other arithmetic  1.75 us (1%)
    ppermute x22, waiting for transfers between devices, shift(): return lax.ppermute(value, AXES, pairs)  42 us
    pallas_call x8, Pallas kernels, call(): pl.pallas_call(body, out_shape=out_shape, compiler_params=pltpu.CompilerP...  35.6 us
    ppermute x22, starting transfers between devices, shift(): return lax.ppermute(value, AXES, pairs)  33.6 us
    all_to_all x1, blocking collectives, on_device(): lax.all_to_all(sent, AXES, 0, 0, axis_index_groups=groups('ab'), tiled=True)  17.2 us
    all_to_all x1, waiting for transfers between devices, on_device(): lax.all_to_all(last, AXES, 0, 0, axis_index_groups=groups('cb'), tiled=True)  12.2 us
    all_to_all x1, starting transfers between devices, on_device(): lax.all_to_all(last, AXES, 0, 0, axis_index_groups=groups('cb'), tiled=True)  6.12 us
  transfers between devices with their start and end apart: 26, of which 14 were waited for; matrix products, arithmetic and copies ran while one was open for 0% of the time, Pallas kernels for 21%

profile of v5, /device:TPU:0, one launch (start us, length us, event | category | flops | bytes accessed | tf_op | source)
XLA Modules:
  0.0 151.1 jit_solution(8671499563071455293)
XLA Ops:
  0.0 0.0 collective-permute-start
  0.0 0.5 collective-permute-start.1
  0.5 0.7 stack.29.at
  1.2 3.5 %shard_map.119 = (bf16[144,2304]{1,0:T(8,128)(2,1)}, bf16[144,2304]{1,0:T(8,128)(2,1)}, bf16[144,2304]{1,0:T(8,128)(2,1)}, bf16[144,2304]{1,0:T(8,128)(2,1)}) custom-call(s32[8]{0:T(128)} %stack.29.at, bf16[128,7168]{1,0:T(8,128)(2,1)} %w_out.1, bf16[1,512,128]{2,1,0:T(8,128)(2,1)} %w_uv.1, bf16[4,7168]{1,0:T(4,128)(2,1)} %residual.1, s32[4,8]{1,0:T(4,128)} %ids.1, ...), custom_call_target="tpu_custom_call" | custom-call | tf_op jit(solution)/shard_map/pallas_call | solution.py:68
  4.7 1.7 %collective-permute-start.3 = (bf16[144,2304]{1,0:T(8,128)(2,1)}, bf16[144,2304]{1,0:T(8,128)(2,1)S(1)}, u32[]{:S(2)}, u32[]{:S(2)}) collective-permute-start(bf16[144,2304]{1,0:T(8,128)(2,1)} %get-tuple-element.36), channel_id=1, source_target_pairs={{0,4},{4,8},{8,12},{12,0},{1,5},{5,9},{9,13},{13,1},{2,6},{6,10},{... | collective-permute-start | bytes 1990664 | tf_op jit(solution)/shard_map/ppermute | solution.py:49
  6.3 2.9 %collective-permute-start.4 = (bf16[144,2304]{1,0:T(8,128)(2,1)}, bf16[144,2304]{1,0:T(8,128)(2,1)S(1)}, u32[]{:S(2)}, u32[]{:S(2)}) collective-permute-start(bf16[144,2304]{1,0:T(8,128)(2,1)} %get-tuple-element.37), channel_id=1, source_target_pairs={{0,8},{4,12},{8,0},{12,4},{1,9},{5,13},{9,1},{13,5},{2,10},{6,14},... | collective-permute-start | bytes 1990664 | tf_op jit(solution)/shard_map/ppermute | solution.py:49
  9.2 0.0 collective-permute-done.refs_1_
  9.2 1.4 collective-permute-start.5
  10.6 6.6 %shard_map.118 = bf16[256,512]{1,0:T(8,128)(2,1)} custom-call(s32[4]{0:T(128)} %lengths.1, s32[8]{0:T(128)} %stack.29.at, bf16[4,64,576]{2,1,0:T(8,128)(2,1)} %query.1, bf16[4,576,2048]{2,1,0:T(8,128)(2,1)} %bitcast.12), custom_call_target="tpu_custom_call" | custom-call | flops 1140850688 | bytes 9994288 | tf_op jit(solution)/shard_map/pallas_call | solution.py:68
  17.2 17.2 %all_to_all.10 = bf16[16,16,512]{2,1,0:T(8,128)(2,1)S(1)} all-to-all(bf16[16,16,512]{2,1,0:T(8,128)(2,1)} %bitcast.13), channel_id=1, replica_groups={{0,1,2,3,16,17,18,19,32,33,34,35,48,49,50,51},{4,5,6,7,20,21,22,23,36,3..., dimensions={0} | all-to-all | bytes 524288 | tf_op jit(solution)/shard_map/all_to_all | solution.py:473
  34.4 0.0 collective-permute-done.4.w2.p2
  34.4 0.0 copy-start.2
  34.5 1.8 %shard_map.120.h0 = bf16[4,64,128]{2,1,0:T(8,128)(2,1)S(1)} custom-call(s32[8]{0:T(128)S(1)} %copy-done.1, bf16[256,512]{1,0:T(8,128)(2,1)S(1)} %bitcast.10, bf16[144,2304]{1,0:T(8,128)(2,1)S(1)} %copy-done, bf16[144,2304]{1,0:T(8,128)(2,1)S(1)} %collective-permute-done.3.w1.p1, bf16[144,2304]{1,0:T(8,128)(2,1)S(1)} %collective-permute-done.4.w2.p2, ...), custom_call_target="tpu_custom_call" | custom-call | flops 134217728 | bytes 2981920 | tf_op jit(solution)/shard_map/pallas_call | solution.py:68
  36.2 1.5 collective-permute-start.6
  37.7 0.4 collective-permute-start.7
  38.1 2.3 %collective-permute-start.8 = (bf16[4,64,128]{2,1,0:T(8,128)(2,1)S(1)}, bf16[4,64,128]{2,1,0:T(8,128)(2,1)S(1)}, u32[]{:S(2)}, u32[]{:S(2)}) collective-permute-start(bf16[4,64,128]{2,1,0:T(8,128)(2,1)S(1)} %shard_map.120.h0), channel_id=1, source_target_pairs={{0,12},{4,0},{8,4},{12,8},{1,13},{5,1},{9,5},{13,9},{2,14},{6,2},{... | collective-permute-start | bytes 196616 | tf_op jit(solution)/shard_map/ppermute | solution.py:49
  40.5 1.3 collective-permute-done.6.h1
  41.8 1.7 %collective-permute-done.7.h2 = bf16[4,64,128]{2,1,0:T(8,128)(2,1)S(1)} collective-permute-done((bf16[4,64,128]{2,1,0:T(8,128)(2,1)S(1)}, bf16[4,64,128]{2,1,0:T(8,128)(2,1)S(1)}, u32[]{:S(2)}, u32[]{:S(2)}) %collective-permute-start.7) | collective-permute-done | bytes 65568 | tf_op jit(solution)/shard_map/ppermute | solution.py:49
  43.5 0.0 collective-permute-done.8.h3
  43.5 1.7 %shard_map.121 = (bf16[64,1920]{1,0:T(8,128)(2,1)S(1)}, bf16[64,1920]{1,0:T(8,128)(2,1)S(1)}, bf16[64,1920]{1,0:T(8,128)(2,1)S(1)}, bf16[64,1920]{1,0:T(8,128)(2,1)S(1)}) custom-call(s32[8]{0:T(128)S(1)} %copy-done.1, bf16[4,64,128]{2,1,0:T(8,128)(2,1)S(1)} %shard_map.120.h0, bf16[4,64,128]{2,1,0:T(8,128)(2,1)S(1)} %collective-permute-done.6.h1, ...), custom_call_target="tpu_custom_call" | custom-call | flops 469762048 | bytes 3899424 | tf_op jit(solution)/shard_map/pallas_call | solution.py:68
  45.2 0.3 collective-permute-start.10
  45.6 3.0 %collective-permute-start.11 = (bf16[64,1920]{1,0:T(8,128)(2,1)S(1)}, bf16[64,1920]{1,0:T(8,128)(2,1)S(1)}, u32[]{:S(2)}, u32[]{:S(2)}) collective-permute-start(bf16[64,1920]{1,0:T(8,128)(2,1)S(1)} %get-tuple-element.42), channel_id=1, source_target_pairs={{0,48},{16,0},{32,16},{48,32},{4,52},{20,4},{36,20},{52,36},{8,56}... | collective-permute-start | bytes 737288 | tf_op jit(solution)/shard_map/ppermute | solution.py:49
  48.6 0.1 collective-permute-start.9
  48.7 4.0 %collective-permute-done.10 = bf16[64,1920]{1,0:T(8,128)(2,1)S(1)} collective-permute-done((bf16[64,1920]{1,0:T(8,128)(2,1)S(1)}, bf16[64,1920]{1,0:T(8,128)(2,1)S(1)}, u32[]{:S(2)}, u32[]{:S(2)}) %collective-permute-start.10) | collective-permute-done | bytes 245792 | tf_op jit(solution)/shard_map/ppermute | solution.py:49
  52.7 2.2 %collective-permute-done.11 = bf16[64,1920]{1,0:T(8,128)(2,1)S(1)} collective-permute-done((bf16[64,1920]{1,0:T(8,128)(2,1)S(1)}, bf16[64,1920]{1,0:T(8,128)(2,1)S(1)}, u32[]{:S(2)}, u32[]{:S(2)}) %collective-permute-start.11) | collective-permute-done | bytes 245792 | tf_op jit(solution)/shard_map/ppermute | solution.py:49
  54.9 1.4 collective-permute-done.9
  56.3 0.1 add_convert_fusion.2
  56.4 0.5 collective-permute-start.12
  56.9 2.1 %collective-permute-start.13 = (bf16[64,1920]{1,0:T(8,128)(2,1)S(1)}, bf16[64,1920]{1,0:T(8,128)(2,1)S(1)}, u32[]{:S(2)}, u32[]{:S(2)}) collective-permute-start(bf16[64,1920]{1,0:T(8,128)(2,1)S(1)} %add_convert_fusion.2), channel_id=1, source_target_pairs={{0,2},{1,3},{2,0},{3,1},{4,6},{5,7},{6,4},{7,5},{8,10},{9,11},{10,... | collective-permute-start | bytes 737288 | tf_op jit(solution)/shard_map/ppermute | solution.py:49
  59.0 1.6 %collective-permute-start.14 = (bf16[64,1920]{1,0:T(8,128)(2,1)S(1)}, bf16[64,1920]{1,0:T(8,128)(2,1)S(1)}, u32[]{:S(2)}, u32[]{:S(2)}) collective-permute-start(bf16[64,1920]{1,0:T(8,128)(2,1)S(1)} %add_convert_fusion.2), channel_id=1, source_target_pairs={{0,3},{1,0},{2,1},{3,2},{4,7},{5,4},{6,5},{7,6},{8,11},{9,8},{10,9... | collective-permute-start | bytes 737288 | tf_op jit(solution)/shard_map/ppermute | solution.py:49
  60.6 5.9 %collective-permute-done.12 = bf16[64,1920]{1,0:T(8,128)(2,1)S(1)} collective-permute-done((bf16[64,1920]{1,0:T(8,128)(2,1)S(1)}, bf16[64,1920]{1,0:T(8,128)(2,1)S(1)}, u32[]{:S(2)}, u32[]{:S(2)}) %collective-permute-start.12) | collective-permute-done | bytes 245792 | tf_op jit(solution)/shard_map/ppermute | solution.py:49
  66.5 0.0 collective-permute-done.13
  66.5 0.9 collective-permute-done.14
  67.4 0.1 add_convert_fusion.1.s0
  67.5 1.2 collective-permute-start.15
  68.7 2.8 %collective-permute-start.16 = (bf16[64,1920]{1,0:T(8,128)(2,1)S(1)}, bf16[64,1920]{1,0:T(8,128)(2,1)S(1)}, u32[]{:S(2)}, u32[]{:S(2)}) collective-permute-start(bf16[64,1920]{1,0:T(8,128)(2,1)S(1)} %add_convert_fusion.1.s0), channel_id=1, source_target_pairs={{0,8},{4,12},{8,0},{12,4},{1,9},{5,13},{9,1},{13,5},{2,10},{6,14},... | collective-permute-start | bytes 737288 | tf_op jit(solution)/shard_map/ppermute | solution.py:49
  71.5 0.7 collective-permute-start.17
  72.2 2.8 %collective-permute-done.15.s1 = bf16[64,1920]{1,0:T(8,128)(2,1)S(1)} collective-permute-done((bf16[64,1920]{1,0:T(8,128)(2,1)S(1)}, bf16[64,1920]{1,0:T(8,128)(2,1)S(1)}, u32[]{:S(2)}, u32[]{:S(2)}) %collective-permute-start.15) | collective-permute-done | bytes 245792 | tf_op jit(solution)/shard_map/ppermute | solution.py:49
  75.0 3.4 %collective-permute-done.16.s2 = bf16[64,1920]{1,0:T(8,128)(2,1)S(1)} collective-permute-done((bf16[64,1920]{1,0:T(8,128)(2,1)S(1)}, bf16[64,1920]{1,0:T(8,128)(2,1)S(1)}, u32[]{:S(2)}, u32[]{:S(2)}) %collective-permute-start.16) | collective-permute-done | bytes 245792 | tf_op jit(solution)/shard_map/ppermute | solution.py:49
  78.3 0.1 collective-permute-done.17.s3
  78.5 1.0 shard_map.122
  79.5 0.1 collective-permute-start.18
  79.6 3.2 %collective-permute-start.19 = (bf16[64,7296]{1,0:T(8,128)(2,1)S(1)}, bf16[64,7296]{1,0:T(8,128)(2,1)S(1)}, u32[]{:S(2)}, u32[]{:S(2)}) collective-permute-start(bf16[64,7296]{1,0:T(8,128)(2,1)S(1)} %get-tuple-element.44.x), channel_id=1, source_target_pairs={{0,48},{16,0},{32,16},{48,32},{4,52},{20,4},{36,20},{52,36},{8,56}... | collective-permute-start | bytes 2801672 | tf_op jit(solution)/shard_map/ppermute | solution.py:49
  82.8 9.1 %shard_map.123 = (bf16[64,7168]{1,0:T(8,128)(2,1)S(1)}, bf16[1,7168,256]{2,1,0:T(8,128)(2,1)S(1)}, bf16[1,7168,256]{2,1,0:T(8,128)(2,1)S(1)}, bf16[1,7168,256]{2...) custom-call(s32[8]{0:T(128)S(1)} %copy-done.1, ...), custom_call_target="tpu_custom_call" | custom-call | flops 1409286144 | bytes 45891616 | tf_op jit(solution)/shard_map/pallas_call | solution.py:68
  91.9 2.4 %collective-permute-done.18.refs_0_.refs_2_ = bf16[64,7296]{1,0:T(8,128)(2,1)S(1)} collective-permute-done((bf16[64,7296]{1,0:T(8,128)(2,1)S(1)}, bf16[64,7296]{1,0:T(8,128)(2,1)S(1)}, u32[]{:S(2)}, u32[]{:S(2)}) %collective-permute-start.18) | collective-permute-done | bytes 933920 | tf_op jit(solution)/shard_map/ppermute | solution.py:49
  94.4 0.0 collective-permute-done.19.refs_1_.refs_3_
  94.4 0.6 collective-permute-start.22
  95.0 2.8 %collective-permute-start.23 = (bf16[32,7296]{1,0:T(8,128)(2,1)S(1)}, bf16[32,7296]{1,0:T(8,128)(2,1)S(1)}, u32[]{:S(2)}, u32[]{:S(2)}) collective-permute-start(bf16[32,7296]{1,0:T(8,128)(2,1)S(1)} %slice.7), channel_id=1, source_target_pairs={{0,48},{16,0},{32,16},{48,32},{4,52},{20,4},{36,20},{52,36},{8,56}... | collective-permute-start | bytes 1400840 | tf_op jit(solution)/shard_map/ppermute | solution.py:49
  97.8 5.7 %shard_map.124 = (bf16[64,7168]{1,0:T(8,128)(2,1)S(1)}, bf16[64,7168]{1,0:T(8,128)(2,1)S(1)}) custom-call(s32[8]{0:T(128)S(1)} %copy-done.1, bf16[64,7296]{1,0:T(8,128)(2,1)S(1)} %collective-permute-done.18.refs_0_.refs_2_, bf16[64,7296]{1,0:T(8,128)(2,1)S(1)} %collective-permute-done.19.refs_1_.refs_3_, ...), custom_call_target="tpu_custom_call" | custom-call | flops 2818572288 | bytes 27590688 | tf_op jit(solution)/shard_map/pallas_call | solution.py:68
  103.5 2.1 %collective-permute-start.20 = (bf16[64,7168]{1,0:T(8,128)(2,1)S(1)}, bf16[64,7168]{1,0:T(8,128)(2,1)S(1)}, u32[]{:S(2)}, u32[]{:S(2)}) collective-permute-start(bf16[64,7168]{1,0:T(8,128)(2,1)S(1)} %get-tuple-element.61), channel_id=1, source_target_pairs={{0,48},{16,0},{32,16},{48,32},{4,52},{20,4},{36,20},{52,36},{8,56}... | collective-permute-start | bytes 2752520 | tf_op jit(solution)/shard_map/ppermute | solution.py:49
  105.6 0.0 collective-permute-start.21
  105.6 0.0 collective-permute-done.22.refs_0_.refs_2_
  105.6 0.0 collective-permute-done.23.refs_1_.refs_3_
  105.6 6.2 %shard_map.125 = bf16[64,7168]{1,0:T(8,128)(2,1)S(1)} custom-call(s32[8]{0:T(128)S(1)} %copy-done.1, bf16[32,7296]{1,0:T(8,128)(2,1)S(1)} %collective-permute-done.22.refs_0_.refs_2_, bf16[32,7296]{1,0:T(8,128)(2,1)S(1)} %collective-permute-done.23.refs_1_.refs_3_, bf16[32,7296]{1,0:T(8,128)(2,1)S(1)} %collective-permute-done.22.refs_0_.refs_2_, ...), custom_call_target="tpu_custom_call" | custom-call | flops 1409286144 | bytes 24805408 | tf_op jit(solution)/shard_map/pallas_call | solution.py:68
  111.8 2.2 %collective-permute-start.24 = (bf16[64,7168]{1,0:T(8,128)(2,1)S(1)}, bf16[64,7168]{1,0:T(8,128)(2,1)S(1)}, u32[]{:S(2)}, u32[]{:S(2)}) collective-permute-start(bf16[64,7168]{1,0:T(8,128)(2,1)S(1)} %shard_map.125), channel_id=1, source_target_pairs={{0,32},{16,48},{32,0},{48,16},{4,36},{20,52},{36,4},{52,20},{8,40}... | collective-permute-start | bytes 2752520 | tf_op jit(solution)/shard_map/ppermute | solution.py:49
  114.1 2.9 %collective-permute-done.20 = bf16[64,7168]{1,0:T(8,128)(2,1)S(1)} collective-permute-done((bf16[64,7168]{1,0:T(8,128)(2,1)S(1)}, bf16[64,7168]{1,0:T(8,128)(2,1)S(1)}, u32[]{:S(2)}, u32[]{:S(2)}) %collective-permute-start.20) | collective-permute-done | bytes 917536 | tf_op jit(solution)/shard_map/ppermute | solution.py:49
  117.0 13.1 %collective-permute-done.21 = bf16[64,7168]{1,0:T(8,128)(2,1)S(1)} collective-permute-done((bf16[64,7168]{1,0:T(8,128)(2,1)S(1)}, bf16[64,7168]{1,0:T(8,128)(2,1)S(1)}, u32[]{:S(2)}, u32[]{:S(2)}) %collective-permute-start.21) | collective-permute-done | bytes 917536 | tf_op jit(solution)/shard_map/ppermute | solution.py:49
  130.0 0.0 collective-permute-done.24
  130.0 0.5 add_convert_fusion
  130.5 1.3 reshape.18
  131.8 6.1 %all-to-all-start.1 = ((bf16[16,4,7168]{2,1,0:T(4,128)(2,1)}), bf16[16,4,7168]{2,1,0:T(4,128)(2,1)S(1)}, u32[]{:S(2)}, u32[]{:S(2)}) async-start(bf16[16,4,7168]{2,1,0:T(4,128)(2,1)} %reshape.18), calls=%async_computation.1 | async-start | bytes 1835008 | tf_op jit(solution)/shard_map/all_to_all | solution.py:524
  137.9 12.2 %all-to-all-done.1 = bf16[16,4,7168]{2,1,0:T(4,128)(2,1)S(1)} async-done(((bf16[16,4,7168]{2,1,0:T(4,128)(2,1)}), bf16[16,4,7168]{2,1,0:T(4,128)(2,1)S(1)}, u32[]{:S(2)}, u32[]{:S(2)}) %all-to-all-start.1) | async-done | bytes 917536 | tf_op jit(solution)/shard_map/all_to_all | solution.py:524
  150.1 0.4 convert_reduce_fusion
  150.5 0.7 add_convert_fusion.3
  (13 shorter events, 0.1 us)
Async XLA Ops:
  0.0 9.2 %collective-permute-start = (bf16[1,7168,256]{2,1,0:T(8,128)(2,1)}, bf16[1,7168,256]{2,1,0:T(8,128)(2,1)}, u32[]{:S(2)}, u32[]{:S(2)}) collective-permute-start(bf16[1,7168,256]{2,1,0:T(8,128)(2,1)} %refs_0_), channel_id=1, source_target_pairs={{0,64},{64,0},{1,65},{65,1},{2,66},{66,2},{3,67},{67,3},{4,68},{68... | collective-permute-start | bytes 11010056 | tf_op jit(solution)/shard_map/ppermute | solution.py:58
  0.0 34.4 %collective-permute-start.1 = (bf16[1,7168,256]{2,1,0:T(8,128)(2,1)}, bf16[1,7168,256]{2,1,0:T(8,128)(2,1)}, u32[]{:S(2)}, u32[]{:S(2)}) collective-permute-start(bf16[1,7168,256]{2,1,0:T(8,128)(2,1)} %refs_2_), channel_id=1, source_target_pairs={{0,64},{64,0},{1,65},{65,1},{2,66},{66,2},{3,67},{67,3},{4,68},{68... | collective-permute-start | bytes 11010056 | tf_op jit(solution)/shard_map/ppermute | solution.py:58
  0.5 33.9 %collective-permute-start.2 = (bf16[1,256,7168]{2,1,0:T(8,128)(2,1)}, bf16[1,256,7168]{2,1,0:T(8,128)(2,1)}, u32[]{:S(2)}, u32[]{:S(2)}) collective-permute-start(bf16[1,256,7168]{2,1,0:T(8,128)(2,1)} %refs_4_), channel_id=1, source_target_pairs={{0,64},{64,0},{1,65},{65,1},{2,66},{66,2},{3,67},{67,3},{4,68},{68... | collective-permute-start | bytes 11010056 | tf_op jit(solution)/shard_map/ppermute | solution.py:58
  4.7 29.7 %collective-permute-start.3 = (bf16[144,2304]{1,0:T(8,128)(2,1)}, bf16[144,2304]{1,0:T(8,128)(2,1)S(1)}, u32[]{:S(2)}, u32[]{:S(2)}) collective-permute-start(bf16[144,2304]{1,0:T(8,128)(2,1)} %get-tuple-element.36), channel_id=1, source_target_pairs={{0,4},{4,8},{8,12},{12,0},{1,5},{5,9},{9,13},{13,1},{2,6},{6,10},{... | collective-permute-start | bytes 1990664 | tf_op jit(solution)/shard_map/ppermute | solution.py:49
  6.3 28.1 %collective-permute-start.4 = (bf16[144,2304]{1,0:T(8,128)(2,1)}, bf16[144,2304]{1,0:T(8,128)(2,1)S(1)}, u32[]{:S(2)}, u32[]{:S(2)}) collective-permute-start(bf16[144,2304]{1,0:T(8,128)(2,1)} %get-tuple-element.37), channel_id=1, source_target_pairs={{0,8},{4,12},{8,0},{12,4},{1,9},{5,13},{9,1},{13,5},{2,10},{6,14},... | collective-permute-start | bytes 1990664 | tf_op jit(solution)/shard_map/ppermute | solution.py:49
  9.2 25.2 %collective-permute-start.5 = (bf16[144,2304]{1,0:T(8,128)(2,1)}, bf16[144,2304]{1,0:T(8,128)(2,1)S(1)}, u32[]{:S(2)}, u32[]{:S(2)}) collective-permute-start(bf16[144,2304]{1,0:T(8,128)(2,1)} %get-tuple-element.38), channel_id=1, source_target_pairs={{0,12},{4,0},{8,4},{12,8},{1,13},{5,1},{9,5},{13,9},{2,14},{6,2},{... | collective-permute-start | bytes 1990664 | tf_op jit(solution)/shard_map/ppermute | solution.py:49
  10.6 23.9 %copy-start = (bf16[144,2304]{1,0:T(8,128)(2,1)S(1)}, bf16[144,2304]{1,0:T(8,128)(2,1)}, u32[]{:S(2)}) copy-start(bf16[144,2304]{1,0:T(8,128)(2,1)} %get-tuple-element.35.w0.p0) | copy-start | bytes 1990660
  10.6 23.9 %copy-start.1 = (s32[8]{0:T(128)S(1)}, s32[8]{0:T(128)}, u32[]{:S(2)}) copy-start(s32[8]{0:T(128)} %stack.29.at) | copy-start | bytes 100
  34.4 37.8 %copy-start.2 = (bf16[7168]{0:T(1024)(128)(2,1)S(1)}, bf16[7168]{0:T(1024)(128)(2,1)}, u32[]{:S(2)}) copy-start(bf16[7168]{0:T(1024)(128)(2,1)} %param.18) | copy-start | bytes 43012
  36.2 5.5 %collective-permute-start.6 = (bf16[4,64,128]{2,1,0:T(8,128)(2,1)S(1)}, bf16[4,64,128]{2,1,0:T(8,128)(2,1)S(1)}, u32[]{:S(2)}, u32[]{:S(2)}) collective-permute-start(bf16[4,64,128]{2,1,0:T(8,128)(2,1)S(1)} %shard_map.120.h0), channel_id=1, source_target_pairs={{0,4},{4,8},{8,12},{12,0},{1,5},{5,9},{9,13},{13,1},{2,6},{6,10},{... | collective-permute-start | bytes 196616 | tf_op jit(solution)/shard_map/ppermute | solution.py:49
  37.7 5.8 %collective-permute-start.7 = (bf16[4,64,128]{2,1,0:T(8,128)(2,1)S(1)}, bf16[4,64,128]{2,1,0:T(8,128)(2,1)S(1)}, u32[]{:S(2)}, u32[]{:S(2)}) collective-permute-start(bf16[4,64,128]{2,1,0:T(8,128)(2,1)S(1)} %shard_map.120.h0), channel_id=1, source_target_pairs={{0,8},{4,12},{8,0},{12,4},{1,9},{5,13},{9,1},{13,5},{2,10},{6,14},... | collective-permute-start | bytes 196616 | tf_op jit(solution)/shard_map/ppermute | solution.py:49
  38.1 5.3 %collective-permute-start.8 = (bf16[4,64,128]{2,1,0:T(8,128)(2,1)S(1)}, bf16[4,64,128]{2,1,0:T(8,128)(2,1)S(1)}, u32[]{:S(2)}, u32[]{:S(2)}) collective-permute-start(bf16[4,64,128]{2,1,0:T(8,128)(2,1)S(1)} %shard_map.120.h0), channel_id=1, source_target_pairs={{0,12},{4,0},{8,4},{12,8},{1,13},{5,1},{9,5},{13,9},{2,14},{6,2},{... | collective-permute-start | bytes 196616 | tf_op jit(solution)/shard_map/ppermute | solution.py:49
  45.2 7.5 %collective-permute-start.10 = (bf16[64,1920]{1,0:T(8,128)(2,1)S(1)}, bf16[64,1920]{1,0:T(8,128)(2,1)S(1)}, u32[]{:S(2)}, u32[]{:S(2)}) collective-permute-start(bf16[64,1920]{1,0:T(8,128)(2,1)S(1)} %get-tuple-element.41), channel_id=1, source_target_pairs={{0,16},{16,32},{32,48},{48,0},{4,20},{20,36},{36,52},{52,4},{8,24}... | collective-permute-start | bytes 737288 | tf_op jit(solution)/shard_map/ppermute | solution.py:49
  45.6 9.3 %collective-permute-start.11 = (bf16[64,1920]{1,0:T(8,128)(2,1)S(1)}, bf16[64,1920]{1,0:T(8,128)(2,1)S(1)}, u32[]{:S(2)}, u32[]{:S(2)}) collective-permute-start(bf16[64,1920]{1,0:T(8,128)(2,1)S(1)} %get-tuple-element.42), channel_id=1, source_target_pairs={{0,48},{16,0},{32,16},{48,32},{4,52},{20,4},{36,20},{52,36},{8,56}... | collective-permute-start | bytes 737288 | tf_op jit(solution)/shard_map/ppermute | solution.py:49
  48.6 7.7 %collective-permute-start.9 = (bf16[64,1920]{1,0:T(8,128)(2,1)S(1)}, bf16[64,1920]{1,0:T(8,128)(2,1)S(1)}, u32[]{:S(2)}, u32[]{:S(2)}) collective-permute-start(bf16[64,1920]{1,0:T(8,128)(2,1)S(1)} %get-tuple-element.40), channel_id=1, source_target_pairs={{0,32},{16,48},{32,0},{48,16},{4,36},{20,52},{36,4},{52,20},{8,40}... | collective-permute-start | bytes 737288 | tf_op jit(solution)/shard_map/ppermute | solution.py:49
  56.4 10.1 %collective-permute-start.12 = (bf16[64,1920]{1,0:T(8,128)(2,1)S(1)}, bf16[64,1920]{1,0:T(8,128)(2,1)S(1)}, u32[]{:S(2)}, u32[]{:S(2)}) collective-permute-start(bf16[64,1920]{1,0:T(8,128)(2,1)S(1)} %add_convert_fusion.2), channel_id=1, source_target_pairs={{0,1},{1,2},{2,3},{3,0},{4,5},{5,6},{6,7},{7,4},{8,9},{9,10},{10,1... | collective-permute-start | bytes 737288 | tf_op jit(solution)/shard_map/ppermute | solution.py:49
  56.9 9.6 %collective-permute-start.13 = (bf16[64,1920]{1,0:T(8,128)(2,1)S(1)}, bf16[64,1920]{1,0:T(8,128)(2,1)S(1)}, u32[]{:S(2)}, u32[]{:S(2)}) collective-permute-start(bf16[64,1920]{1,0:T(8,128)(2,1)S(1)} %add_convert_fusion.2), channel_id=1, source_target_pairs={{0,2},{1,3},{2,0},{3,1},{4,6},{5,7},{6,4},{7,5},{8,10},{9,11},{10,... | collective-permute-start | bytes 737288 | tf_op jit(solution)/shard_map/ppermute | solution.py:49
  59.0 8.4 %collective-permute-start.14 = (bf16[64,1920]{1,0:T(8,128)(2,1)S(1)}, bf16[64,1920]{1,0:T(8,128)(2,1)S(1)}, u32[]{:S(2)}, u32[]{:S(2)}) collective-permute-start(bf16[64,1920]{1,0:T(8,128)(2,1)S(1)} %add_convert_fusion.2), channel_id=1, source_target_pairs={{0,3},{1,0},{2,1},{3,2},{4,7},{5,4},{6,5},{7,6},{8,11},{9,8},{10,9... | collective-permute-start | bytes 737288 | tf_op jit(solution)/shard_map/ppermute | solution.py:49
  67.5 7.5 %collective-permute-start.15 = (bf16[64,1920]{1,0:T(8,128)(2,1)S(1)}, bf16[64,1920]{1,0:T(8,128)(2,1)S(1)}, u32[]{:S(2)}, u32[]{:S(2)}) collective-permute-start(bf16[64,1920]{1,0:T(8,128)(2,1)S(1)} %add_convert_fusion.1.s0), channel_id=1, source_target_pairs={{0,4},{4,8},{8,12},{12,0},{1,5},{5,9},{9,13},{13,1},{2,6},{6,10},{... | collective-permute-start | bytes 737288 | tf_op jit(solution)/shard_map/ppermute | solution.py:49
  68.7 9.6 %collective-permute-start.16 = (bf16[64,1920]{1,0:T(8,128)(2,1)S(1)}, bf16[64,1920]{1,0:T(8,128)(2,1)S(1)}, u32[]{:S(2)}, u32[]{:S(2)}) collective-permute-start(bf16[64,1920]{1,0:T(8,128)(2,1)S(1)} %add_convert_fusion.1.s0), channel_id=1, source_target_pairs={{0,8},{4,12},{8,0},{12,4},{1,9},{5,13},{9,1},{13,5},{2,10},{6,14},... | collective-permute-start | bytes 737288 | tf_op jit(solution)/shard_map/ppermute | solution.py:49
  71.5 6.9 %collective-permute-start.17 = (bf16[64,1920]{1,0:T(8,128)(2,1)S(1)}, bf16[64,1920]{1,0:T(8,128)(2,1)S(1)}, u32[]{:S(2)}, u32[]{:S(2)}) collective-permute-start(bf16[64,1920]{1,0:T(8,128)(2,1)S(1)} %add_convert_fusion.1.s0), channel_id=1, source_target_pairs={{0,12},{4,0},{8,4},{12,8},{1,13},{5,1},{9,5},{13,9},{2,14},{6,2},{... | collective-permute-start | bytes 737288 | tf_op jit(solution)/shard_map/ppermute | solution.py:49
  79.5 14.8 %collective-permute-start.18 = (bf16[64,7296]{1,0:T(8,128)(2,1)S(1)}, bf16[64,7296]{1,0:T(8,128)(2,1)S(1)}, u32[]{:S(2)}, u32[]{:S(2)}) collective-permute-start(bf16[64,7296]{1,0:T(8,128)(2,1)S(1)} %get-tuple-element.44.x), channel_id=1, source_target_pairs={{0,16},{16,32},{32,48},{48,0},{4,20},{20,36},{36,52},{52,4},{8,24}... | collective-permute-start | bytes 2801672 | tf_op jit(solution)/shard_map/ppermute | solution.py:49
  79.6 14.8 %collective-permute-start.19 = (bf16[64,7296]{1,0:T(8,128)(2,1)S(1)}, bf16[64,7296]{1,0:T(8,128)(2,1)S(1)}, u32[]{:S(2)}, u32[]{:S(2)}) collective-permute-start(bf16[64,7296]{1,0:T(8,128)(2,1)S(1)} %get-tuple-element.44.x), channel_id=1, source_target_pairs={{0,48},{16,0},{32,16},{48,32},{4,52},{20,4},{36,20},{52,36},{8,56}... | collective-permute-start | bytes 2801672 | tf_op jit(solution)/shard_map/ppermute | solution.py:49
  94.4 11.2 %collective-permute-start.22 = (bf16[32,7296]{1,0:T(8,128)(2,1)S(1)}, bf16[32,7296]{1,0:T(8,128)(2,1)S(1)}, u32[]{:S(2)}, u32[]{:S(2)}) collective-permute-start(bf16[32,7296]{1,0:T(8,128)(2,1)S(1)} %slice.6), channel_id=1, source_target_pairs={{0,16},{16,32},{32,48},{48,0},{4,20},{20,36},{36,52},{52,4},{8,24}... | collective-permute-start | bytes 1400840 | tf_op jit(solution)/shard_map/ppermute | solution.py:49
  95.0 10.6 %collective-permute-start.23 = (bf16[32,7296]{1,0:T(8,128)(2,1)S(1)}, bf16[32,7296]{1,0:T(8,128)(2,1)S(1)}, u32[]{:S(2)}, u32[]{:S(2)}) collective-permute-start(bf16[32,7296]{1,0:T(8,128)(2,1)S(1)} %slice.7), channel_id=1, source_target_pairs={{0,48},{16,0},{32,16},{48,32},{4,52},{20,4},{36,20},{52,36},{8,56}... | collective-permute-start | bytes 1400840 | tf_op jit(solution)/shard_map/ppermute | solution.py:49
  103.5 13.5 %collective-permute-start.20 = (bf16[64,7168]{1,0:T(8,128)(2,1)S(1)}, bf16[64,7168]{1,0:T(8,128)(2,1)S(1)}, u32[]{:S(2)}, u32[]{:S(2)}) collective-permute-start(bf16[64,7168]{1,0:T(8,128)(2,1)S(1)} %get-tuple-element.61), channel_id=1, source_target_pairs={{0,48},{16,0},{32,16},{48,32},{4,52},{20,4},{36,20},{52,36},{8,56}... | collective-permute-start | bytes 2752520 | tf_op jit(solution)/shard_map/ppermute | solution.py:49
  105.6 24.4 %collective-permute-start.21 = (bf16[64,7168]{1,0:T(8,128)(2,1)S(1)}, bf16[64,7168]{1,0:T(8,128)(2,1)S(1)}, u32[]{:S(2)}, u32[]{:S(2)}) collective-permute-start(bf16[64,7168]{1,0:T(8,128)(2,1)S(1)} %get-tuple-element.62), channel_id=1, source_target_pairs={{0,16},{16,32},{32,48},{48,0},{4,20},{20,36},{36,52},{52,4},{8,24}... | collective-permute-start | bytes 2752520 | tf_op jit(solution)/shard_map/ppermute | solution.py:49
  111.8 18.2 %collective-permute-start.24 = (bf16[64,7168]{1,0:T(8,128)(2,1)S(1)}, bf16[64,7168]{1,0:T(8,128)(2,1)S(1)}, u32[]{:S(2)}, u32[]{:S(2)}) collective-permute-start(bf16[64,7168]{1,0:T(8,128)(2,1)S(1)} %shard_map.125), channel_id=1, source_target_pairs={{0,32},{16,48},{32,0},{48,16},{4,36},{20,52},{36,4},{52,20},{8,40}... | collective-permute-start | bytes 2752520 | tf_op jit(solution)/shard_map/ppermute | solution.py:49
  131.8 18.3 %all-to-all-start.1 = ((bf16[16,4,7168]{2,1,0:T(4,128)(2,1)}), bf16[16,4,7168]{2,1,0:T(4,128)(2,1)S(1)}, u32[]{:S(2)}, u32[]{:S(2)}) async-start(bf16[16,4,7168]{2,1,0:T(4,128)(2,1)} %reshape.18), calls=%async_computation.1 | async-start | bytes 1835008 | tf_op jit(solution)/shard_map/all_to_all | solution.py:524

commit v6 on v5

--- a/solution.py
+++ b/solution.py
@@ -425,6 +425,15 @@
     return out, held[0:2], held[2:4], held[4:6]
 
 
+def sum_kernel(at, p0, p1, p2, p3, out):
+    rows = out.shape[1]
+    for i in range(p0.shape[0] // GROUP):
+        span = slice(i * GROUP, (i + 1) * GROUP)
+        total = sum(p[span, :].astype(f32) for p in (p0, p1, p2, p3))
+        for j in range(GROUP // rows):
+            out[i * (GROUP // rows) + j] = total[j * rows : (j + 1) * rows].astype(bf16)
+
+
 def on_device(
     queries,
     latent_cache,
@@ -520,7 +529,9 @@
     near_sums = experts(at, near, gates, ups, downs, 2)
     (far_sum,) = experts(at, far, gates, ups, downs, 1)
     sums = [shift(near_sums[0], "a", -1), shift(near_sums[1], "a", -3), shift(far_sum, "a", -2)]
-    last = added([own_sum] + sums).reshape(16, rows, width)
+    last = call(
+        sum_kernel, jax.ShapeDtypeStruct((16, rows, width), bf16), (at, own_sum, *sums), 0, 16
+    )
     last = lax.all_to_all(last, AXES, 0, 0, axis_index_groups=groups("cb"), tiled=True)
     combined = jnp.sum(last.astype(f32), axis=0)
     mine = lax.dynamic_slice_in_dim(mine, b * rows, rows, 0)

time: 153 us -> 151 us (0.987); the launches traced: 151 us -> 151 us
  Pallas kernels: 35.6 us -> 37.6 us
    pallas_call x8 -> x9, Pallas kernels: 35.6 us -> 37.6 us  [call(): pl.pallas_call(body, out_shape=out_shape, compiler_params=pltpu.CompilerP...]
  transfers between devices with their start and end apart: 26 -> 26, of which waited for: 14 -> 15; matrix products, arithmetic and copies ran while one was open for 0% -> 0% of each run, Pallas kernels for 21% -> 21%
where the time goes in v6:
time: 151 us
  waiting for transfers between devices  55.4 us (37%)
  starting transfers between devices  38.9 us (26%)
  Pallas kernels  37.6 us (25%)
  blocking collectives  16.9 us (11%)
    ppermute x22, waiting for transfers between devices, shift(): return lax.ppermute(value, AXES, pairs)  43.2 us
    pallas_call x9, Pallas kernels, call(): pl.pallas_call(body, out_shape=out_shape, compiler_params=pltpu.CompilerP...  37.6 us
    ppermute x22, starting transfers between devices, shift(): return lax.ppermute(value, AXES, pairs)  32.3 us
    all_to_all x1, blocking collectives, on_device(): lax.all_to_all(sent, AXES, 0, 0, axis_index_groups=groups('ab'), tiled=True)  16.9 us
    all_to_all x1, waiting for transfers between devices, on_device(): lax.all_to_all(last, AXES, 0, 0, axis_index_groups=groups('cb'), tiled=True)  12.2 us
    all_to_all x1, starting transfers between devices, on_device(): lax.all_to_all(last, AXES, 0, 0, axis_index_groups=groups('cb'), tiled=True)  6.08 us
  transfers between devices with their start and end apart: 26, of which 15 were waited for; matrix products, arithmetic and copies ran while one was open for 0% of the time, Pallas kernels for 21%

profile of v6, /device:TPU:0, one launch (start us, length us, event | category | flops | bytes accessed | tf_op | source)
XLA Modules:
  0.0 150.9 jit_solution(14105349645134138927)
XLA Ops:
  0.0 0.0 collective-permute-start
  0.0 0.5 collective-permute-start.1
  0.5 0.0 collective-permute-start.2
  0.5 0.7 stack.29.at
  1.2 3.5 %shard_map.119 = (bf16[144,2304]{1,0:T(8,128)(2,1)}, bf16[144,2304]{1,0:T(8,128)(2,1)}, bf16[144,2304]{1,0:T(8,128)(2,1)}, bf16[144,2304]{1,0:T(8,128)(2,1)}) custom-call(s32[8]{0:T(128)} %stack.29.at, bf16[128,7168]{1,0:T(8,128)(2,1)} %w_out.1, bf16[1,512,128]{2,1,0:T(8,128)(2,1)} %w_uv.1, bf16[4,7168]{1,0:T(4,128)(2,1)} %residual.1, s32[4,8]{1,0:T(4,128)} %ids.1, ...), custom_call_target="tpu_custom_call" | custom-call | tf_op jit(solution)/shard_map/pallas_call | solution.py:68
  4.7 1.7 %collective-permute-start.3 = (bf16[144,2304]{1,0:T(8,128)(2,1)}, bf16[144,2304]{1,0:T(8,128)(2,1)S(1)}, u32[]{:S(2)}, u32[]{:S(2)}) collective-permute-start(bf16[144,2304]{1,0:T(8,128)(2,1)} %get-tuple-element.36), channel_id=1, source_target_pairs={{0,4},{4,8},{8,12},{12,0},{1,5},{5,9},{9,13},{13,1},{2,6},{6,10},{... | collective-permute-start | bytes 1990664 | tf_op jit(solution)/shard_map/ppermute | solution.py:49
  6.3 2.9 %collective-permute-start.4 = (bf16[144,2304]{1,0:T(8,128)(2,1)}, bf16[144,2304]{1,0:T(8,128)(2,1)S(1)}, u32[]{:S(2)}, u32[]{:S(2)}) collective-permute-start(bf16[144,2304]{1,0:T(8,128)(2,1)} %get-tuple-element.37), channel_id=1, source_target_pairs={{0,8},{4,12},{8,0},{12,4},{1,9},{5,13},{9,1},{13,5},{2,10},{6,14},... | collective-permute-start | bytes 1990664 | tf_op jit(solution)/shard_map/ppermute | solution.py:49
  9.2 0.0 collective-permute-done.refs_1_
  9.2 1.4 collective-permute-start.5
  10.6 6.6 %shard_map.118 = bf16[256,512]{1,0:T(8,128)(2,1)} custom-call(s32[4]{0:T(128)} %lengths.1, s32[8]{0:T(128)} %stack.29.at, bf16[4,64,576]{2,1,0:T(8,128)(2,1)} %query.1, bf16[4,576,2048]{2,1,0:T(8,128)(2,1)} %bitcast.12), custom_call_target="tpu_custom_call" | custom-call | flops 1140850688 | bytes 9994288 | tf_op jit(solution)/shard_map/pallas_call | solution.py:68
  17.2 16.9 %all_to_all.10 = bf16[16,16,512]{2,1,0:T(8,128)(2,1)S(1)} all-to-all(bf16[16,16,512]{2,1,0:T(8,128)(2,1)} %bitcast.13), channel_id=1, replica_groups={{0,1,2,3,16,17,18,19,32,33,34,35,48,49,50,51},{4,5,6,7,20,21,22,23,36,3..., dimensions={0} | all-to-all | bytes 524288 | tf_op jit(solution)/shard_map/all_to_all | solution.py:482
  34.1 0.0 collective-permute-done.4.w2.p2
  34.2 0.0 copy-start.2
  34.2 1.8 %shard_map.120.h0 = bf16[4,64,128]{2,1,0:T(8,128)(2,1)S(1)} custom-call(s32[8]{0:T(128)S(1)} %copy-done.1, bf16[256,512]{1,0:T(8,128)(2,1)S(1)} %bitcast.10, bf16[144,2304]{1,0:T(8,128)(2,1)S(1)} %copy-done, bf16[144,2304]{1,0:T(8,128)(2,1)S(1)} %collective-permute-done.3.w1.p1, bf16[144,2304]{1,0:T(8,128)(2,1)S(1)} %collective-permute-done.4.w2.p2, ...), custom_call_target="tpu_custom_call" | custom-call | flops 134217728 | bytes 2981920 | tf_op jit(solution)/shard_map/pallas_call | solution.py:68
  35.9 0.6 collective-permute-start.6
  36.5 1.5 collective-permute-start.7
  38.0 1.3 collective-permute-start.8
  39.3 2.2 %collective-permute-done.6.h1 = bf16[4,64,128]{2,1,0:T(8,128)(2,1)S(1)} collective-permute-done((bf16[4,64,128]{2,1,0:T(8,128)(2,1)S(1)}, bf16[4,64,128]{2,1,0:T(8,128)(2,1)S(1)}, u32[]{:S(2)}, u32[]{:S(2)}) %collective-permute-start.6) | collective-permute-done | bytes 65568 | tf_op jit(solution)/shard_map/ppermute | solution.py:49
  41.5 0.8 collective-permute-done.7.h2
  42.3 0.7 collective-permute-done.8.h3
  43.0 1.7 %shard_map.121 = (bf16[64,1920]{1,0:T(8,128)(2,1)S(1)}, bf16[64,1920]{1,0:T(8,128)(2,1)S(1)}, bf16[64,1920]{1,0:T(8,128)(2,1)S(1)}, bf16[64,1920]{1,0:T(8,128)(2,1)S(1)}) custom-call(s32[8]{0:T(128)S(1)} %copy-done.1, bf16[4,64,128]{2,1,0:T(8,128)(2,1)S(1)} %shard_map.120.h0, bf16[4,64,128]{2,1,0:T(8,128)(2,1)S(1)} %collective-permute-done.6.h1, ...), custom_call_target="tpu_custom_call" | custom-call | flops 469762048 | bytes 3899424 | tf_op jit(solution)/shard_map/pallas_call | solution.py:68
  44.8 0.5 collective-permute-start.10
  45.3 2.8 %collective-permute-start.11 = (bf16[64,1920]{1,0:T(8,128)(2,1)S(1)}, bf16[64,1920]{1,0:T(8,128)(2,1)S(1)}, u32[]{:S(2)}, u32[]{:S(2)}) collective-permute-start(bf16[64,1920]{1,0:T(8,128)(2,1)S(1)} %get-tuple-element.42), channel_id=1, source_target_pairs={{0,48},{16,0},{32,16},{48,32},{4,52},{20,4},{36,20},{52,36},{8,56}... | collective-permute-start | bytes 737288 | tf_op jit(solution)/shard_map/ppermute | solution.py:49
  48.1 0.1 collective-permute-start.9
  48.2 4.0 %collective-permute-done.10 = bf16[64,1920]{1,0:T(8,128)(2,1)S(1)} collective-permute-done((bf16[64,1920]{1,0:T(8,128)(2,1)S(1)}, bf16[64,1920]{1,0:T(8,128)(2,1)S(1)}, u32[]{:S(2)}, u32[]{:S(2)}) %collective-permute-start.10) | collective-permute-done | bytes 245792 | tf_op jit(solution)/shard_map/ppermute | solution.py:49
  52.3 2.2 %collective-permute-done.11 = bf16[64,1920]{1,0:T(8,128)(2,1)S(1)} collective-permute-done((bf16[64,1920]{1,0:T(8,128)(2,1)S(1)}, bf16[64,1920]{1,0:T(8,128)(2,1)S(1)}, u32[]{:S(2)}, u32[]{:S(2)}) %collective-permute-start.11) | collective-permute-done | bytes 245792 | tf_op jit(solution)/shard_map/ppermute | solution.py:49
  54.4 1.4 collective-permute-done.9
  55.8 0.1 add_convert_fusion.1
  55.9 0.5 collective-permute-start.12
  56.4 2.1 %collective-permute-start.13 = (bf16[64,1920]{1,0:T(8,128)(2,1)S(1)}, bf16[64,1920]{1,0:T(8,128)(2,1)S(1)}, u32[]{:S(2)}, u32[]{:S(2)}) collective-permute-start(bf16[64,1920]{1,0:T(8,128)(2,1)S(1)} %add_convert_fusion.1), channel_id=1, source_target_pairs={{0,2},{1,3},{2,0},{3,1},{4,6},{5,7},{6,4},{7,5},{8,10},{9,11},{10,... | collective-permute-start | bytes 737288 | tf_op jit(solution)/shard_map/ppermute | solution.py:49
  58.5 1.6 %collective-permute-start.14 = (bf16[64,1920]{1,0:T(8,128)(2,1)S(1)}, bf16[64,1920]{1,0:T(8,128)(2,1)S(1)}, u32[]{:S(2)}, u32[]{:S(2)}) collective-permute-start(bf16[64,1920]{1,0:T(8,128)(2,1)S(1)} %add_convert_fusion.1), channel_id=1, source_target_pairs={{0,3},{1,0},{2,1},{3,2},{4,7},{5,4},{6,5},{7,6},{8,11},{9,8},{10,9... | collective-permute-start | bytes 737288 | tf_op jit(solution)/shard_map/ppermute | solution.py:49
  60.1 5.9 %collective-permute-done.12 = bf16[64,1920]{1,0:T(8,128)(2,1)S(1)} collective-permute-done((bf16[64,1920]{1,0:T(8,128)(2,1)S(1)}, bf16[64,1920]{1,0:T(8,128)(2,1)S(1)}, u32[]{:S(2)}, u32[]{:S(2)}) %collective-permute-start.12) | collective-permute-done | bytes 245792 | tf_op jit(solution)/shard_map/ppermute | solution.py:49
  66.0 0.0 collective-permute-done.13
  66.0 0.9 collective-permute-done.14
  66.9 0.1 add_convert_fusion.s0
  67.0 1.4 collective-permute-start.15
  68.4 2.6 %collective-permute-start.16 = (bf16[64,1920]{1,0:T(8,128)(2,1)S(1)}, bf16[64,1920]{1,0:T(8,128)(2,1)S(1)}, u32[]{:S(2)}, u32[]{:S(2)}) collective-permute-start(bf16[64,1920]{1,0:T(8,128)(2,1)S(1)} %add_convert_fusion.s0), channel_id=1, source_target_pairs={{0,8},{4,12},{8,0},{12,4},{1,9},{5,13},{9,1},{13,5},{2,10},{6,14},... | collective-permute-start | bytes 737288 | tf_op jit(solution)/shard_map/ppermute | solution.py:49
  71.0 0.4 collective-permute-start.17
  71.4 3.1 %collective-permute-done.15.s1 = bf16[64,1920]{1,0:T(8,128)(2,1)S(1)} collective-permute-done((bf16[64,1920]{1,0:T(8,128)(2,1)S(1)}, bf16[64,1920]{1,0:T(8,128)(2,1)S(1)}, u32[]{:S(2)}, u32[]{:S(2)}) %collective-permute-start.15) | collective-permute-done | bytes 245792 | tf_op jit(solution)/shard_map/ppermute | solution.py:49
  74.5 3.3 %collective-permute-done.16.s2 = bf16[64,1920]{1,0:T(8,128)(2,1)S(1)} collective-permute-done((bf16[64,1920]{1,0:T(8,128)(2,1)S(1)}, bf16[64,1920]{1,0:T(8,128)(2,1)S(1)}, u32[]{:S(2)}, u32[]{:S(2)}) %collective-permute-start.16) | collective-permute-done | bytes 245792 | tf_op jit(solution)/shard_map/ppermute | solution.py:49
  77.8 0.2 collective-permute-done.17.s3
  78.1 1.0 shard_map.122
  79.1 0.1 collective-permute-start.18
  79.2 3.2 %collective-permute-start.19 = (bf16[64,7296]{1,0:T(8,128)(2,1)S(1)}, bf16[64,7296]{1,0:T(8,128)(2,1)S(1)}, u32[]{:S(2)}, u32[]{:S(2)}) collective-permute-start(bf16[64,7296]{1,0:T(8,128)(2,1)S(1)} %get-tuple-element.44.x), channel_id=1, source_target_pairs={{0,48},{16,0},{32,16},{48,32},{4,52},{20,4},{36,20},{52,36},{8,56}... | collective-permute-start | bytes 2801672 | tf_op jit(solution)/shard_map/ppermute | solution.py:49
  82.4 9.1 %shard_map.123 = (bf16[64,7168]{1,0:T(8,128)(2,1)S(1)}, bf16[1,7168,256]{2,1,0:T(8,128)(2,1)S(1)}, bf16[1,7168,256]{2,1,0:T(8,128)(2,1)S(1)}, bf16[1,7168,256]{2...) custom-call(s32[8]{0:T(128)S(1)} %copy-done.1, ...), custom_call_target="tpu_custom_call" | custom-call | flops 1409286144 | bytes 45891616 | tf_op jit(solution)/shard_map/pallas_call | solution.py:68
  91.5 2.4 %collective-permute-done.18.refs_0_.refs_2_ = bf16[64,7296]{1,0:T(8,128)(2,1)S(1)} collective-permute-done((bf16[64,7296]{1,0:T(8,128)(2,1)S(1)}, bf16[64,7296]{1,0:T(8,128)(2,1)S(1)}, u32[]{:S(2)}, u32[]{:S(2)}) %collective-permute-start.18) | collective-permute-done | bytes 933920 | tf_op jit(solution)/shard_map/ppermute | solution.py:49
  93.9 0.0 collective-permute-done.19.refs_1_.refs_3_
  94.0 0.6 collective-permute-start.22
  94.6 2.8 %collective-permute-start.23 = (bf16[32,7296]{1,0:T(8,128)(2,1)S(1)}, bf16[32,7296]{1,0:T(8,128)(2,1)S(1)}, u32[]{:S(2)}, u32[]{:S(2)}) collective-permute-start(bf16[32,7296]{1,0:T(8,128)(2,1)S(1)} %slice.7), channel_id=1, source_target_pairs={{0,48},{16,0},{32,16},{48,32},{4,52},{20,4},{36,20},{52,36},{8,56}... | collective-permute-start | bytes 1400840 | tf_op jit(solution)/shard_map/ppermute | solution.py:49
  97.4 5.7 %shard_map.124 = (bf16[64,7168]{1,0:T(8,128)(2,1)S(1)}, bf16[64,7168]{1,0:T(8,128)(2,1)S(1)}) custom-call(s32[8]{0:T(128)S(1)} %copy-done.1, bf16[64,7296]{1,0:T(8,128)(2,1)S(1)} %collective-permute-done.18.refs_0_.refs_2_, bf16[64,7296]{1,0:T(8,128)(2,1)S(1)} %collective-permute-done.19.refs_1_.refs_3_, ...), custom_call_target="tpu_custom_call" | custom-call | flops 2818572288 | bytes 27590688 | tf_op jit(solution)/shard_map/pallas_call | solution.py:68
  103.1 2.1 %collective-permute-start.20 = (bf16[64,7168]{1,0:T(8,128)(2,1)S(1)}, bf16[64,7168]{1,0:T(8,128)(2,1)S(1)}, u32[]{:S(2)}, u32[]{:S(2)}) collective-permute-start(bf16[64,7168]{1,0:T(8,128)(2,1)S(1)} %get-tuple-element.61), channel_id=1, source_target_pairs={{0,48},{16,0},{32,16},{48,32},{4,52},{20,4},{36,20},{52,36},{8,56}... | collective-permute-start | bytes 2752520 | tf_op jit(solution)/shard_map/ppermute | solution.py:49
  105.2 0.0 collective-permute-start.21
  105.2 0.0 collective-permute-done.22.refs_0_.refs_2_
  105.2 0.0 collective-permute-done.23.refs_1_.refs_3_
  105.2 6.2 %shard_map.125 = bf16[64,7168]{1,0:T(8,128)(2,1)S(1)} custom-call(s32[8]{0:T(128)S(1)} %copy-done.1, bf16[32,7296]{1,0:T(8,128)(2,1)S(1)} %collective-permute-done.22.refs_0_.refs_2_, bf16[32,7296]{1,0:T(8,128)(2,1)S(1)} %collective-permute-done.23.refs_1_.refs_3_, bf16[32,7296]{1,0:T(8,128)(2,1)S(1)} %collective-permute-done.22.refs_0_.refs_2_, ...), custom_call_target="tpu_custom_call" | custom-call | flops 1409286144 | bytes 24805408 | tf_op jit(solution)/shard_map/pallas_call | solution.py:68
  111.4 2.2 %collective-permute-start.24 = (bf16[64,7168]{1,0:T(8,128)(2,1)S(1)}, bf16[64,7168]{1,0:T(8,128)(2,1)S(1)}, u32[]{:S(2)}, u32[]{:S(2)}) collective-permute-start(bf16[64,7168]{1,0:T(8,128)(2,1)S(1)} %shard_map.125), channel_id=1, source_target_pairs={{0,32},{16,48},{32,0},{48,16},{4,36},{20,52},{36,4},{52,20},{8,40}... | collective-permute-start | bytes 2752520 | tf_op jit(solution)/shard_map/ppermute | solution.py:49
  113.6 2.9 %collective-permute-done.20.p1 = bf16[64,7168]{1,0:T(8,128)(2,1)S(1)} collective-permute-done((bf16[64,7168]{1,0:T(8,128)(2,1)S(1)}, bf16[64,7168]{1,0:T(8,128)(2,1)S(1)}, u32[]{:S(2)}, u32[]{:S(2)}) %collective-permute-start.20) | collective-permute-done | bytes 917536 | tf_op jit(solution)/shard_map/ppermute | solution.py:49
  116.6 13.0 %collective-permute-done.21.p2 = bf16[64,7168]{1,0:T(8,128)(2,1)S(1)} collective-permute-done((bf16[64,7168]{1,0:T(8,128)(2,1)S(1)}, bf16[64,7168]{1,0:T(8,128)(2,1)S(1)}, u32[]{:S(2)}, u32[]{:S(2)}) %collective-permute-start.21) | collective-permute-done | bytes 917536 | tf_op jit(solution)/shard_map/ppermute | solution.py:49
  129.6 0.0 collective-permute-done.24.p3
  129.6 2.0 %shard_map.126 = bf16[16,4,7168]{2,1,0:T(4,128)(2,1)} custom-call(s32[8]{0:T(128)S(1)} %copy-done.1, bf16[64,7168]{1,0:T(8,128)(2,1)S(1)} %get-tuple-element.52.p0, bf16[64,7168]{1,0:T(8,128)(2,1)S(1)} %collective-permute-done.20.p1, bf16[64,7168]{1,0:T(8,128)(2,1)S(1)} %collective-permute-done.21.p2, bf16[64,7168]{1,0:T(8,128)(2,1)S(1)} %collective-permute-done.24.p3), custom_call_target="tpu_custom_call" | custom-call | tf_op jit(solution)/shard_map/pallas_call | solution.py:68
  131.6 6.1 %all-to-all-start.1 = ((bf16[16,4,7168]{2,1,0:T(4,128)(2,1)}), bf16[16,4,7168]{2,1,0:T(4,128)(2,1)S(1)}, u32[]{:S(2)}, u32[]{:S(2)}) async-start(bf16[16,4,7168]{2,1,0:T(4,128)(2,1)} %shard_map.126), calls=%async_computation.1 | async-start | bytes 1835008 | tf_op jit(solution)/shard_map/all_to_all | solution.py:535
  137.7 12.2 %all-to-all-done.1 = bf16[16,4,7168]{2,1,0:T(4,128)(2,1)S(1)} async-done(((bf16[16,4,7168]{2,1,0:T(4,128)(2,1)}), bf16[16,4,7168]{2,1,0:T(4,128)(2,1)S(1)}, u32[]{:S(2)}, u32[]{:S(2)}) %all-to-all-start.1) | async-done | bytes 917536 | tf_op jit(solution)/shard_map/all_to_all | solution.py:535
  149.9 0.4 convert_reduce_fusion
  150.3 0.7 add_convert_fusion.2
  (12 shorter events, 0.1 us)
Async XLA Ops:
  0.0 9.2 %collective-permute-start = (bf16[1,7168,256]{2,1,0:T(8,128)(2,1)}, bf16[1,7168,256]{2,1,0:T(8,128)(2,1)}, u32[]{:S(2)}, u32[]{:S(2)}) collective-permute-start(bf16[1,7168,256]{2,1,0:T(8,128)(2,1)} %refs_0_), channel_id=1, source_target_pairs={{0,64},{64,0},{1,65},{65,1},{2,66},{66,2},{3,67},{67,3},{4,68},{68... | collective-permute-start | bytes 11010056 | tf_op jit(solution)/shard_map/ppermute | solution.py:58
  0.0 34.1 %collective-permute-start.1 = (bf16[1,7168,256]{2,1,0:T(8,128)(2,1)}, bf16[1,7168,256]{2,1,0:T(8,128)(2,1)}, u32[]{:S(2)}, u32[]{:S(2)}) collective-permute-start(bf16[1,7168,256]{2,1,0:T(8,128)(2,1)} %refs_2_), channel_id=1, source_target_pairs={{0,64},{64,0},{1,65},{65,1},{2,66},{66,2},{3,67},{67,3},{4,68},{68... | collective-permute-start | bytes 11010056 | tf_op jit(solution)/shard_map/ppermute | solution.py:58
  0.5 33.6 %collective-permute-start.2 = (bf16[1,256,7168]{2,1,0:T(8,128)(2,1)}, bf16[1,256,7168]{2,1,0:T(8,128)(2,1)}, u32[]{:S(2)}, u32[]{:S(2)}) collective-permute-start(bf16[1,256,7168]{2,1,0:T(8,128)(2,1)} %refs_4_), channel_id=1, source_target_pairs={{0,64},{64,0},{1,65},{65,1},{2,66},{66,2},{3,67},{67,3},{4,68},{68... | collective-permute-start | bytes 11010056 | tf_op jit(solution)/shard_map/ppermute | solution.py:58
  4.7 29.5 %collective-permute-start.3 = (bf16[144,2304]{1,0:T(8,128)(2,1)}, bf16[144,2304]{1,0:T(8,128)(2,1)S(1)}, u32[]{:S(2)}, u32[]{:S(2)}) collective-permute-start(bf16[144,2304]{1,0:T(8,128)(2,1)} %get-tuple-element.36), channel_id=1, source_target_pairs={{0,4},{4,8},{8,12},{12,0},{1,5},{5,9},{9,13},{13,1},{2,6},{6,10},{... | collective-permute-start | bytes 1990664 | tf_op jit(solution)/shard_map/ppermute | solution.py:49
  6.3 27.8 %collective-permute-start.4 = (bf16[144,2304]{1,0:T(8,128)(2,1)}, bf16[144,2304]{1,0:T(8,128)(2,1)S(1)}, u32[]{:S(2)}, u32[]{:S(2)}) collective-permute-start(bf16[144,2304]{1,0:T(8,128)(2,1)} %get-tuple-element.37), channel_id=1, source_target_pairs={{0,8},{4,12},{8,0},{12,4},{1,9},{5,13},{9,1},{13,5},{2,10},{6,14},... | collective-permute-start | bytes 1990664 | tf_op jit(solution)/shard_map/ppermute | solution.py:49
  9.2 24.9 %collective-permute-start.5 = (bf16[144,2304]{1,0:T(8,128)(2,1)}, bf16[144,2304]{1,0:T(8,128)(2,1)S(1)}, u32[]{:S(2)}, u32[]{:S(2)}) collective-permute-start(bf16[144,2304]{1,0:T(8,128)(2,1)} %get-tuple-element.38), channel_id=1, source_target_pairs={{0,12},{4,0},{8,4},{12,8},{1,13},{5,1},{9,5},{13,9},{2,14},{6,2},{... | collective-permute-start | bytes 1990664 | tf_op jit(solution)/shard_map/ppermute | solution.py:49
  10.6 23.6 %copy-start = (bf16[144,2304]{1,0:T(8,128)(2,1)S(1)}, bf16[144,2304]{1,0:T(8,128)(2,1)}, u32[]{:S(2)}) copy-start(bf16[144,2304]{1,0:T(8,128)(2,1)} %get-tuple-element.35.w0.p0) | copy-start | bytes 1990660
  10.6 23.6 %copy-start.1 = (s32[8]{0:T(128)S(1)}, s32[8]{0:T(128)}, u32[]{:S(2)}) copy-start(s32[8]{0:T(128)} %stack.29.at) | copy-start | bytes 100
  34.2 37.2 %copy-start.2 = (bf16[7168]{0:T(1024)(128)(2,1)S(1)}, bf16[7168]{0:T(1024)(128)(2,1)}, u32[]{:S(2)}) copy-start(bf16[7168]{0:T(1024)(128)(2,1)} %param.18) | copy-start | bytes 43012
  35.9 5.5 %collective-permute-start.6 = (bf16[4,64,128]{2,1,0:T(8,128)(2,1)S(1)}, bf16[4,64,128]{2,1,0:T(8,128)(2,1)S(1)}, u32[]{:S(2)}, u32[]{:S(2)}) collective-permute-start(bf16[4,64,128]{2,1,0:T(8,128)(2,1)S(1)} %shard_map.120.h0), channel_id=1, source_target_pairs={{0,4},{4,8},{8,12},{12,0},{1,5},{5,9},{9,13},{13,1},{2,6},{6,10},{... | collective-permute-start | bytes 196616 | tf_op jit(solution)/shard_map/ppermute | solution.py:49
  36.5 5.8 %collective-permute-start.7 = (bf16[4,64,128]{2,1,0:T(8,128)(2,1)S(1)}, bf16[4,64,128]{2,1,0:T(8,128)(2,1)S(1)}, u32[]{:S(2)}, u32[]{:S(2)}) collective-permute-start(bf16[4,64,128]{2,1,0:T(8,128)(2,1)S(1)} %shard_map.120.h0), channel_id=1, source_target_pairs={{0,8},{4,12},{8,0},{12,4},{1,9},{5,13},{9,1},{13,5},{2,10},{6,14},... | collective-permute-start | bytes 196616 | tf_op jit(solution)/shard_map/ppermute | solution.py:49
  38.0 5.1 %collective-permute-start.8 = (bf16[4,64,128]{2,1,0:T(8,128)(2,1)S(1)}, bf16[4,64,128]{2,1,0:T(8,128)(2,1)S(1)}, u32[]{:S(2)}, u32[]{:S(2)}) collective-permute-start(bf16[4,64,128]{2,1,0:T(8,128)(2,1)S(1)} %shard_map.120.h0), channel_id=1, source_target_pairs={{0,12},{4,0},{8,4},{12,8},{1,13},{5,1},{9,5},{13,9},{2,14},{6,2},{... | collective-permute-start | bytes 196616 | tf_op jit(solution)/shard_map/ppermute | solution.py:49
  44.8 7.5 %collective-permute-start.10 = (bf16[64,1920]{1,0:T(8,128)(2,1)S(1)}, bf16[64,1920]{1,0:T(8,128)(2,1)S(1)}, u32[]{:S(2)}, u32[]{:S(2)}) collective-permute-start(bf16[64,1920]{1,0:T(8,128)(2,1)S(1)} %get-tuple-element.41), channel_id=1, source_target_pairs={{0,16},{16,32},{32,48},{48,0},{4,20},{20,36},{36,52},{52,4},{8,24}... | collective-permute-start | bytes 737288 | tf_op jit(solution)/shard_map/ppermute | solution.py:49
  45.3 9.2 %collective-permute-start.11 = (bf16[64,1920]{1,0:T(8,128)(2,1)S(1)}, bf16[64,1920]{1,0:T(8,128)(2,1)S(1)}, u32[]{:S(2)}, u32[]{:S(2)}) collective-permute-start(bf16[64,1920]{1,0:T(8,128)(2,1)S(1)} %get-tuple-element.42), channel_id=1, source_target_pairs={{0,48},{16,0},{32,16},{48,32},{4,52},{20,4},{36,20},{52,36},{8,56}... | collective-permute-start | bytes 737288 | tf_op jit(solution)/shard_map/ppermute | solution.py:49
  48.1 7.7 %collective-permute-start.9 = (bf16[64,1920]{1,0:T(8,128)(2,1)S(1)}, bf16[64,1920]{1,0:T(8,128)(2,1)S(1)}, u32[]{:S(2)}, u32[]{:S(2)}) collective-permute-start(bf16[64,1920]{1,0:T(8,128)(2,1)S(1)} %get-tuple-element.40), channel_id=1, source_target_pairs={{0,32},{16,48},{32,0},{48,16},{4,36},{20,52},{36,4},{52,20},{8,40}... | collective-permute-start | bytes 737288 | tf_op jit(solution)/shard_map/ppermute | solution.py:49
  55.9 10.1 %collective-permute-start.12 = (bf16[64,1920]{1,0:T(8,128)(2,1)S(1)}, bf16[64,1920]{1,0:T(8,128)(2,1)S(1)}, u32[]{:S(2)}, u32[]{:S(2)}) collective-permute-start(bf16[64,1920]{1,0:T(8,128)(2,1)S(1)} %add_convert_fusion.1), channel_id=1, source_target_pairs={{0,1},{1,2},{2,3},{3,0},{4,5},{5,6},{6,7},{7,4},{8,9},{9,10},{10,1... | collective-permute-start | bytes 737288 | tf_op jit(solution)/shard_map/ppermute | solution.py:49
  56.4 9.6 %collective-permute-start.13 = (bf16[64,1920]{1,0:T(8,128)(2,1)S(1)}, bf16[64,1920]{1,0:T(8,128)(2,1)S(1)}, u32[]{:S(2)}, u32[]{:S(2)}) collective-permute-start(bf16[64,1920]{1,0:T(8,128)(2,1)S(1)} %add_convert_fusion.1), channel_id=1, source_target_pairs={{0,2},{1,3},{2,0},{3,1},{4,6},{5,7},{6,4},{7,5},{8,10},{9,11},{10,... | collective-permute-start | bytes 737288 | tf_op jit(solution)/shard_map/ppermute | solution.py:49
  58.5 8.4 %collective-permute-start.14 = (bf16[64,1920]{1,0:T(8,128)(2,1)S(1)}, bf16[64,1920]{1,0:T(8,128)(2,1)S(1)}, u32[]{:S(2)}, u32[]{:S(2)}) collective-permute-start(bf16[64,1920]{1,0:T(8,128)(2,1)S(1)} %add_convert_fusion.1), channel_id=1, source_target_pairs={{0,3},{1,0},{2,1},{3,2},{4,7},{5,4},{6,5},{7,6},{8,11},{9,8},{10,9... | collective-permute-start | bytes 737288 | tf_op jit(solution)/shard_map/ppermute | solution.py:49
  67.0 7.5 %collective-permute-start.15 = (bf16[64,1920]{1,0:T(8,128)(2,1)S(1)}, bf16[64,1920]{1,0:T(8,128)(2,1)S(1)}, u32[]{:S(2)}, u32[]{:S(2)}) collective-permute-start(bf16[64,1920]{1,0:T(8,128)(2,1)S(1)} %add_convert_fusion.s0), channel_id=1, source_target_pairs={{0,4},{4,8},{8,12},{12,0},{1,5},{5,9},{9,13},{13,1},{2,6},{6,10},{... | collective-permute-start | bytes 737288 | tf_op jit(solution)/shard_map/ppermute | solution.py:49
  68.4 9.4 %collective-permute-start.16 = (bf16[64,1920]{1,0:T(8,128)(2,1)S(1)}, bf16[64,1920]{1,0:T(8,128)(2,1)S(1)}, u32[]{:S(2)}, u32[]{:S(2)}) collective-permute-start(bf16[64,1920]{1,0:T(8,128)(2,1)S(1)} %add_convert_fusion.s0), channel_id=1, source_target_pairs={{0,8},{4,12},{8,0},{12,4},{1,9},{5,13},{9,1},{13,5},{2,10},{6,14},... | collective-permute-start | bytes 737288 | tf_op jit(solution)/shard_map/ppermute | solution.py:49
  71.0 7.1 %collective-permute-start.17 = (bf16[64,1920]{1,0:T(8,128)(2,1)S(1)}, bf16[64,1920]{1,0:T(8,128)(2,1)S(1)}, u32[]{:S(2)}, u32[]{:S(2)}) collective-permute-start(bf16[64,1920]{1,0:T(8,128)(2,1)S(1)} %add_convert_fusion.s0), channel_id=1, source_target_pairs={{0,12},{4,0},{8,4},{12,8},{1,13},{5,1},{9,5},{13,9},{2,14},{6,2},{... | collective-permute-start | bytes 737288 | tf_op jit(solution)/shard_map/ppermute | solution.py:49
  79.1 14.8 %collective-permute-start.18 = (bf16[64,7296]{1,0:T(8,128)(2,1)S(1)}, bf16[64,7296]{1,0:T(8,128)(2,1)S(1)}, u32[]{:S(2)}, u32[]{:S(2)}) collective-permute-start(bf16[64,7296]{1,0:T(8,128)(2,1)S(1)} %get-tuple-element.44.x), channel_id=1, source_target_pairs={{0,16},{16,32},{32,48},{48,0},{4,20},{20,36},{36,52},{52,4},{8,24}... | collective-permute-start | bytes 2801672 | tf_op jit(solution)/shard_map/ppermute | solution.py:49
  79.2 14.8 %collective-permute-start.19 = (bf16[64,7296]{1,0:T(8,128)(2,1)S(1)}, bf16[64,7296]{1,0:T(8,128)(2,1)S(1)}, u32[]{:S(2)}, u32[]{:S(2)}) collective-permute-start(bf16[64,7296]{1,0:T(8,128)(2,1)S(1)} %get-tuple-element.44.x), channel_id=1, source_target_pairs={{0,48},{16,0},{32,16},{48,32},{4,52},{20,4},{36,20},{52,36},{8,56}... | collective-permute-start | bytes 2801672 | tf_op jit(solution)/shard_map/ppermute | solution.py:49
  94.0 11.2 %collective-permute-start.22 = (bf16[32,7296]{1,0:T(8,128)(2,1)S(1)}, bf16[32,7296]{1,0:T(8,128)(2,1)S(1)}, u32[]{:S(2)}, u32[]{:S(2)}) collective-permute-start(bf16[32,7296]{1,0:T(8,128)(2,1)S(1)} %slice.6), channel_id=1, source_target_pairs={{0,16},{16,32},{32,48},{48,0},{4,20},{20,36},{36,52},{52,4},{8,24}... | collective-permute-start | bytes 1400840 | tf_op jit(solution)/shard_map/ppermute | solution.py:49
  94.6 10.6 %collective-permute-start.23 = (bf16[32,7296]{1,0:T(8,128)(2,1)S(1)}, bf16[32,7296]{1,0:T(8,128)(2,1)S(1)}, u32[]{:S(2)}, u32[]{:S(2)}) collective-permute-start(bf16[32,7296]{1,0:T(8,128)(2,1)S(1)} %slice.7), channel_id=1, source_target_pairs={{0,48},{16,0},{32,16},{48,32},{4,52},{20,4},{36,20},{52,36},{8,56}... | collective-permute-start | bytes 1400840 | tf_op jit(solution)/shard_map/ppermute | solution.py:49
  103.1 13.5 %collective-permute-start.20 = (bf16[64,7168]{1,0:T(8,128)(2,1)S(1)}, bf16[64,7168]{1,0:T(8,128)(2,1)S(1)}, u32[]{:S(2)}, u32[]{:S(2)}) collective-permute-start(bf16[64,7168]{1,0:T(8,128)(2,1)S(1)} %get-tuple-element.61), channel_id=1, source_target_pairs={{0,48},{16,0},{32,16},{48,32},{4,52},{20,4},{36,20},{52,36},{8,56}... | collective-permute-start | bytes 2752520 | tf_op jit(solution)/shard_map/ppermute | solution.py:49
  105.2 24.4 %collective-permute-start.21 = (bf16[64,7168]{1,0:T(8,128)(2,1)S(1)}, bf16[64,7168]{1,0:T(8,128)(2,1)S(1)}, u32[]{:S(2)}, u32[]{:S(2)}) collective-permute-start(bf16[64,7168]{1,0:T(8,128)(2,1)S(1)} %get-tuple-element.62), channel_id=1, source_target_pairs={{0,16},{16,32},{32,48},{48,0},{4,20},{20,36},{36,52},{52,4},{8,24}... | collective-permute-start | bytes 2752520 | tf_op jit(solution)/shard_map/ppermute | solution.py:49
  111.4 18.2 %collective-permute-start.24 = (bf16[64,7168]{1,0:T(8,128)(2,1)S(1)}, bf16[64,7168]{1,0:T(8,128)(2,1)S(1)}, u32[]{:S(2)}, u32[]{:S(2)}) collective-permute-start(bf16[64,7168]{1,0:T(8,128)(2,1)S(1)} %shard_map.125), channel_id=1, source_target_pairs={{0,32},{16,48},{32,0},{48,16},{4,36},{20,52},{36,4},{52,20},{8,40}... | collective-permute-start | bytes 2752520 | tf_op jit(solution)/shard_map/ppermute | solution.py:49
  131.6 18.3 %all-to-all-start.1 = ((bf16[16,4,7168]{2,1,0:T(4,128)(2,1)}), bf16[16,4,7168]{2,1,0:T(4,128)(2,1)S(1)}, u32[]{:S(2)}, u32[]{:S(2)}) async-start(bf16[16,4,7168]{2,1,0:T(4,128)(2,1)} %shard_map.126), calls=%async_computation.1 | async-start | bytes 1835008 | tf_op jit(solution)/shard_map/all_to_all | solution.py:535
